TPU v7x, 32 devices: a whole 2x2x4 slice. The times are simulated.
32 devices in a mesh: ctx: 16 (over z, y, core), fsdp: 2 (over x).
Axes of the slice: x: 2, y: 2, z: 4, core: 2. Of those that a mesh axis runs over, the one named last changes fastest.
Arguments:
- hidden: bfloat16 [1024, 4, 2048], P('ctx', 'fsdp'), may hold values from -6 to 6
- cotangent: bfloat16 [1024, 4, 2048], P('ctx', 'fsdp'), may hold values from -6 to 6
- pairing: int32 [16], replicated, may hold values from 0 to 15, each once
- ln1_gain: bfloat16 [2048], P(('ctx', 'fsdp')), may hold values from 0.5 to 1.5
- ln1_bias: bfloat16 [2048], P(('ctx', 'fsdp')), may hold values from -3 to 3
- qkv_weight: bfloat16 [2048, 6144], P(('ctx', 'fsdp')), may hold values from -0.125 to 0.125
- qkv_bias: bfloat16 [6144], P(('ctx', 'fsdp')), may hold values from -3 to 3
- out_weight: bfloat16 [2048, 2048], P(('ctx', 'fsdp')), may hold values from -2 to 2
- out_bias: bfloat16 [2048], P(('ctx', 'fsdp')), may hold values from -3 to 3
- ln2_gain: bfloat16 [2048], P(('ctx', 'fsdp')), may hold values from 0.5 to 1.5
- ln2_bias: bfloat16 [2048], P(('ctx', 'fsdp')), may hold values from -3 to 3
- up_weight: bfloat16 [2048, 8192], P(('ctx', 'fsdp')), may hold values from -0.125 to 0.125
- up_bias: bfloat16 [8192], P(('ctx', 'fsdp')), may hold values from -3 to 3
- down_weight: bfloat16 [2048, 8192], P(('ctx', 'fsdp')), may hold values from -0.0625 to 0.0625
- down_bias: bfloat16 [2048], P(('ctx', 'fsdp')), may hold values from -3 to 3
Outputs:
- output: bfloat16 [1024, 4, 2048], P('ctx', 'fsdp')
- grad_hidden: float32 [1024, 4, 2048], P('ctx', 'fsdp')
- grad_ln1_gain: float32 [2048], P(('ctx', 'fsdp'))
- grad_ln1_bias: float32 [2048], P(('ctx', 'fsdp'))
- grad_qkv_weight: float32 [2048, 6144], P(('ctx', 'fsdp'))
- grad_qkv_bias: float32 [6144], P(('ctx', 'fsdp'))
- grad_out_weight: float32 [2048, 2048], P(('ctx', 'fsdp'))
- grad_out_bias: float32 [2048], P(('ctx', 'fsdp'))
- grad_ln2_gain: float32 [2048], P(('ctx', 'fsdp'))
- grad_ln2_bias: float32 [2048], P(('ctx', 'fsdp'))
- grad_up_weight: float32 [2048, 8192], P(('ctx', 'fsdp'))
- grad_up_bias: float32 [8192], P(('ctx', 'fsdp'))
- grad_down_weight: float32 [2048, 8192], P(('ctx', 'fsdp'))
- grad_down_bias: float32 [2048], P(('ctx', 'fsdp'))
Inputs may be any that keep to these rules, and one draw needn't show every extreme that they name: `pairing`: each device number appears once.
All inputs are finite; a program needn't handle non-finite values.
Results may differ from a plain program's by a relative error of at most 0.0095.
Values may be sent and summed in bfloat16 or wider, within the bound.
A program may use at most 640 MiB of HBM per device.

v0:
```python
import jax
import jax.numpy as jnp
from jax import lax
from jax.sharding import PartitionSpec as P

HEAD = 256
ROT = 64


LN_EPSILON = 1e-05
VERY_LOW = -1e30


def layer_norm(values, ln_gain, ln_shift):
    average = jnp.mean(values, axis=-1, keepdims=True)
    centered = values - average
    spread = jnp.mean(centered * centered, axis=-1, keepdims=True)
    return centered * lax.rsqrt(spread + LN_EPSILON) * ln_gain + ln_shift


def gelu_exact(values):
    return jax.nn.gelu(values, approximate=False)


def rotate(values, positions):
    half_rot = ROT // 2
    frequency = 1.0 / 10000.0 ** (jnp.arange(half_rot).astype(values.dtype) * 2.0 / ROT)
    angles = positions.astype(values.dtype)[:, None] * frequency[None, :]
    shape_out = (angles.shape[0],) + (1,) * (values.ndim - 2) + (ROT,)
    cosine = jnp.concatenate([jnp.cos(angles), jnp.cos(angles)], axis=-1).reshape(shape_out)
    sine_part = jnp.concatenate([jnp.sin(angles), jnp.sin(angles)], axis=-1).reshape(shape_out)
    rot_part = values[..., :ROT]
    turned = jnp.concatenate([-rot_part[..., half_rot:], rot_part[..., :half_rot]], axis=-1)
    return jnp.concatenate([rot_part * cosine + turned * sine_part, values[..., ROT:]], axis=-1)


def row_positions(pairing, first_row, row_count, block_rows, ctx_count):
    row_ids = first_row + jnp.arange(row_count, dtype=jnp.int32)
    device_ids = row_ids // (2 * block_rows)
    within = row_ids % (2 * block_rows)
    matches = device_ids[:, None] == jnp.arange(ctx_count, dtype=jnp.int32)[None, :]
    owned_block = jnp.sum(jnp.where(matches, pairing[None, :], 0), axis=1)
    blocks = jnp.where(within < block_rows, owned_block, 2 * ctx_count - 1 - owned_block)
    return blocks * block_rows + within % block_rows


def heads_view(values, row_total, seq_count):
    return values.reshape(row_total, seq_count, -1, HEAD)


def contract_rows(left, right):
    return lax.dot_general(
        left, right, (((0,), (0,)), ((), ())), preferred_element_type=jnp.float32
    )


def contract_cols(left, right):
    return lax.dot_general(
        left, right, (((1,), (1,)), ((), ())), preferred_element_type=jnp.float32
    )


def pair_grads(
    query_rows, grad_rows, log_rows, delta_rows, query_pos, key_heads, value_heads, key_pos, scaling
):
    scores = (
        jnp.einsum("qshd,kshd->shqk", query_rows, key_heads, preferred_element_type=jnp.float32)
        * scaling
    )
    allowed = key_pos[None, None, None, :] <= query_pos[None, None, :, None]
    probabilities = jnp.where(allowed, jnp.exp(scores - log_rows[..., None]), 0.0)
    prob_grad = jnp.einsum(
        "qshd,kshd->shqk", grad_rows, value_heads, preferred_element_type=jnp.float32
    )
    score_grad = (probabilities * (prob_grad - delta_rows[..., None])).astype(jnp.bfloat16)
    return (score_grad, probabilities.astype(jnp.bfloat16))


def body(
    hidden,
    cotangent,
    pairing,
    ln1_gain,
    ln1_bias,
    qkv_weight,
    qkv_bias,
    out_weight,
    out_bias,
    ln2_gain,
    ln2_bias,
    up_weight,
    up_bias,
    down_weight,
    down_bias,
):
    local_rows, seq_count, model_width = hidden.shape
    block_rows = local_rows // 2
    ctx_count = lax.axis_size("ctx")
    head_count = model_width // HEAD
    scaling = HEAD ** (-0.5)
    tokens = local_rows * seq_count
    total_rows = local_rows * ctx_count
    params = (
        lax.all_gather(ln1_gain, ("ctx", "fsdp"), axis=0, tiled=True),
        lax.all_gather(ln1_bias, ("ctx", "fsdp"), axis=0, tiled=True),
        lax.all_gather(qkv_weight, ("ctx", "fsdp"), axis=0, tiled=True),
        lax.all_gather(qkv_bias, ("ctx", "fsdp"), axis=0, tiled=True),
        lax.all_gather(out_weight, ("ctx", "fsdp"), axis=0, tiled=True),
        lax.all_gather(out_bias, ("ctx", "fsdp"), axis=0, tiled=True),
        lax.all_gather(ln2_gain, ("ctx", "fsdp"), axis=0, tiled=True),
        lax.all_gather(ln2_bias, ("ctx", "fsdp"), axis=0, tiled=True),
        lax.all_gather(up_weight, ("ctx", "fsdp"), axis=0, tiled=True),
        lax.all_gather(up_bias, ("ctx", "fsdp"), axis=0, tiled=True),
        lax.all_gather(down_weight, ("ctx", "fsdp"), axis=0, tiled=True),
        lax.all_gather(down_bias, ("ctx", "fsdp"), axis=0, tiled=True),
    )
    (
        gain_one,
        shift_one,
        w_qkv,
        b_qkv,
        w_out,
        b_out,
        gain_two,
        shift_two,
        w_up,
        b_up,
        w_down,
        b_down,
    ) = params
    ff_width = w_up.shape[1]
    hidden_f = hidden.astype(jnp.float32).reshape(tokens, model_width)
    own_pos = row_positions(
        pairing, lax.axis_index("ctx") * local_rows, local_rows, block_rows, ctx_count
    )
    normed_one, ln_one_pull = jax.vjp(
        layer_norm, hidden_f, gain_one.astype(jnp.float32), shift_one.astype(jnp.float32)
    )
    normed_one_low = normed_one.astype(jnp.bfloat16)
    projected = jnp.dot(normed_one_low, w_qkv, preferred_element_type=jnp.float32) + b_qkv.astype(
        jnp.float32
    )
    query_f, rotation_pull = jax.vjp(
        lambda values: rotate(values, own_pos),
        heads_view(projected[:, :model_width], local_rows, seq_count),
    )
    query_b = query_f.astype(jnp.bfloat16)
    key_b = (
        rotate(
            heads_view(projected[:, model_width : 2 * model_width], local_rows, seq_count), own_pos
        )
        .astype(jnp.bfloat16)
        .reshape(local_rows, seq_count, model_width)
    )
    value_b = (
        projected[:, 2 * model_width :]
        .astype(jnp.bfloat16)
        .reshape(local_rows, seq_count, model_width)
    )
    running_max = jnp.full((seq_count, head_count, local_rows), VERY_LOW, jnp.float32)
    key_piece = lax.all_gather(key_b, "ctx", axis=0, tiled=True)
    value_piece = lax.all_gather(value_b, "ctx", axis=0, tiled=True)
    row_total = key_piece.shape[0]
    key_pos = row_positions(pairing, jnp.int32(0), row_total, block_rows, ctx_count)
    scores = (
        jnp.einsum(
            "qshd,kshd->shqk",
            query_b,
            heads_view(key_piece, row_total, seq_count),
            preferred_element_type=jnp.float32,
        )
        * scaling
    )
    allowed = key_pos[None, None, None, :] <= own_pos[None, None, :, None]
    piece_max = jnp.max(jnp.where(allowed, scores, VERY_LOW), axis=-1)
    new_max = jnp.maximum(running_max, piece_max)
    weights = jnp.where(allowed, jnp.exp(scores - new_max[..., None]), 0.0)
    new_total = jnp.sum(weights, axis=-1)
    mixture = jnp.einsum(
        "shqk,kshd->qshd",
        weights.astype(jnp.bfloat16),
        heads_view(value_piece, row_total, seq_count),
        preferred_element_type=jnp.float32,
    )
    log_total = new_max + jnp.log(new_total)
    attended = mixture / jnp.transpose(new_total, (2, 0, 1))[..., None]
    attended_low = attended.astype(jnp.bfloat16).reshape(tokens, model_width)
    branch_attn = jnp.dot(attended_low, w_out, preferred_element_type=jnp.float32) + b_out.astype(
        jnp.float32
    )
    normed_two, ln_two_pull = jax.vjp(
        layer_norm, hidden_f, gain_two.astype(jnp.float32), shift_two.astype(jnp.float32)
    )
    normed_two_low = normed_two.astype(jnp.bfloat16)
    inner_act = jnp.dot(normed_two_low, w_up, preferred_element_type=jnp.float32) + b_up.astype(
        jnp.float32
    )
    activated_f, gelu_pull = jax.vjp(gelu_exact, inner_act)
    activated = activated_f.astype(jnp.bfloat16)
    branch_mlp = contract_cols(activated, w_down) + b_down.astype(jnp.float32)
    output = (
        (hidden_f + branch_attn + branch_mlp)
        .astype(jnp.bfloat16)
        .reshape(local_rows, seq_count, model_width)
    )
    back_qkv, back_out, back_up, back_down = (
        lax.all_gather(qkv_weight, ("ctx", "fsdp"), axis=0, tiled=True),
        lax.all_gather(out_weight, ("ctx", "fsdp"), axis=0, tiled=True),
        lax.all_gather(up_weight, ("ctx", "fsdp"), axis=0, tiled=True),
        lax.all_gather(down_weight, ("ctx", "fsdp"), axis=0, tiled=True),
    )
    grad_out = cotangent.reshape(tokens, model_width)
    grad_f = grad_out.astype(jnp.float32)
    bias_sum = jnp.sum(grad_f, axis=0)
    up_grad = jnp.dot(grad_out, back_down, preferred_element_type=jnp.float32)
    inner_grad = gelu_pull(up_grad)[0].astype(jnp.bfloat16)
    norm_two_grad = contract_cols(inner_grad, back_up)
    dx_two, dgain_two, dshift_two = ln_two_pull(norm_two_grad)
    up_bias_sum = jnp.sum(inner_grad, axis=0, dtype=jnp.float32)
    mlp_small = jnp.concatenate(
        [
            up_bias_sum.reshape(model_width, -1),
            jnp.stack([bias_sum, dgain_two, dshift_two], axis=1),
        ],
        axis=1,
    )
    up_w_sum, down_w_sum, mlp_small_sum = (
        lax.psum_scatter(
            contract_rows(normed_two_low, inner_grad),
            ("ctx", "fsdp"),
            scatter_dimension=0,
            tiled=True,
        ),
        lax.psum_scatter(
            contract_rows(grad_out, activated), ("ctx", "fsdp"), scatter_dimension=0, tiled=True
        ),
        lax.psum_scatter(mlp_small, ("ctx", "fsdp"), scatter_dimension=0, tiled=True),
    )
    ratio = ff_width // model_width
    attn_grad = contract_cols(grad_out, back_out).astype(jnp.bfloat16)
    out_w_grad = contract_rows(attended_low, grad_out)
    grad_heads = heads_view(attn_grad, local_rows, seq_count)
    row_delta = jnp.einsum("qshd,qshd->shq", grad_heads.astype(jnp.float32), attended)
    keys_all, values_all = (
        lax.all_gather(key_b, "ctx", axis=0, tiled=True),
        lax.all_gather(value_b, "ctx", axis=0, tiled=True),
    )
    key_block = 512
    block_count = total_rows // key_block
    starts = jnp.arange(block_count, dtype=jnp.int32) * key_block

    def query_step(query_grad, inputs):
        key_piece, value_piece, offset = inputs
        key_pos = row_positions(pairing, offset, key_block, block_rows, ctx_count)
        key_heads = heads_view(key_piece, key_block, seq_count)
        value_heads = heads_view(value_piece, key_block, seq_count)
        score_grad, unused = pair_grads(
            query_b,
            grad_heads,
            log_total,
            row_delta,
            own_pos,
            key_heads,
            value_heads,
            key_pos,
            scaling,
        )
        query_grad = (
            query_grad
            + jnp.einsum(
                "shqk,kshd->qshd", score_grad, key_heads, preferred_element_type=jnp.float32
            )
            * scaling
        )
        return (query_grad, None)

    query_grad, unused_out = lax.scan(
        query_step,
        jnp.zeros((local_rows, seq_count, head_count, HEAD), jnp.float32),
        (
            keys_all.reshape(block_count, key_block, seq_count, model_width),
            values_all.reshape(block_count, key_block, seq_count, model_width),
            starts,
        ),
    )
    queries_all, grads_all = (
        lax.all_gather(query_b, "ctx", axis=0, tiled=True),
        lax.all_gather(grad_heads, "ctx", axis=0, tiled=True),
    )
    logs_all, deltas_all = (
        lax.all_gather(log_total, "ctx", axis=2, tiled=True),
        lax.all_gather(row_delta, "ctx", axis=2, tiled=True),
    )
    own_keys = heads_view(key_b, local_rows, seq_count)
    own_values = heads_view(value_b, local_rows, seq_count)

    def key_step(carry, inputs):
        key_acc, value_acc = carry
        query_piece, grad_piece, log_piece, delta_piece, offset = inputs
        query_pos = row_positions(pairing, offset, key_block, block_rows, ctx_count)
        score_grad, probs_low = pair_grads(
            query_piece,
            grad_piece,
            log_piece,
            delta_piece,
            query_pos,
            own_keys,
            own_values,
            own_pos,
            scaling,
        )
        key_acc = (
            key_acc
            + jnp.einsum(
                "shqk,qshd->kshd", score_grad, query_piece, preferred_element_type=jnp.float32
            )
            * scaling
        )
        value_acc = value_acc + jnp.einsum(
            "shqk,qshd->kshd", probs_low, grad_piece, preferred_element_type=jnp.float32
        )
        return ((key_acc, value_acc), None)

    empty_acc = jnp.zeros((local_rows, seq_count, head_count, HEAD), jnp.float32)
    log_blocks = jnp.moveaxis(logs_all.reshape(seq_count, head_count, block_count, key_block), 2, 0)
    delta_blocks = jnp.moveaxis(
        deltas_all.reshape(seq_count, head_count, block_count, key_block), 2, 0
    )
    (key_sum, value_sum), unused_keys = lax.scan(
        key_step,
        (empty_acc, empty_acc),
        (
            queries_all.reshape(block_count, key_block, seq_count, head_count, HEAD),
            grads_all.reshape(block_count, key_block, seq_count, head_count, HEAD),
            log_blocks,
            delta_blocks,
            starts,
        ),
    )
    key_owned = key_sum.reshape(local_rows, seq_count, model_width)
    value_owned = value_sum.reshape(local_rows, seq_count, model_width)
    query_pre = rotation_pull(query_grad)[0].reshape(tokens, model_width)
    key_pre = rotation_pull(heads_view(key_owned, local_rows, seq_count))[0].reshape(
        tokens, model_width
    )
    value_pre = value_owned.reshape(tokens, model_width)
    projected_grad = jnp.concatenate([query_pre, key_pre, value_pre], axis=1).astype(jnp.bfloat16)
    norm_one_grad = contract_cols(projected_grad, back_qkv)
    dx_one, dgain_one, dshift_one = ln_one_pull(norm_one_grad)
    qkv_bias_sum = jnp.sum(projected_grad, axis=0, dtype=jnp.float32)
    attn_small = jnp.concatenate(
        [
            qkv_bias_sum.reshape(model_width, -1),
            jnp.stack([bias_sum, dgain_one, dshift_one], axis=1),
        ],
        axis=1,
    )
    qkv_w_sum, out_w_sum, attn_small_sum = (
        lax.psum_scatter(
            contract_rows(normed_one_low, projected_grad),
            ("ctx", "fsdp"),
            scatter_dimension=0,
            tiled=True,
        ),
        lax.psum_scatter(out_w_grad, ("ctx", "fsdp"), scatter_dimension=0, tiled=True),
        lax.psum_scatter(attn_small, ("ctx", "fsdp"), scatter_dimension=0, tiled=True),
    )
    grad_hidden = (grad_f + dx_one + dx_two).reshape(local_rows, seq_count, model_width)
    return (
        output,
        grad_hidden,
        attn_small_sum[:, 4],
        attn_small_sum[:, 5],
        qkv_w_sum,
        attn_small_sum[:, :3].reshape(-1),
        out_w_sum,
        attn_small_sum[:, 3],
        mlp_small_sum[:, ratio + 1],
        mlp_small_sum[:, ratio + 2],
        up_w_sum,
        mlp_small_sum[:, :ratio].reshape(-1),
        down_w_sum,
        mlp_small_sum[:, ratio],
    )


def solution(mesh):
    return jax.shard_map(
        body,
        mesh=mesh,
        in_specs=(
            P("ctx", "fsdp", None),
            P("ctx", "fsdp", None),
            P(),
            P(("ctx", "fsdp")),
            P(("ctx", "fsdp")),
            P(("ctx", "fsdp"), None),
            P(("ctx", "fsdp")),
            P(("ctx", "fsdp"), None),
            P(("ctx", "fsdp")),
            P(("ctx", "fsdp")),
            P(("ctx", "fsdp")),
            P(("ctx", "fsdp"), None),
            P(("ctx", "fsdp")),
            P(("ctx", "fsdp"), None),
            P(("ctx", "fsdp")),
        ),
        out_specs=(
            P("ctx", "fsdp", None),
            P("ctx", "fsdp", None),
            P(("ctx", "fsdp")),
            P(("ctx", "fsdp")),
            P(("ctx", "fsdp"), None),
            P(("ctx", "fsdp")),
            P(("ctx", "fsdp"), None),
            P(("ctx", "fsdp")),
            P(("ctx", "fsdp")),
            P(("ctx", "fsdp")),
            P(("ctx", "fsdp"), None),
            P(("ctx", "fsdp")),
            P(("ctx", "fsdp"), None),
            P(("ctx", "fsdp")),
        ),
        check_vma=False,
    )
```

profile of v0, /device:TPU:9, one launch (start us, length us, event | category | flops | bytes accessed | tf_op | source)
XLA Modules:
  0.0 4882.0 jit_solution(16574739266735055638)
XLA Ops:
  20.0 42.1 all-reduce.15
  63.2 103.3 %all-gather.10.cloned.1.call-done = bf16[2048,6144]{1,0:T(8,128)(2,1)} async-done(((bf16[64,6144]{1,0:T(8,128)(2,1)}), bf16[2048,6144]{1,0:T(8,128)(2,1)}) %all-gather.10.cloned.1.call-update) | async-done | bytes 25165840 | tf_op jit(solution)/shard_map/all_gather | solution.py:106
  183.3 63.6 %all-gather.16.cloned.1.call-done = bf16[2048,2048]{1,0:T(8,128)(2,1)} async-done(((bf16[64,2048]{1,0:T(8,128)(2,1)}), bf16[2048,2048]{1,0:T(8,128)(2,1)}) %all-gather.16.cloned.1.call-update) | async-done | bytes 8388624 | tf_op jit(solution)/shard_map/all_gather | solution.py:108
  258.7 51.2 %all-gather = bf16[32,1,256]{2,1,0:T(2,128)(2,1)S(1)} all-gather(bf16[1,1,256]{2,1,0:T(2,128)(2,1)S(1)} %reshape.566), channel_id=1, replica_groups=mesh['ctx'=16,'fsdp'=2] {'ctx','fsdp'}, dimensions={0}, use_global_device_ids=true | all-gather | bytes 16896 | tf_op jit(solution)/shard_map/all_gather | solution.py:113
  334.6 63.9 %all-gather.12.cloned.1.call-done = bf16[1024,2,2048]{2,1,0:T(2,128)(2,1)} async-done(((bf16[64,2,2048]{2,1,0:T(2,128)(2,1)}), bf16[1024,2,2048]{2,1,0:T(2,128)(2,1)}) %all-gather.12.cloned.1.call-update) | async-done | bytes 8388624 | tf_op jit(solution)/shard_map/all_gather | solution.py:162
  398.5 21.2 copy.214
  434.6 26.9 all_gather.75
  463.9 25.8 all_gather.77
  490.1 81.3 %while.30 = (s32[]{:T(128)}, f32[64,2,8,256]{3,0,2,1:T(8,128)S(1)}, bf16[2,512,2,2048]{3,1,0,2:T(8,128)(2,1)}, s32[2]{0:T(128)S(1)}, s32[16]{0:T(128)S(1)}, /*in...) while((s32[]{:T(128)}, f32[64,2,8,256]{3,0,2,1:T(8,128)S(1)}, ...), condition=%wide.region_8.9_spmd.clone, body=%wide.region_6.8_spmd.clone.sunk | while | flops 809317888 | bytes 53563880 | solution.py:277
  572.7 47.1 while.31
  642.0 116.5 %all-gather.18.cloned.1.call-done = bf16[2048,8192]{1,0:T(8,128)(2,1)} async-done(((bf16[64,8192]{1,0:T(8,128)(2,1)}), bf16[2048,8192]{1,0:T(8,128)(2,1)}) %all-gather.18.cloned.1.call-update) | async-done | bytes 33554448 | tf_op jit(solution)/shard_map/all_gather | solution.py:112
  758.5 17.2 convolution_add_fusion
  775.7 178.7 %all-gather.20.cloned.1.call-done = bf16[2048,8192]{1,0:T(8,128)(2,1)} async-done(((bf16[64,8192]{1,0:T(8,128)(2,1)}), bf16[2048,8192]{1,0:T(8,128)(2,1)}) %all-gather.20.cloned.1.call-update) | async-done | bytes 33554448 | tf_op jit(solution)/shard_map/all_gather | solution.py:114
  954.4 23.2 convert_reduce_fusion
  977.6 19.9 multiply_reduce_fusion.1
  1014.2 19.6 fusion.85
  1035.3 23.3 fusion.86
  1063.0 23.2 convolution_bitcast_fusion
  1086.2 61.3 %copy.268 = f32[2048,8192]{1,0:T(8,128)} copy(f32[2048,8192]{0,1:T(8,128)} %convolution_bitcast_fusion) | data formatting | bytes 134217728
  1178.5 72.2 %reduce-scatter.21.cloned.1.call-done = f32[64,7]{1,0:T(8,128)} async-done(((f32[2048,7]{1,0:T(8,128)}), f32[64,7]{1,0:T(8,128)}) %reduce-scatter.21.cloned.1.call-update) | async-done | bytes 1808
  1254.8 368.1 %reduce-scatter.15.cloned.1.call-done = f32[64,2048]{1,0:T(8,128)} async-done(((f32[2048,2048]{1,0:T(8,128)}), f32[64,2048]{1,0:T(8,128)}) %reduce-scatter.15.cloned.1.call-update) | async-done | bytes 524304 | tf_op jit(solution)/shard_map/reduce_scatter | solution.py:365
  1622.9 438.2 %reduce-scatter.13.cloned.1.call-done = f32[64,6144]{1,0:T(8,128)} async-done(((f32[2048,6144]{1,0:T(8,128)}), f32[64,6144]{1,0:T(8,128)}) %reduce-scatter.13.cloned.1.call-update) | async-done | bytes 1572880 | tf_op jit(solution)/shard_map/reduce_scatter | solution.py:359
  2061.1 1406.0 %reduce-scatter.17.cloned.1.call-done = f32[64,8192]{1,0:T(8,128)} async-done(((f32[2048,8192]{1,0:T(8,128)}), f32[64,8192]{1,0:T(8,128)}) %reduce-scatter.17.cloned.1.call-update) | async-done | bytes 2097168 | tf_op jit(solution)/shard_map/reduce_scatter | solution.py:228
  3467.1 1408.2 %reduce-scatter.23.cloned.1.call-done = f32[64,8192]{1,0:T(8,128)} async-done(((f32[2048,8192]{1,0:T(8,128)}), f32[64,8192]{1,0:T(8,128)}) %reduce-scatter.23.cloned.1.call-update) | async-done | bytes 2097168
  (298 shorter events, 293.2 us)
Async XLA Ops:
  7.2 159.3 %all-gather.10.cloned.1.call-start = ((), (), s32[]{:S(2)}) async-start(), calls=%async_computation.6 | async-start | bytes 25952256 | tf_op jit(solution)/shard_map/all_gather | solution.py:106
  7.9 238.9 %all-gather.16.cloned.1.call-start = ((), (), s32[]{:S(2)}) async-start(), calls=%async_computation.9 | async-start | bytes 8650752 | tf_op jit(solution)/shard_map/all_gather | solution.py:108
  8.7 314.0 %all-gather.14.cloned.1.call-start = ((), (), s32[]{:S(2)}) async-start(), calls=%async_computation.8 | async-start | bytes 8912896 | tf_op jit(solution)/shard_map/all_gather | solution.py:161
  9.9 166.7 %copy-start = (f32[128,2048]{1,0:T(8,128)}, f32[128,2048]{1,0:T(8,128)S(1)}, u32[]{:S(2)}) copy-start(f32[128,2048]{1,0:T(8,128)S(1)} %reshape.529) | copy-start | bytes 3145732
  12.0 164.6 %copy-start.29 = (f32[128]{0:T(128)}, f32[128]{0:T(128)S(1)}, u32[]{:S(2)}) copy-start(f32[128]{0:T(128)S(1)} %div.90) | copy-start | bytes 1540
  14.0 162.6 %copy-start.31 = (f32[128]{0:T(128)}, f32[128]{0:T(128)S(1)}, u32[]{:S(2)}) copy-start(f32[128]{0:T(128)S(1)} %rsqrt.13) | copy-start | bytes 1540
  63.2 192.5 %copy-start.21 = (f32[64,64]{1,0:T(8,128)}, f32[64,64]{1,0:T(8,128)S(1)}, u32[]{:S(2)}) copy-start(f32[64,64]{1,0:T(8,128)S(1)} %get-tuple-element.823) | copy-start | bytes 49156
  63.2 192.5 %copy-start.23 = (f32[64,64]{1,0:T(8,128)}, f32[64,64]{1,0:T(8,128)S(1)}, u32[]{:S(2)}) copy-start(f32[64,64]{1,0:T(8,128)S(1)} %get-tuple-element.824) | copy-start | bytes 49156
  180.5 218.0 %all-gather.12.cloned.1.call-start = ((), (), s32[]{:S(2)}) async-start(), calls=%async_computation.7 | async-start | bytes 8912896 | tf_op jit(solution)/shard_map/all_gather | solution.py:162
  183.0 389.7 %all-gather.24.cloned.1.call-start = ((), (), s32[]{:S(2)}) async-start(), calls=%async_computation.13 | async-start | bytes 8912896 | tf_op jit(solution)/shard_map/all_gather | solution.py:288
  254.0 318.7 %all-gather.22.cloned.1.call-start = ((), (), s32[]{:S(2)}) async-start(), calls=%async_computation.12 | async-start | bytes 8912896 | tf_op jit(solution)/shard_map/all_gather | solution.py:287
  257.1 501.4 %all-gather.18.cloned.1.call-start = ((), (), s32[]{:S(2)}) async-start(), calls=%async_computation.10 | async-start | bytes 34603008 | tf_op jit(solution)/shard_map/all_gather | solution.py:112
  257.8 696.6 %all-gather.20.cloned.1.call-start = ((), (), s32[]{:S(2)}) async-start(), calls=%async_computation.11 | async-start | bytes 34603008 | tf_op jit(solution)/shard_map/all_gather | solution.py:114
  258.6 915.7 %reduce-scatter.19.cloned.1.call-start = ((), (), s32[]{:S(2)}) async-start(), calls=%async_computation.17 | async-start | bytes 1081344
  627.4 131.0 %copy-start.1 = (f32[128,2048]{1,0:T(8,128)S(1)}, f32[128,2048]{1,0:T(8,128)}, u32[]{:S(2)}) copy-start(f32[128,2048]{1,0:T(8,128)} %copy-done) | copy-start | bytes 3145732
  627.4 131.0 %copy-start.20 = (f32[2048]{0:T(1024)S(1)}, f32[2048]{0:T(1024)}, u32[]{:S(2)}) copy-start(f32[2048]{0:T(1024)} %convert_element_type.123) | copy-start | bytes 24580
  627.4 131.0 %copy-start.27 = (f32[2048]{0:T(1024)S(1)}, f32[2048]{0:T(1024)}, u32[]{:S(2)}) copy-start(f32[2048]{0:T(1024)} %convert_element_type.124) | copy-start | bytes 24580
  758.5 196.0 %copy-start.5 = (bf16[128,2048]{1,0:T(8,128)(2,1)S(1)}, bf16[128,2048]{1,0:T(8,128)(2,1)}, u32[]{:S(2)}) copy-start(bf16[128,2048]{1,0:T(8,128)(2,1)} %copy-done.4) | copy-start | bytes 1572868
  775.7 201.9 %copy-start.18 = (f32[2048]{0:T(1024)S(1)}, f32[2048]{0:T(1024)}, u32[]{:S(2)}) copy-start(f32[2048]{0:T(1024)} %copy-done.17) | copy-start | bytes 24580
  999.0 251.6 %reduce-scatter.21.cloned.1.call-start = ((), (), s32[]{:S(2)}) async-start(), calls=%async_computation.18 | async-start | bytes 1081344
  1004.1 618.8 %reduce-scatter.15.cloned.1.call-start = ((), (), s32[]{:S(2)}) async-start(), calls=%async_computation.15 | async-start | bytes 17301504 | tf_op jit(solution)/shard_map/reduce_scatter | solution.py:365
  1013.5 1047.6 %reduce-scatter.13.cloned.1.call-start = ((), (), s32[]{:S(2)}) async-start(), calls=%async_computation.14 | async-start | bytes 51904512 | tf_op jit(solution)/shard_map/reduce_scatter | solution.py:359
  1033.8 2433.4 %reduce-scatter.17.cloned.1.call-start = ((), (), s32[]{:S(2)}) async-start(), calls=%async_computation.16 | async-start | bytes 69206016 | tf_op jit(solution)/shard_map/reduce_scatter | solution.py:228
  1058.7 3816.6 %reduce-scatter.23.cloned.1.call-start = ((), (), s32[]{:S(2)}) async-start(), calls=%async_computation.19 | async-start | bytes 69206016
  (32 other events, 1039.8 us)
Sparse Core Ops, SparseCore 0:
  10.9 155.5 all-gather.9
  169.5 77.3 all-gather.15
  249.6 72.9 all-gather.13
  325.2 73.1 all-gather.11
  400.5 85.9 all-gather.23
  489.1 74.4 all-gather.21
  566.6 191.7 all-gather.17
  761.4 192.9 all-gather.19
  999.2 118.4 reduce-scatter.18
  1119.8 130.7 reduce-scatter.20
  1253.5 369.3 reduce-scatter.14
  1629.8 431.2 reduce-scatter.12
  2064.0 1403.0 reduce-scatter.16
  3469.9 1405.3 reduce-scatter.22
where the time goes:
time: 4900 us; the launch traced here: 4880 us
  waiting for transfers between devices  4230 us (86%)
  matrix products  252 us (5%)
  local copies, waits for them, and re-layouts  210 us (4%)
  blocking collectives  146 us (3%)
    unnamed x17, waiting for transfers between devices  1480 us
    reduce_scatter x1, waiting for transfers between devices, body(): lax.psum_scatter(contract_rows(normed_two_low, inner_grad), ('ctx', 'fsdp...  1410 us
    reduce_scatter x1, waiting for transfers between devices, body(): lax.psum_scatter(contract_rows(normed_one_low, projected_grad), ('ctx', '...  438 us
    reduce_scatter x1, waiting for transfers between devices, body(): lax.psum_scatter(out_w_grad, ('ctx', 'fsdp'), scatter_dimension=0, tiled=...  368 us
    all_gather x1, waiting for transfers between devices, body(): lax.all_gather(down_weight, ('ctx', 'fsdp'), axis=0, tiled=True)  179 us
    all_gather x1, waiting for transfers between devices, body(): lax.all_gather(up_weight, ('ctx', 'fsdp'), axis=0, tiled=True)  116 us
    all_gather x1, waiting for transfers between devices, body(): lax.all_gather(qkv_weight, ('ctx', 'fsdp'), axis=0, tiled=True)  103 us
  transfers between devices with their start and end apart: 14, of which 11 were waited for; matrix products, arithmetic and copies ran while one was open for 9% of the time, Pallas kernels for 0%

commit v1 on v0

--- a/solution.py
+++ b/solution.py
@@ -1,6 +1,8 @@
 import jax
 import jax.numpy as jnp
 from jax import lax
+from jax.experimental import pallas as pl
+from jax.experimental.pallas import tpu as pltpu
 from jax.sharding import PartitionSpec as P
 
 HEAD = 256
@@ -76,7 +78,7 @@
     return (score_grad, probabilities.astype(jnp.bfloat16))
 
 
-def body(
+def general_body(
     hidden,
     cotangent,
     pairing,
@@ -384,7 +386,706 @@
     )
 
 
+MESH = pl.DeviceIdType.MESH
+CORES = 2
+LINE_Y = 2
+VMEM_BYTES = 60 * 2**20
+
+
+def split_fits(mesh):
+    return mesh.shape["ctx"] == 16 and mesh.shape["fsdp"] == 2
+
+
+class Place:
+    def __init__(self, ctx_count):
+        self.chips = ctx_count // CORES
+        self.line = self.chips // LINE_Y
+        index = lax.axis_index("ctx")
+        self.c = index % CORES
+        self.chip = index // CORES
+        self.y = self.chip % LINE_Y
+        self.z = self.chip // LINE_Y
+        self.x = lax.axis_index("fsdp")
+
+    def at(self, z, y, c, x):
+        return ((z * LINE_Y + y) * CORES + c, x)
+
+    def other_core(self):
+        return self.at(self.z, self.y, 1 - self.c, self.x)
+
+    def other_plane(self):
+        return self.at(self.z, self.y, self.c, 1 - self.x)
+
+    def other_y(self):
+        return self.at(self.z, 1 - self.y, self.c, self.x)
+
+    def plane_offsets(self):
+        return [(dz, dy) for dz in range(self.line) for dy in range(LINE_Y) if dz or dy]
+
+    def shifted(self, dz, dy):
+        return (self.z + dz) % self.line, (self.y + dy) % LINE_Y
+
+
+class Copies:
+    def __init__(self, send, recv, local):
+        self.send, self.recv, self.local = send, recv, local
+        self.remotes, self.locals = 0, 0
+
+    def remote(self, src, dst, device):
+        i = self.remotes
+        self.remotes += 1
+        return pltpu.make_async_remote_copy(
+            src_ref=src,
+            dst_ref=dst,
+            send_sem=self.send.at[i],
+            recv_sem=self.recv.at[i],
+            device_id=device,
+            device_id_type=MESH,
+        )
+
+    def inside(self, src, dst):
+        i = self.locals
+        self.locals += 1
+        return pltpu.make_async_copy(src, dst, self.local.at[i])
+
+
+def greet(place):
+    barrier = pltpu.get_barrier_semaphore()
+    partners = [place.other_core(), place.other_plane()]
+    for dz, dy in place.plane_offsets():
+        z, y = place.shifted(dz, dy)
+        partners.append(place.at(z, y, place.c, place.x))
+    for partner in partners:
+        pl.semaphore_signal(barrier, inc=1, device_id=partner, device_id_type=MESH)
+    pl.semaphore_wait(barrier, len(partners))
+
+
+class TokenGather:
+    def __init__(self, place, copies, own, whole):
+        self.place = place
+        self.whole = whole
+        c, chip, z, y = place.c, place.chip, place.z, place.y
+        self.first = copies.remote(own.at[1 - c], whole.at[chip, c], place.other_core())
+        self.mine = copies.inside(own.at[c], whole.at[chip, c])
+        last = place.line - 1
+        up = place.at(jnp.minimum(z + 1, last), y, c, place.x)
+        down = place.at(jnp.maximum(z - 1, 0), y, c, place.x)
+
+        def pair(zz):
+            return whole.at[jnp.clip(zz, 0, last) * LINE_Y + y]
+
+        self.ups = [copies.remote(pair(z - j), pair(z - j), up) for j in range(last)]
+        self.downs = [copies.remote(pair(z + j), pair(z + j), down) for j in range(last)]
+        self.over_own = copies.remote(pair(z), pair(z), place.other_y())
+        self.over_ups = [copies.remote(pair(z - 1 - j), pair(z - 1 - j), place.other_y()) for j in range(last)]
+        self.over_downs = [copies.remote(pair(z + 1 + j), pair(z + 1 + j), place.other_y()) for j in range(last)]
+        self.last = last
+
+    def start(self):
+        self.mine.start()
+        self.first.start()
+
+    def spread(self):
+        self.mine.wait()
+        self.first.wait_recv()
+        z = self.place.z
+        pl.when(z < self.last)(lambda: self.ups[0].start())
+        pl.when(z > 0)(lambda: self.downs[0].start())
+        self.over_own.start()
+
+    def step(self, j):
+        z, last = self.place.z, self.last
+
+        @pl.when(z - 1 - j >= 0)
+        def _():
+            self.ups[j].wait_recv()
+            if j + 1 < last:
+                pl.when(z < last)(lambda: self.ups[j + 1].start())
+            self.over_ups[j].start()
+
+        @pl.when(z + 1 + j <= last)
+        def _():
+            self.downs[j].wait_recv()
+            if j + 1 < last:
+                pl.when(z > 0)(lambda: self.downs[j + 1].start())
+            self.over_downs[j].start()
+
+    def finish(self):
+        z, last = self.place.z, self.last
+        self.over_own.wait_recv()
+        for j in range(last):
+            pl.when(z - 1 - j >= 0)(lambda: self.over_ups[j].wait_recv())
+            pl.when(z + 1 + j <= last)(lambda: self.over_downs[j].wait_recv())
+
+    def drain(self):
+        z, last = self.place.z, self.last
+        self.first.wait_send()
+        self.over_own.wait_send()
+        for j in range(last):
+            pl.when((z - j >= 0) & (z < last))(lambda: self.ups[j].wait_send())
+            pl.when((z + j <= last) & (z > 0))(lambda: self.downs[j].wait_send())
+            pl.when(z - 1 - j >= 0)(lambda: self.over_ups[j].wait_send())
+            pl.when(z + 1 + j <= last)(lambda: self.over_downs[j].wait_send())
+
+
+class WeightGather:
+    def __init__(self, place, copies, pieces, whole):
+        self.place = place
+        group = 2 * place.c + place.x
+        self.scattered = []
+        for dz, dy in place.plane_offsets():
+            z, y = place.shifted(dz, dy)
+            device = place.at(z, y, place.c, place.x)
+            for src, dst in pieces(z * LINE_Y + y, place.chip, group):
+                self.scattered.append(copies.remote(src, dst, device))
+        self.kept = [copies.inside(src, dst) for src, dst in pieces(place.chip, place.chip, group)]
+        mine = whole.at[:, group]
+        self.across = copies.remote(mine, mine, place.other_plane())
+        pair = whole.at[:, pl.ds(2 * place.c, 2)]
+        self.swap = copies.remote(pair, pair, place.other_core())
+
+    def scatter(self):
+        for copy in self.scattered + self.kept:
+            copy.start()
+
+    def cross(self):
+        for copy in self.kept:
+            copy.wait()
+        for copy in self.scattered:
+            copy.wait_recv()
+        self.across.start()
+
+    def share(self):
+        self.across.wait_recv()
+        self.swap.start()
+
+    def finish(self):
+        self.swap.wait_recv()
+
+    def drain(self):
+        for copy in self.scattered + [self.across, self.swap]:
+            copy.wait_send()
+
+
+def gather_kernel(
+    ctx_count,
+    hid,
+    cot,
+    qkv,
+    up,
+    down,
+    out,
+    small,
+    hid_all,
+    cot_all,
+    qkv_all,
+    up_all,
+    down_all,
+    out_all,
+    small_all,
+    send,
+    recv,
+    local,
+):
+    place = Place(ctx_count)
+    copies = Copies(send, recv, local)
+    width = out.shape[1]
+    head = qkv_all.shape[3] // 3
+    part = up_all.shape[3]
+
+    def qkv_pieces(to, row, group):
+        return [
+            (
+                qkv.at[:, pl.ds(pl.multiple_of(k * width + to * head, head), head)],
+                qkv_all.at[row, group, :, pl.ds(k * head, head)],
+            )
+            for k in range(3)
+        ]
+
+    def slice_pieces(source, whole):
+        return lambda to, row, group: [
+            (source.at[:, pl.ds(pl.multiple_of(to * part, part), part)], whole.at[row, group])
+        ]
+
+    hid_g = TokenGather(place, copies, hid, hid_all)
+    cot_g = TokenGather(place, copies, cot, cot_all)
+    small_g = WeightGather(place, copies, lambda to, row, group: [(small, small_all.at[row, group])], small_all)
+    qkv_g = WeightGather(place, copies, qkv_pieces, qkv_all)
+    up_g = WeightGather(place, copies, slice_pieces(up, up_all), up_all)
+    down_g = WeightGather(place, copies, slice_pieces(down, down_all), down_all)
+    group = 2 * place.c + place.x
+    out_mine = copies.inside(out, out_all.at[group])
+    out_across = copies.remote(out, out_all.at[group], place.other_plane())
+    out_pair = out_all.at[pl.ds(2 * place.c, 2)]
+    out_swap = copies.remote(out_pair, out_pair, place.other_core())
+
+    greet(place)
+    hid_g.start()
+    cot_g.start()
+    small_g.scatter()
+    qkv_g.scatter()
+    hid_g.spread()
+    out_mine.start()
+    out_across.start()
+    up_g.scatter()
+    small_g.cross()
+    hid_g.step(0)
+    qkv_g.cross()
+    small_g.share()
+    hid_g.step(1)
+    cot_g.spread()
+    hid_g.step(2)
+    down_g.scatter()
+    qkv_g.share()
+    cot_g.step(0)
+    up_g.cross()
+    cot_g.step(1)
+    cot_g.step(2)
+    out_mine.wait()
+    out_across.wait_recv()
+    out_swap.start()
+    down_g.cross()
+    up_g.share()
+    down_g.share()
+    hid_g.finish()
+    cot_g.finish()
+    for gather in (small_g, qkv_g, up_g, down_g):
+        gather.finish()
+    out_swap.wait_recv()
+    for gather in (hid_g, cot_g, small_g, qkv_g, up_g, down_g):
+        gather.drain()
+    out_across.wait_send()
+    out_swap.wait_send()
+
+
+def gather_all(ctx_count, hid, cot, qkv, up, down, out, small):
+    chips = ctx_count // CORES
+    rows = qkv.shape[0]
+    groups = CORES * 2
+    shapes = [
+        ((chips, CORES) + hid.shape[1:], hid.dtype),
+        ((chips, CORES) + cot.shape[1:], cot.dtype),
+        ((chips, groups, rows, qkv.shape[1] // chips), qkv.dtype),
+        ((chips, groups, rows, up.shape[1] // chips), up.dtype),
+        ((chips, groups, rows, down.shape[1] // chips), down.dtype),
+        ((groups, rows, out.shape[1]), out.dtype),
+        ((chips, groups) + small.shape, small.dtype),
+    ]
+    operands = (hid, cot, qkv, up, down, out, small)
+    anywhere = pl.BlockSpec(memory_space=pl.ANY)
+    return pl.pallas_call(
+        lambda *refs: gather_kernel(ctx_count, *refs),
+        out_shape=[jax.ShapeDtypeStruct(*shape) for shape in shapes],
+        in_specs=[anywhere] * len(operands),
+        out_specs=[anywhere] * len(shapes),
+        scratch_shapes=[
+            pltpu.SemaphoreType.DMA((88,)),
+            pltpu.SemaphoreType.DMA((88,)),
+            pltpu.SemaphoreType.DMA((16,)),
+        ],
+        compiler_params=pltpu.CompilerParams(
+            collective_id=0, has_side_effects=True, vmem_limit_bytes=VMEM_BYTES
+        ),
+        name="gather_all",
+    )(*operands)
+
+
+def add_into(total, other, steps):
+    @pl.loop(0, steps)
+    def _(k):
+        both = total[k].astype(jnp.float32) + other[k].astype(jnp.float32)
+        total[k] = both.astype(total.dtype)
+
+
+class GradScatter:
+    def __init__(self, place, copies, partial, kept, from_core, from_plane, result):
+        self.place = place
+        c, x, chip = place.c, place.x, place.chip
+        self.kept, self.from_core, self.from_plane = kept, from_core, from_plane
+        self.load = copies.inside(partial.at[:, pl.ds(2 * c, 2)], kept)
+        self.swap = copies.remote(partial.at[:, pl.ds(2 * (1 - c), 2)], from_core, place.other_core())
+        self.across = copies.remote(kept.at[:, 1 - x], from_plane, place.other_plane())
+        self.scattered = []
+        for dz, dy in place.plane_offsets():
+            z, y = place.shifted(dz, dy)
+            self.scattered.append(
+                copies.remote(kept.at[z * LINE_Y + y, x], result.at[chip], place.at(z, y, c, x))
+            )
+        self.own = copies.inside(kept.at[chip, x], result.at[chip])
+
+    def start(self):
+        self.load.start()
+        self.swap.start()
+
+    def cross(self):
+        self.load.wait()
+        self.swap.wait_recv()
+        add_into(self.kept, self.from_core, self.kept.shape[0])
+        self.across.start()
+
+    def scatter(self):
+        self.across.wait_recv()
+        x = self.place.x
+
+        @pl.loop(0, self.kept.shape[0])
+        def _(k):
+            both = self.kept[k, x].astype(jnp.float32) + self.from_plane[k].astype(jnp.float32)
+            self.kept[k, x] = both.astype(self.kept.dtype)
+
+        for copy in self.scattered + [self.own]:
+            copy.start()
+
+    def finish(self):
+        self.own.wait()
+        for copy in self.scattered:
+            copy.wait_recv()
+
+    def drain(self):
+        for copy in self.scattered + [self.swap, self.across]:
+            copy.wait_send()
+
+
+class TokenScatter:
+    def __init__(self, place, copies, partial, kept, from_y, from_z, total, result):
+        self.place = place
+        z, y, c, x = place.z, place.y, place.c, place.x
+        self.kept, self.from_y, self.from_z, self.total = kept, from_y, from_z, total
+        self.load = copies.inside(partial.at[:, y], kept)
+        self.over = copies.remote(partial.at[:, 1 - y], from_y, place.other_y())
+        self.along = []
+        for dz in range(1, place.line):
+            to = (z + dz) % place.line
+            self.along.append(copies.remote(kept.at[to], from_z.at[dz - 1], place.at(to, y, c, x)))
+        self.swap = copies.remote(total.at[1 - c], result.at[c], place.other_core())
+        self.own = copies.inside(total.at[c], result.at[c])
+
+    def start(self):
+        self.load.start()
+        self.over.start()
+
+    def along_z(self):
+        self.load.wait()
+        self.over.wait_recv()
+        add_into(self.kept, self.from_y, self.kept.shape[0])
+        for copy in self.along:
+            copy.start()
+
+    def reduce(self):
+        for copy in self.along:
+            copy.wait_recv()
+        z = self.place.z
+
+        @pl.loop(0, CORES)
+        def _(k):
+            total = self.kept[z, k].astype(jnp.float32)
+            for dz in range(self.place.line - 1):
+                total = total + self.from_z[dz, k].astype(jnp.float32)
+            self.total[k] = total
+
+        self.swap.start()
+        self.own.start()
+
+    def finish(self):
+        self.own.wait()
+        self.swap.wait_recv()
+
+    def drain(self):
+        self.over.wait_send()
+        for copy in self.along:
+            copy.wait_send()
+        self.swap.wait_send()
+
+
+def scatter_kernel(ctx_count, count_grads, *refs):
+    place = Place(ctx_count)
+    take = iter(refs)
+    grads = [next(take) for _ in range(count_grads)]
+    grad_out, out_part, hid_part = next(take), next(take), next(take)
+    grad_results = [next(take) for _ in range(count_grads)]
+    grad_out_result, out_result, hid_result = next(take), next(take), next(take)
+    grad_scratch = [[next(take) for _ in range(3)] for _ in range(count_grads)]
+    grad_out_scratch = [next(take) for _ in range(3)]
+    token_scratch = [[next(take) for _ in range(4)] for _ in range(2)]
+    copies = Copies(next(take), next(take), next(take))
+    scatters = [
+        GradScatter(place, copies, grads[i], *grad_scratch[i], grad_results[i]) for i in range(count_grads)
+    ]
+    outs_s = TokenScatter(place, copies, out_part, *token_scratch[0], out_result)
+    hid_s = TokenScatter(place, copies, hid_part, *token_scratch[1], hid_result)
+    c, x = place.c, place.x
+    kept, from_core, from_plane = grad_out_scratch
+    load = copies.inside(grad_out.at[pl.ds(2 * c, 2)], kept)
+    swap = copies.remote(grad_out.at[pl.ds(2 * (1 - c), 2)], from_core, place.other_core())
+    across = copies.remote(kept.at[1 - x], from_plane, place.other_plane())
+    own = copies.inside(kept.at[x], grad_out_result)
+
+    greet(place)
+    for scatter in scatters:
+        scatter.start()
+    load.start()
+    swap.start()
+    outs_s.start()
+    for scatter in scatters:
+        scatter.cross()
+    load.wait()
+    swap.wait_recv()
+    add_into(kept, from_core, 2)
+    across.start()
+    hid_s.start()
+    scatters[0].scatter()
+    outs_s.along_z()
+    for scatter in scatters[1:]:
+        scatter.scatter()
+    across.wait_recv()
+    kept[x] = (kept[x].astype(jnp.float32) + from_plane[...].astype(jnp.float32)).astype(kept.dtype)
+    own.start()
+    hid_s.along_z()
+    outs_s.reduce()
+    hid_s.reduce()
+    for scatter in scatters + [outs_s, hid_s]:
+        scatter.finish()
+    own.wait()
+    for scatter in scatters + [outs_s, hid_s]:
+        scatter.drain()
+    swap.wait_send()
+    across.wait_send()
+
+
+def scatter_all(ctx_count, grads, grad_out, out_part, hid_part):
+    chips = ctx_count // CORES
+    line = chips // LINE_Y
+    count = len(grads)
+    grad_out_shape = grad_out.shape[1:]
+    token = (CORES,) + out_part.shape[3:]
+    out_shape = [jax.ShapeDtypeStruct((chips,) + g.shape[2:], g.dtype) for g in grads]
+    out_shape += [jax.ShapeDtypeStruct(grad_out_shape, grad_out.dtype)]
+    out_shape += [jax.ShapeDtypeStruct(token, jnp.float32)] * 2
+    scratch = []
+    for g in grads:
+        scratch.append(pltpu.VMEM((chips, 2) + g.shape[2:], g.dtype))
+        scratch.append(pltpu.VMEM((chips, 2) + g.shape[2:], g.dtype))
+        scratch.append(pltpu.VMEM((chips,) + g.shape[2:], g.dtype))
+    scratch.append(pltpu.VMEM((2,) + grad_out_shape, grad_out.dtype))
+    scratch.append(pltpu.VMEM((2,) + grad_out_shape, grad_out.dtype))
+    scratch.append(pltpu.VMEM(grad_out_shape, grad_out.dtype))
+    for part in (out_part, hid_part):
+        scratch.append(pltpu.VMEM((line,) + token, part.dtype))
+        scratch.append(pltpu.VMEM((line,) + token, part.dtype))
+        scratch.append(pltpu.VMEM((line - 1,) + token, part.dtype))
+        scratch.append(pltpu.VMEM(token, jnp.float32))
+    operands = list(grads) + [grad_out, out_part, hid_part]
+    anywhere = pl.BlockSpec(memory_space=pl.ANY)
+    return pl.pallas_call(
+        lambda *refs: scatter_kernel(ctx_count, count, *refs),
+        out_shape=out_shape,
+        in_specs=[anywhere] * len(operands),
+        out_specs=[anywhere] * len(out_shape),
+        scratch_shapes=scratch
+        + [
+            pltpu.SemaphoreType.DMA((64,)),
+            pltpu.SemaphoreType.DMA((64,)),
+            pltpu.SemaphoreType.DMA((16,)),
+        ],
+        compiler_params=pltpu.CompilerParams(
+            collective_id=1, has_side_effects=True, vmem_limit_bytes=VMEM_BYTES
+        ),
+        name="scatter_all",
+    )(*operands)
+
+
+def split_body(
+    hidden,
+    cotangent,
+    pairing,
+    ln1_gain,
+    ln1_bias,
+    qkv_weight,
+    qkv_bias,
+    out_weight,
+    out_bias,
+    ln2_gain,
+    ln2_bias,
+    up_weight,
+    up_bias,
+    down_weight,
+    down_bias,
+):
+    local_rows, seq_count, width = hidden.shape
+    ctx_count = lax.axis_size("ctx")
+    chips = ctx_count // CORES
+    total_rows = local_rows * ctx_count
+    scaling = HEAD ** (-0.5)
+    f32, b16 = jnp.float32, jnp.bfloat16
+    head_id = lax.axis_index("ctx") // CORES
+
+    owned = width // (ctx_count * 2)
+    vectors = (ln1_gain, ln1_bias, ln2_gain, ln2_bias, out_bias, down_bias, qkv_bias, up_bias)
+    flat = jnp.concatenate([v.astype(f32) for v in vectors])
+    used = flat.shape[0]
+    small_rows = 8 * (-(-used // 1024))
+    small = jnp.pad(flat, (0, small_rows * 128 - used)).reshape(small_rows, 128)
+
+    hid_all, cot_all, w_qkv, w_up, w_down, w_out, small_all = gather_all(
+        ctx_count,
+        jnp.swapaxes(hidden, 0, 1),
+        jnp.swapaxes(cotangent, 0, 1),
+        qkv_weight,
+        up_weight,
+        down_weight,
+        out_weight,
+        small,
+    )
+    w_qkv = w_qkv.reshape(width, -1)
+    w_up = w_up.reshape(width, -1)
+    w_down = w_down.reshape(width, -1)
+    w_out = w_out.reshape(-1, width)
+    part = w_up.shape[1]
+    smalls = small_all.reshape(ctx_count * 2, -1)
+    full = []
+    at = 0
+    for v in vectors:
+        full.append(smalls[:, at : at + v.shape[0]].reshape(-1))
+        at += v.shape[0]
+    gain_one, shift_one, gain_two, shift_two, b_out, b_down, b_qkv, b_up = full
+    b_qkv = lax.dynamic_slice_in_dim(b_qkv.reshape(3, -1), head_id * HEAD, HEAD, axis=1).reshape(-1)
+    b_up = lax.dynamic_slice_in_dim(b_up, head_id * part, part)
+
+    x = hid_all.reshape(total_rows, width).astype(f32)
+    cot = cot_all.reshape(total_rows, width)
+    average = jnp.mean(x, axis=-1, keepdims=True)
+    spread = jnp.mean((x - average) ** 2, axis=-1, keepdims=True)
+    xhat = (x - average) * lax.rsqrt(spread + LN_EPSILON)
+    norm_one = (xhat * gain_one + shift_one).astype(b16)
+    norm_two = (xhat * gain_two + shift_two).astype(b16)
+    positions = row_positions(pairing, jnp.int32(0), total_rows, local_rows // 2, ctx_count)
+
+    projected = jnp.dot(norm_one, w_qkv, preferred_element_type=f32) + b_qkv
+    (query_f, key_f), rotation_pull = jax.vjp(
+        lambda q, k: (rotate(q, positions), rotate(k, positions)),
+        projected[:, :HEAD],
+        projected[:, HEAD : 2 * HEAD],
+    )
+    query, key = query_f.astype(b16), key_f.astype(b16)
+    value = projected[:, 2 * HEAD :].astype(b16)
+    scores = contract_cols(query, key) * scaling
+    allowed = positions[None, :] <= positions[:, None]
+    highest = jnp.max(jnp.where(allowed, scores, VERY_LOW), axis=-1, keepdims=True)
+    weights = jnp.where(allowed, jnp.exp(scores - highest), 0.0)
+    probs = weights / jnp.sum(weights, axis=-1, keepdims=True)
+    probs_low = probs.astype(b16)
+    attended = jnp.dot(probs_low, value, preferred_element_type=f32)
+    attended_low = attended.astype(b16)
+
+    inner = jnp.dot(norm_two, w_up, preferred_element_type=f32) + b_up
+    activated_f, gelu_pull = jax.vjp(gelu_exact, inner)
+    activated = activated_f.astype(b16)
+    out_part = jnp.dot(attended_low, w_out, preferred_element_type=f32) + contract_cols(activated, w_down)
+
+    up_grad = jnp.dot(cot, w_down, preferred_element_type=f32)
+    inner_grad = gelu_pull(up_grad)[0].astype(b16)
+    norm_two_grad = contract_cols(inner_grad, w_up)
+    grad_up = contract_rows(norm_two, inner_grad)
+    grad_down = contract_rows(cot, activated)
+
+    attended_grad = contract_cols(cot, w_out).astype(b16)
+    grad_out = contract_rows(attended_low, cot)
+    row_delta = jnp.sum(attended_grad.astype(f32) * attended, axis=-1, keepdims=True)
+    prob_grad = contract_cols(attended_grad, value)
+    score_grad = (probs * (prob_grad - row_delta)).astype(b16)
+    query_grad = jnp.dot(score_grad, key, preferred_element_type=f32) * scaling
+    key_grad = contract_rows(score_grad, query) * scaling
+    value_grad = contract_rows(probs_low, attended_grad)
+    query_pre, key_pre = rotation_pull((query_grad, key_grad))
+    projected_grad = jnp.concatenate([query_pre, key_pre, value_grad], axis=1).astype(b16)
+    norm_one_grad = contract_cols(projected_grad, w_qkv)
+    grad_qkv = contract_rows(norm_one, projected_grad)
+    hid_part = norm_one_grad * gain_one + norm_two_grad * gain_two
+
+    cot_sum = jnp.where(head_id == 0, jnp.sum(cot.astype(f32), axis=0), 0.0)
+    qkv_sum = jnp.sum(projected_grad.astype(f32), axis=0).reshape(3, HEAD)
+    qkv_sum = lax.dynamic_update_slice_in_dim(
+        jnp.zeros((3, width), f32), qkv_sum, head_id * HEAD, axis=1
+    )
+    up_sum = lax.dynamic_update_slice_in_dim(
+        jnp.zeros((part * chips,), f32),
+        jnp.sum(inner_grad.astype(f32), axis=0),
+        head_id * part,
+        axis=0,
+    )
+    sums = (
+        jnp.sum(norm_one_grad * xhat, axis=0),
+        jnp.sum(norm_one_grad, axis=0),
+        jnp.sum(norm_two_grad * xhat, axis=0),
+        jnp.sum(norm_two_grad, axis=0),
+        cot_sum,
+        qkv_sum,
+        up_sum,
+    )
+    tiles = jnp.concatenate([v.reshape(ctx_count * 2, -1) for v in sums], axis=1)
+    tile_used = tiles.shape[1]
+    tile_rows = 8 * (-(-tile_used // 1024))
+    tiles = jnp.pad(tiles, ((0, 0), (0, tile_rows * 128 - tile_used)))
+
+    groups = 2 * CORES
+    line = chips // LINE_Y
+    by_owner = (chips, groups, owned, -1)
+    by_rows = (line, LINE_Y, CORES, local_rows, width)
+    small_sum, qkv_sum, up_sum, down_sum, out_sum, out_rows, hid_rows = scatter_all(
+        ctx_count,
+        [
+            tiles.reshape(chips, groups, tile_rows, 128),
+            grad_qkv.astype(b16).reshape(by_owner),
+            grad_up.astype(b16).reshape(by_owner),
+            grad_down.astype(b16).reshape(by_owner),
+        ],
+        grad_out.astype(b16).reshape(groups, owned, width),
+        out_part.astype(b16).reshape(by_rows),
+        hid_part.astype(b16).reshape(by_rows),
+    )
+
+    own = hidden.astype(f32)
+    output = (own + jnp.swapaxes(out_rows, 0, 1) + (b_out + b_down)).astype(b16)
+    average = jnp.mean(own, axis=-1, keepdims=True)
+    spread = jnp.mean((own - average) ** 2, axis=-1, keepdims=True)
+    scale = lax.rsqrt(spread + LN_EPSILON)
+    xhat = (own - average) * scale
+    e = jnp.swapaxes(hid_rows, 0, 1)
+    grad_hidden = cotangent.astype(f32) + scale * (
+        e - jnp.mean(e, axis=-1, keepdims=True) - xhat * jnp.mean(e * xhat, axis=-1, keepdims=True)
+    )
+    mine = jnp.sum(small_sum, axis=0).reshape(-1)
+    cuts = []
+    at = 0
+    for v in sums:
+        step = v.size // (ctx_count * 2)
+        cuts.append(mine[at : at + step])
+        at += step
+
+    def columns(pieces, thirds):
+        rows = pieces.shape[1]
+        split = pieces.astype(f32).reshape(chips, rows, thirds, -1)
+        return jnp.transpose(split, (1, 2, 0, 3)).reshape(rows, -1)
+
+    return (
+        output,
+        grad_hidden,
+        cuts[0],
+        cuts[1],
+        columns(qkv_sum, 3),
+        cuts[5],
+        out_sum.astype(f32),
+        cuts[4],
+        cuts[2],
+        cuts[3],
+        columns(up_sum, 1),
+        cuts[6],
+        columns(down_sum, 1),
+        cuts[4],
+    )
+
+
 def solution(mesh):
+    body = split_body if split_fits(mesh) else general_body
     return jax.shard_map(
         body,
         mesh=mesh,

time: 4900 us -> 522 us (0.11)
  waiting for transfers between devices: 4230 us -> 0 us
  Pallas kernels: 0 us -> 369 us
  local copies, waits for them, and re-layouts: 210 us -> 27.1 us
  matrix products: 252 us -> 95.3 us
  blocking collectives: 146 us -> 0 us
    reduce_scatter x3 -> x0, waiting for transfers between devices: 2210 us -> none  [the longest x1 1410 us: body(): lax.psum_scatter(contract_rows(normed_two_low, inner_grad), ('ctx', 'fsdp...]
    unnamed x17 -> x0, waiting for transfers between devices: 1480 us -> none
    all_gather x8 -> x0, waiting for transfers between devices: 531 us -> none  [the longest x1 179 us: body(): lax.all_gather(down_weight, ('ctx', 'fsdp'), axis=0, tiled=True)]
    pallas_call x0 -> x2, Pallas kernels: none -> 369 us  [the longest x1 225 us: scatter_all(): pl.pallas_call(lambda *refs: scatter_kernel(ctx_count, count, *refs), out...]
    all_gather x3 -> x0, blocking collectives: 104 us -> none  [the longest x1 51.2 us: body(): lax.all_gather(up_bias, ('ctx', 'fsdp'), axis=0, tiled=True)]
    dot_general x16 -> x6, matrix products: 120 us -> 36 us  [the longest x1 17.5 us: split_body(): inner = jnp.dot(norm_two, w_up, preferred_element_type=f32) + b_up]
    dynamic_slice x14 -> x2, local copies, waits for them, and re-layouts: 69.9 us -> 0.02 us  [the longest x1 0.01 us: split_body(): lax.dynamic_slice_in_dim(b_qkv.reshape(3, -1), head_id * HEAD, HEAD, axis=1)]
    unnamed x126 -> x55, local copies, waits for them, and re-layouts: 84 us -> 14.7 us
  transfers between devices with their start and end apart: 14 -> 0, of which waited for: 11 -> 0; matrix products, arithmetic and copies ran while one was open for 9% -> 0% of each run, Pallas kernels for 0% -> 0%
where the time goes in v1:
time: 522 us; the launch traced here: 518 us
  Pallas kernels  369 us (71%)
  matrix products  95.3 us (18%)
  local copies, waits for them, and re-layouts  27.1 us (5%)
  other arithmetic  25.4 us (5%)
    pallas_call x1, Pallas kernels, scatter_all(): pl.pallas_call(lambda *refs: scatter_kernel(ctx_count, count, *refs), out...  225 us
    pallas_call x1, Pallas kernels, gather_all(): pl.pallas_call(lambda *refs: gather_kernel(ctx_count, *refs), out_shape=[...  144 us
    dot_general x6, matrix products, contract_cols(): lax.dot_general(left, right, (((1,), (1,)), ((), ())), preferred_element_...  29.8 us
    dot_general x6, matrix products, contract_rows(): lax.dot_general(left, right, (((0,), (0,)), ((), ())), preferred_element_...  29.5 us
    dot_general x1, matrix products, split_body(): inner = jnp.dot(norm_two, w_up, preferred_element_type=f32) + b_up  17.5 us
    unnamed x55, local copies, waits for them, and re-layouts  14.7 us

profile of v1, /device:TPU:9, one launch (start us, length us, event | category | flops | bytes accessed | tf_op | source)
XLA Modules:
  0.0 518.3 jit_solution(997590890736942497)
XLA Ops:
  3.4 5.4 %concatenate.33 = bf16[832]{0:T(1024)(128)(2,1)S(1)} concatenate(bf16[64]{0:T(256)(128)(2,1)} %param.18, bf16[64]{0:T(256)(128)(2,1)} %param.19, bf16[64]{0:T(256)(128)(2,1)} %param.24, bf16[64]{0:T(256)(128)(2,1)} %param.25, bf16[64]{0:T(256)(128)(2,1)} %param.23, bf16[64]{0:T(256)(128)(2,1)} %param.29, bf16[192]{0:T(256)(128)(2,1)} %param.21, bf16[256]{0:T(256)(128)(2,1)} %param.27), dimensions={0} | concatenate | bytes 3328 | tf_op jit(solution)/shard_map/concatenate | solution.py:923
  10.7 2.0 copy.98
  12.7 2.0 copy.99
  14.7 144.1 %gather_all.1 = (bf16[8,2,64,2048]{3,2,1,0:T(8,128)(2,1)}, bf16[8,2,64,2048]{3,2,1,0:T(8,128)(2,1)}, bf16[8,4,64,768]{3,2,1,0:T(8,128)(2,1)}, bf16[8,4,64,1024]{...) custom-call(bf16[2,64,2048]{2,1,0:T(8,128)(2,1)} %bitcast.131, ...), custom_call_target="tpu_custom_call" | custom-call | tf_op jit(solution)/shard_map/gather_all/pallas_call | solution.py:676
  159.7 2.8 convert_reduce_fusion.1
  162.6 5.0 convert_reduce_fusion
  168.5 3.6 convolution_convert_fusion.5
  172.1 4.4 add_convert_fusion.4
  176.5 3.6 fusion.64
  188.5 4.6 convolution_convert_fusion.3
  193.1 17.5 %multiply_convert_fusion = (bf16[1024,1024]{0,1:T(8,128)(2,1)}, f32[1024,1024]{0,1:T(8,128)}, f32[1024,1024]{0,1:T(8,128)}) fusion(f32[1024]{0:T(1024)S(1)} %dynamic_slice.7, bf16[1024,2048]{1,0:T(8,128)(2,1)S(1)} %bitcast.127, bf16[2048,1024]{1,0:T(8,128)(2,1)} %bitcast.146), kind=kOutput, calls=%fused_computation.18 | convolution fusion | flops 4364173312 | bytes 18878464 | tf_op jit(solution)/shard_map/dot_general | solution.py:979
  210.6 10.1 %convert_reduce_fusion.2 = (f32[1024]{0:T(1024)S(1)}, bf16[1024,1024]{0,1:T(8,128)(2,1)}) fusion(f32[1024,1024]{0,1:T(8,128)} %get-tuple-element.105, f32[1024,1024]{0,1:T(8,128)} %get-tuple-element.153, f32[1024]{0:T(1024)S(1)} %dynamic_slice.7, bf16[1024,2048]{1,0:T(8,128)(2,1)S(1)} %bitcast.126, bf16[2048,1024]{1,0:T(8,128)(2,1)S(1)} %bitcast.148), kind=kOutput, calls=%fused_computation.19 | convolution fusion | flops 4312792064 | bytes 18882560 | tf_op jit(solution)/shard_map/dot_general | solution.py:984
  221.0 9.6 %convolution_convert_fusion = bf16[2048,1024]{1,0:T(8,128)(2,1)} fusion(bf16[1024,2048]{1,0:T(8,128)(2,1)} %bitcast.125, bf16[1024,1024]{0,1:T(8,128)(2,1)} %get-tuple-element.104), kind=kOutput, calls=%fused_computation.35 | convolution fusion | flops 4297064448 | bytes 10485760 | tf_op jit(solution)/shard_map/dot_general | solution.py:54
  230.5 4.5 fusion.68
  235.1 3.3 add_convert_fusion.1
  239.2 6.9 %fusion.67 = f32[1024,2048]{1,0:T(8,128)} fusion(bf16[1024,1024]{0,1:T(8,128)(2,1)S(1)} %copy-done.18, bf16[2048,1024]{1,0:T(8,128)(2,1)S(1)} %bitcast.147), kind=kOutput, calls=%fused_computation.155 | convolution fusion | flops 4294967296 | bytes 14680064 | tf_op jit(solution)/shard_map/dot_general | solution.py:60
  246.2 13.0 %fusion.56 = (f32[2048]{0:T(1024)S(1)}, f32[2048]{0:T(1024)S(1)}, bf16[1024,2048]{1,0:T(8,128)(2,1)}, f32[2048]{0:T(1024)S(1)}, f32[2048]{0:T(1024)S(1)}, /*inde...) fusion(f32[1024]{0:T(1024)S(1)} %rsqrt.21, f32[1024]{0:T(1024)S(1)} %div.63, ...), kind=kOutput, calls=%fused_computation.146 | convolution fusion | flops 3265781760 | bytes 29958144 | tf_op jit(solution)/shard_map/dot_general | solution.py:60
  260.3 7.6 %convolution_convert_fusion.2 = bf16[2048,768]{1,0:T(8,128)(2,1)} fusion(bf16[1024,2048]{1,0:T(8,128)(2,1)} %get-tuple-element.114, bf16[1024,256]{0,1:T(8,128)(2,1)S(1)} %convolution_convert_fusion.4, bf16[1024,256]{0,1:T(8,128)(2,1)S(1)} %add_convert_fusion.7, bf16[1024,256]{0,1:T(8,128)(2,1)S(1)} %add_convert_fusion.8), kind=kOutput, calls=%fused_computation.37 | convolution fusion | flops 3227516928 | bytes 8912896 | tf_op jit(solution)/shard_map/dot_general | solution.py:54
  267.9 6.2 %convolution_convert_fusion.1 = bf16[2048,1024]{1,0:T(8,128)(2,1)} fusion(bf16[1024,2048]{1,0:T(8,128)(2,1)S(1)} %copy-done.17, bf16[1024,1024]{0,1:T(8,128)(2,1)S(1)} %copy-done.19), kind=kOutput, calls=%fused_computation.36 | convolution fusion | flops 4297064448 | bytes 10485760 | tf_op jit(solution)/shard_map/dot_general | solution.py:54
  274.1 225.2 %scatter_all.1 = (f32[8,8,128]{2,1,0:T(8,128)}, bf16[8,64,768]{2,1,0:T(8,128)(2,1)}, bf16[8,64,1024]{2,1,0:T(8,128)(2,1)}, bf16[8,64,1024]{2,1,0:T(8,128)(2,1)},...) custom-call(f32[8,4,8,128]{3,2,1,0:T(8,128)} %bitcast.141, ...), custom_call_target="tpu_custom_call" | custom-call | tf_op jit(solution)/shard_map/scatter_all/pallas_call | solution.py:878
  500.9 2.3 fusion.17
  503.3 1.8 copy.77
  509.0 2.6 reshape.379
  512.6 1.6 copy.84
  (121 shorter events, 27.3 us)
Async XLA Ops:
  162.6 5.8 %copy-start.6 = (bf16[4,64,2048]{2,1,0:T(8,128)(2,1)S(1)}, bf16[4,64,2048]{2,1,0:T(8,128)(2,1)}, u32[]{:S(2)}) copy-start(bf16[4,64,2048]{2,1,0:T(8,128)(2,1)} %get-tuple-element.32) | copy-start | bytes 3145732
  168.5 3.6 copy-start
  172.1 4.4 copy-start.15
  188.5 4.6 copy-start.4
  193.1 17.5 %copy-start.3 = (bf16[8,2,64,2048]{3,2,1,0:T(8,128)(2,1)S(1)}, bf16[8,2,64,2048]{3,2,1,0:T(8,128)(2,1)}, u32[]{:S(2)}) copy-start(bf16[8,2,64,2048]{3,2,1,0:T(8,128)(2,1)} %get-tuple-element.31) | copy-start | bytes 12582916
  193.1 17.5 %copy-start.13 = (bf16[8,4,64,1024]{3,2,1,0:T(8,128)(2,1)S(1)}, bf16[8,4,64,1024]{3,2,1,0:T(8,128)(2,1)}, u32[]{:S(2)}) copy-start(bf16[8,4,64,1024]{3,2,1,0:T(8,128)(2,1)} %get-tuple-element.34) | copy-start | bytes 12582916
  220.9 9.6 %copy-start.14 = (bf16[8,4,64,1024]{3,2,1,0:T(8,128)(2,1)S(1)}, bf16[8,4,64,1024]{3,2,1,0:T(8,128)(2,1)}, u32[]{:S(2)}) copy-start(bf16[8,4,64,1024]{3,2,1,0:T(8,128)(2,1)} %get-tuple-element.34) | copy-start | bytes 12582916
  221.0 9.6 %copy-start.20 = (bf16[1024,1024]{0,1:T(8,128)(2,1)S(1)}, bf16[1024,1024]{0,1:T(8,128)(2,1)}, u32[]{:S(2)}) copy-start(bf16[1024,1024]{0,1:T(8,128)(2,1)} %get-tuple-element.104) | copy-start | bytes 6291460
  235.1 3.4 copy-start.12
  235.1 4.1 copy-start.18
  239.2 6.9 %copy-start.1 = (bf16[8,2,64,2048]{3,2,1,0:T(8,128)(2,1)S(1)}, bf16[8,2,64,2048]{3,2,1,0:T(8,128)(2,1)}, u32[]{:S(2)}) copy-start(bf16[8,2,64,2048]{3,2,1,0:T(8,128)(2,1)} %get-tuple-element.28) | copy-start | bytes 12582916
  239.2 6.9 %copy-start.16 = (bf16[8,4,64,768]{3,2,1,0:T(8,128)(2,1)S(1)}, bf16[8,4,64,768]{3,2,1,0:T(8,128)(2,1)}, u32[]{:S(2)}) copy-start(bf16[8,4,64,768]{3,2,1,0:T(8,128)(2,1)} %get-tuple-element.30) | copy-start | bytes 9437188
  260.3 7.6 %copy-start.17 = (bf16[1024,2048]{1,0:T(8,128)(2,1)S(1)}, bf16[1024,2048]{1,0:T(8,128)(2,1)}, u32[]{:S(2)}) copy-start(bf16[1024,2048]{1,0:T(8,128)(2,1)} %get-tuple-element.113) | copy-start | bytes 12582916
  260.3 7.6 %copy-start.19 = (bf16[1024,1024]{0,1:T(8,128)(2,1)S(1)}, bf16[1024,1024]{0,1:T(8,128)(2,1)}, u32[]{:S(2)}) copy-start(bf16[1024,1024]{0,1:T(8,128)(2,1)} %get-tuple-element.107) | copy-start | bytes 6291460
  274.1 225.2 %copy-start.2 = (bf16[64,2,2048]{2,1,0:T(2,128)(2,1)S(1)}, bf16[64,2,2048]{2,1,0:T(2,128)(2,1)}, u32[]{:S(2)}) copy-start(bf16[64,2,2048]{2,1,0:T(2,128)(2,1)} %param.15) | copy-start | bytes 1572868
  274.1 226.8 %copy-start.5 = (bf16[64,2,2048]{2,1,0:T(2,128)(2,1)S(1)}, bf16[64,2,2048]{2,1,0:T(2,128)(2,1)}, u32[]{:S(2)}) copy-start(bf16[64,2,2048]{2,1,0:T(2,128)(2,1)} %param.16) | copy-start | bytes 1572868
  499.3 5.7 %copy-start.10 = (f32[8,8,128]{2,1,0:T(8,128)S(1)}, f32[8,8,128]{2,1,0:T(8,128)}, u32[]{:S(2)}) copy-start(f32[8,8,128]{2,1,0:T(8,128)} %get-tuple-element.37) | copy-start | bytes 98308
  500.9 7.3 %copy-start.9 = (bf16[64,2048]{1,0:T(8,128)(2,1)S(1)}, bf16[64,2048]{1,0:T(8,128)(2,1)}, u32[]{:S(2)}) copy-start(bf16[64,2048]{1,0:T(8,128)(2,1)} %get-tuple-element.39) | copy-start | bytes 786436
  506.9 10.7 %copy-start.11 = (f32[64]{0:T(128)}, f32[64]{0:T(128)S(1)}, u32[]{:S(2)}) copy-start(f32[64]{0:T(128)S(1)} %get-tuple-element.185) | copy-start | bytes 772
  509.0 5.2 copy-start.8
  514.2 1.7 copy-start.7

commit v2 on v1

--- a/solution.py
+++ b/solution.py
@@ -431,9 +431,14 @@
         self.send, self.recv, self.local = send, recv, local
         self.remotes, self.locals = 0, 0
 
+    def reserve(self, count):
+        self.remotes += count
+        return self.remotes - count
+
     def remote(self, src, dst, device):
-        i = self.remotes
-        self.remotes += 1
+        return self.remote_at(self.reserve(1), src, dst, device)
+
+    def remote_at(self, i, src, dst, device):
         return pltpu.make_async_remote_copy(
             src_ref=src,
             dst_ref=dst,
@@ -465,14 +470,17 @@
         self.place = place
         self.whole = whole
         c, chip, z, y = place.c, place.chip, place.z, place.y
-        self.first = copies.remote(own.at[1 - c], whole.at[chip, c], place.other_core())
-        self.mine = copies.inside(own.at[c], whole.at[chip, c])
+        rows = own.shape[1]
+        block = whole.at[pl.ds(pl.multiple_of((chip * CORES + c) * rows, rows), rows)]
+        self.first = copies.remote(own.at[1 - c], block, place.other_core())
+        self.mine = copies.inside(own.at[c], block)
         last = place.line - 1
         up = place.at(jnp.minimum(z + 1, last), y, c, place.x)
         down = place.at(jnp.maximum(z - 1, 0), y, c, place.x)
 
         def pair(zz):
-            return whole.at[jnp.clip(zz, 0, last) * LINE_Y + y]
+            first = (jnp.clip(zz, 0, last) * LINE_Y + y) * CORES * rows
+            return whole.at[pl.ds(pl.multiple_of(first, CORES * rows), CORES * rows)]
 
         self.ups = [copies.remote(pair(z - j), pair(z - j), up) for j in range(last)]
         self.downs = [copies.remote(pair(z + j), pair(z + j), down) for j in range(last)]
@@ -567,6 +575,200 @@
             copy.wait_send()
 
 
+def nn(left, right):
+    return lax.dot_general(left, right, (((1,), (0,)), ((), ())), preferred_element_type=jnp.float32)
+
+
+def tile(i, size):
+    return pl.ds(pl.multiple_of(i * size, size), size)
+
+
+def flat_rows(values):
+    return values.reshape(-1, values.shape[-1])
+
+
+GAIN_ONE, SHIFT_ONE, GAIN_TWO, SHIFT_TWO, OUT_BIAS, DOWN_BIAS, QKV_BIAS, UP_BIAS, SMALL_ROWS = (
+    0,
+    1,
+    2,
+    3,
+    4,
+    5,
+    6,
+    9,
+    16,
+)
+LANES = 128
+
+
+def lanes_of(shape):
+    return lax.broadcasted_iota(jnp.int32, shape, len(shape) - 1)
+
+
+def assemble_small(place, small, vec, qkv_rows, qkv_bias, up_bias):
+    chips, groups = small.shape[:2]
+    low = lanes_of((1, LANES)) < LANES // 2
+    for pair in range(chips * groups // 2):
+        chip, group = pair // (groups // 2), pair % (groups // 2) * 2
+        for row in range(4):
+            a = small[chip, group, row : row + 1, :]
+            b = small[chip, group + 1, row : row + 1, :]
+            vec[row : row + 1, pair * LANES : (pair + 1) * LANES] = jnp.where(low, a, b)
+        qkv_rows[3 * pair : 3 * pair + 1, :] = small[chip, group, QKV_BIAS : QKV_BIAS + 1, :]
+        a = small[chip, group, QKV_BIAS + 1 : QKV_BIAS + 2, :]
+        b = small[chip, group + 1, QKV_BIAS + 1 : QKV_BIAS + 2, :]
+        qkv_rows[3 * pair + 1 : 3 * pair + 2, :] = jnp.where(low, a, b)
+        qkv_rows[3 * pair + 2 : 3 * pair + 3, :] = small[chip, group + 1, QKV_BIAS + 2 : QKV_BIAS + 3, :]
+    third = qkv_rows.shape[0] // 3
+    per_head = HEAD // LANES
+    for k in range(3):
+        for u in range(per_head):
+            at = (k * per_head + u) * LANES
+            qkv_bias[0:1, at : at + LANES] = qkv_rows[pl.ds(k * third + place.chip * per_head + u, 1), :]
+    for group in range(groups):
+        for u in range(2):
+            at = (group * 2 + u) * LANES
+            row = UP_BIAS + u
+            up_bias[0:1, at : at + LANES] = small[pl.ds(place.chip, 1), group, row : row + 1, :].reshape(1, LANES)
+
+
+def norm_rows(start, count, hid, vec, norm_one, norm_two, stats):
+    step = 16
+
+    @pl.loop(0, count // step)
+    def _(i):
+        at = pl.ds(pl.multiple_of(start + i * step, step), step)
+        x = hid[at, :].astype(jnp.float32)
+        average = jnp.mean(x, axis=1, keepdims=True)
+        centered = x - average
+        scale = lax.rsqrt(jnp.mean(centered * centered, axis=1, keepdims=True) + LN_EPSILON)
+        stats[at, 0:1] = average
+        stats[at, 1:2] = scale
+        xhat = centered * scale
+        norm_one[at, :] = (xhat * vec[0:1, :] + vec[1:2, :]).astype(jnp.bfloat16)
+        norm_two[at, :] = (xhat * vec[2:3, :] + vec[3:4, :]).astype(jnp.bfloat16)
+
+
+def turned_half(values):
+    half_rot = ROT // 2
+    lane = lanes_of(values.shape)
+    width = values.shape[-1]
+    return jnp.where(
+        lane < half_rot,
+        pltpu.roll(values, width - half_rot, 1),
+        jnp.where(lane < ROT, pltpu.roll(values, half_rot, 1), 0.0),
+    )
+
+
+def project(norm_one, weight, bias, cosine, sine, query, key, value):
+    step = 256
+
+    @pl.loop(0, norm_one.shape[0] // step)
+    def _(i):
+        at = tile(i, step)
+        both = nn(norm_one[at, :], flat_rows(weight[...])) + bias[0:1, :]
+        cos, sin = cosine[at, :], sine[at, :]
+        for k, target in enumerate((query, key)):
+            first = both[:, k * HEAD : k * HEAD + LANES]
+            target[at, 0:LANES] = (first * cos + turned_half(first) * sin).astype(jnp.bfloat16)
+            target[at, LANES:HEAD] = both[:, k * HEAD + LANES : (k + 1) * HEAD].astype(jnp.bfloat16)
+        value[at, :] = both[:, 2 * HEAD :].astype(jnp.bfloat16)
+
+
+def attend(query, key, value, sine, key_pos, attended, attended_low, probs, probs_low):
+    step = 256
+
+    @pl.loop(0, query.shape[0] // step)
+    def _(i):
+        at = tile(i, step)
+        scores = contract_cols(query[at, :], key[...]) * HEAD**-0.5
+        allowed = key_pos[0:1, :] <= sine[at, ROT : ROT + 1]
+        scores = jnp.where(allowed, scores, VERY_LOW)
+        highest = jnp.max(scores, axis=1, keepdims=True)
+        weights = jnp.where(allowed, jnp.exp(scores - highest), 0.0)
+        weights = weights / jnp.sum(weights, axis=1, keepdims=True)
+        low = weights.astype(jnp.bfloat16)
+        probs[at, :] = weights
+        probs_low[at, :] = low
+        total = nn(low, value[...])
+        attended[at, :] = total
+        attended_low[at, :] = total.astype(jnp.bfloat16)
+
+
+def feed_inner(norm_two, weight, bias, activated, slope):
+    step = 128
+
+    @pl.loop(0, norm_two.shape[0] // step)
+    def _(i):
+        at = tile(i, step)
+        inner = nn(norm_two[at, :], flat_rows(weight[...])) + bias[0:1, :]
+        normal = 0.5 + 0.5 * lax.erf(inner * 0.5**0.5)
+        activated[at, :] = (inner * normal).astype(jnp.bfloat16)
+        density = (2.0 * jnp.pi) ** -0.5 * jnp.exp(-0.5 * inner * inner)
+        slope[at, :] = normal + inner * density
+
+
+def attended_grads(cot, weight, attended_low, attended_grad, weight_grad):
+    @pl.loop(0, cot.shape[0] // 256)
+    def _(i):
+        at = tile(i, 256)
+        attended_grad[at, :] = contract_cols(cot[at, :], flat_rows(weight[...])).astype(jnp.bfloat16)
+
+    @pl.loop(0, cot.shape[1] // 512)
+    def _(i):
+        at = tile(i, 512)
+        grad = contract_rows(attended_low[...], cot[:, at]).astype(jnp.bfloat16)
+        weight_grad[:, :, at] = grad.reshape(weight_grad.shape[0], weight_grad.shape[1], 512)
+
+
+def attention_grads(
+    query, key, value, cosine, sine, attended, attended_grad, probs, probs_low, score_grad, projected_grad
+):
+    step = 256
+    scaling = HEAD**-0.5
+
+    def put(at, k, grad):
+        first = grad[:, 0:LANES]
+        back = first * cosine[at, :] - turned_half(first) * sine[at, :]
+        projected_grad[at, k * HEAD : k * HEAD + LANES] = back.astype(jnp.bfloat16)
+        projected_grad[at, k * HEAD + LANES : (k + 1) * HEAD] = grad[:, LANES:].astype(jnp.bfloat16)
+
+    @pl.loop(0, query.shape[0] // step)
+    def _(i):
+        at = tile(i, step)
+        own = attended_grad[at, :]
+        row_delta = jnp.sum(own.astype(jnp.float32) * attended[at, :], axis=1, keepdims=True)
+        grad = (probs[at, :] * (contract_cols(own, value[...]) - row_delta)).astype(jnp.bfloat16)
+        score_grad[at, :] = grad
+        put(at, 0, nn(grad, key[...]) * scaling)
+
+    @pl.loop(0, query.shape[0] // step)
+    def _(i):
+        at = tile(i, step)
+        put(at, 1, contract_rows(score_grad[:, at], query[...]) * scaling)
+        projected_grad[at, 2 * HEAD :] = contract_rows(probs_low[:, at], attended_grad[...]).astype(jnp.bfloat16)
+
+
+def weight_grads(tokens, grads, result):
+    chips, groups, rows = result.shape[:3]
+    step = groups * rows
+
+    @pl.loop(0, chips)
+    def _(k):
+        grad = contract_rows(tokens[:, tile(k, step)], grads[...]).astype(jnp.bfloat16)
+        result[k] = grad.reshape(result.shape[1:])
+
+
+def column_sums(values, result):
+    step = 16
+
+    def add(i, total):
+        return total + values[tile(i, step), :].astype(jnp.float32)
+
+    total = lax.fori_loop(0, values.shape[0] // step, add, jnp.zeros((step, values.shape[1]), jnp.float32))
+    result[0:1, :] = jnp.sum(total, axis=0, keepdims=True)
+
+
 def gather_kernel(
     ctx_count,
     hid,
@@ -576,6 +778,9 @@
     down,
     out,
     small,
+    cosine_in,
+    sine_in,
+    key_pos_in,
     hid_all,
     cot_all,
     qkv_all,
@@ -583,6 +788,49 @@
     down_all,
     out_all,
     small_all,
+    attended_low_out,
+    projected_grad_out,
+    norm_two_out,
+    activated_out,
+    slope_out,
+    qkv_grad_out,
+    down_grad_out,
+    out_grad_out,
+    vec_out,
+    stats_out,
+    qkv_sum_out,
+    cot_sum_out,
+    hid_v,
+    cot_v,
+    qkv_v,
+    up_v,
+    out_v,
+    small_v,
+    cosine,
+    sine,
+    key_pos,
+    vec,
+    qkv_rows,
+    qkv_bias,
+    up_bias,
+    norm_one,
+    norm_two,
+    stats,
+    query,
+    key,
+    value,
+    attended,
+    attended_low,
+    probs,
+    probs_low,
+    activated,
+    slope,
+    attended_grad,
+    score_grad,
+    projected_grad,
+    out_grad,
+    qkv_sum,
+    cot_sum,
     send,
     recv,
     local,
@@ -618,7 +866,44 @@
     out_across = copies.remote(out, out_all.at[group], place.other_plane())
     out_pair = out_all.at[pl.ds(2 * place.c, 2)]
     out_swap = copies.remote(out_pair, out_pair, place.other_core())
-
+    loads = {
+        name: copies.inside(src, dst)
+        for name, src, dst in (
+            ("cosine", cosine_in, cosine),
+            ("sine", sine_in, sine),
+            ("key_pos", key_pos_in, key_pos),
+            ("small", small_all, small_v),
+            ("hid", hid_all, hid_v),
+            ("cot", cot_all, cot_v),
+            ("qkv", qkv_all, qkv_v),
+            ("up", up_all, up_v),
+            ("out", out_all, out_v),
+        )
+    }
+    stores = {
+        name: copies.inside(src, dst)
+        for name, src, dst in (
+            ("vec", vec, vec_out),
+            ("stats", stats, stats_out),
+            ("attended_low", attended_low, attended_low_out),
+            ("norm_two", norm_two, norm_two_out),
+            ("activated", activated, activated_out),
+            ("slope", slope, slope_out),
+            ("out_grad", out_grad, out_grad_out),
+            ("projected_grad", projected_grad, projected_grad_out),
+            ("qkv_grad", qkv_v, qkv_grad_out),
+            ("down_grad", up_v, down_grad_out),
+            ("qkv_sum", qkv_sum, qkv_sum_out),
+            ("cot_sum", cot_sum, cot_sum_out),
+        )
+    }
+
+    def fetch(name):
+        loads[name].start()
+        loads[name].wait()
+
+    for name in ("cosine", "sine", "key_pos"):
+        loads[name].start()
     greet(place)
     hid_g.start()
     cot_g.start()
@@ -636,52 +921,148 @@
     cot_g.spread()
     hid_g.step(2)
     down_g.scatter()
+    small_g.finish()
+    fetch("small")
+    assemble_small(place, small_v, vec, qkv_rows, qkv_bias, up_bias)
+    stores["vec"].start()
     qkv_g.share()
     cot_g.step(0)
+    hid_g.finish()
+    fetch("hid")
+    rows = hid_v.shape[0]
+    norm_rows(0, rows // 2, hid_v, vec, norm_one, norm_two, stats)
+    cot_g.step(1)
     up_g.cross()
-    cot_g.step(1)
+    norm_rows(rows // 2, rows // 2, hid_v, vec, norm_one, norm_two, stats)
+    stores["norm_two"].start()
+    stores["stats"].start()
     cot_g.step(2)
+    qkv_g.finish()
+    fetch("qkv")
+    for name in ("cosine", "sine", "key_pos"):
+        loads[name].wait()
+    project(norm_one, qkv_v, qkv_bias, cosine, sine, query, key, value)
     out_mine.wait()
     out_across.wait_recv()
     out_swap.start()
     down_g.cross()
     up_g.share()
+    attend(query, key, value, sine, key_pos, attended, attended_low, probs, probs_low)
+    stores["attended_low"].start()
+    up_g.finish()
+    fetch("up")
     down_g.share()
-    hid_g.finish()
+    feed_inner(norm_two, up_v, up_bias, activated, slope)
+    stores["activated"].start()
+    stores["slope"].start()
     cot_g.finish()
-    for gather in (small_g, qkv_g, up_g, down_g):
-        gather.finish()
+    loads["cot"].start()
     out_swap.wait_recv()
+    fetch("out")
+    loads["cot"].wait()
+    attended_grads(cot_v, out_v, attended_low, attended_grad, out_grad)
+    stores["out_grad"].start()
+    weight_grads(cot_v, activated, up_v)
+    stores["down_grad"].start()
+    column_sums(cot_v, cot_sum)
+    stores["cot_sum"].start()
+    attention_grads(
+        query, key, value, cosine, sine, attended, attended_grad, probs, probs_low, score_grad, projected_grad
+    )
+    stores["projected_grad"].start()
+    weight_grads(norm_one, projected_grad, qkv_v)
+    stores["qkv_grad"].start()
+    column_sums(projected_grad, qkv_sum)
+    stores["qkv_sum"].start()
+    down_g.finish()
+    for store in stores.values():
+        store.wait()
     for gather in (hid_g, cot_g, small_g, qkv_g, up_g, down_g):
         gather.drain()
     out_across.wait_send()
     out_swap.wait_send()
 
 
-def gather_all(ctx_count, hid, cot, qkv, up, down, out, small):
+def gather_all(ctx_count, hid, cot, qkv, up, down, out, small, cosine, sine, key_pos):
+    f32, b16 = jnp.float32, jnp.bfloat16
     chips = ctx_count // CORES
     rows = qkv.shape[0]
     groups = CORES * 2
-    shapes = [
-        ((chips, CORES) + hid.shape[1:], hid.dtype),
-        ((chips, CORES) + cot.shape[1:], cot.dtype),
-        ((chips, groups, rows, qkv.shape[1] // chips), qkv.dtype),
-        ((chips, groups, rows, up.shape[1] // chips), up.dtype),
-        ((chips, groups, rows, down.shape[1] // chips), down.dtype),
-        ((groups, rows, out.shape[1]), out.dtype),
-        ((chips, groups) + small.shape, small.dtype),
+    tokens = ctx_count * hid.shape[1]
+    width = out.shape[1]
+    head3, part = qkv.shape[1] // chips, up.shape[1] // chips
+    head = head3 // 3
+    qkv_s = ((chips, groups, rows, head3), b16)
+    part_s = ((chips, groups, rows, part), b16)
+    out_s = ((groups, rows, width), b16)
+    small_s = ((chips, groups) + small.shape, f32)
+    wide_s, narrow_s = ((tokens, width), b16), ((tokens, head), b16)
+    results = [
+        wide_s,
+        wide_s,
+        qkv_s,
+        part_s,
+        part_s,
+        out_s,
+        small_s,
+        narrow_s,
+        ((tokens, head3), b16),
+        wide_s,
+        ((tokens, part), b16),
+        ((tokens, part), f32),
+        qkv_s,
+        part_s,
+        out_s,
+        ((8, width), f32),
+        ((tokens, LANES), f32),
+        ((8, head3), f32),
+        ((8, width), f32),
     ]
-    operands = (hid, cot, qkv, up, down, out, small)
+    scratch = [
+        wide_s,
+        wide_s,
+        qkv_s,
+        part_s,
+        out_s,
+        small_s,
+        ((tokens, LANES), f32),
+        ((tokens, LANES), f32),
+        ((8, tokens), f32),
+        ((8, width), f32),
+        ((3 * width // LANES, LANES), f32),
+        ((8, head3), f32),
+        ((8, part), f32),
+        wide_s,
+        wide_s,
+        ((tokens, LANES), f32),
+        narrow_s,
+        narrow_s,
+        narrow_s,
+        ((tokens, head), f32),
+        narrow_s,
+        ((tokens, tokens), f32),
+        ((tokens, tokens), b16),
+        ((tokens, part), b16),
+        ((tokens, part), f32),
+        narrow_s,
+        ((tokens, tokens), b16),
+        ((tokens, head3), b16),
+        out_s,
+        ((8, head3), f32),
+        ((8, width), f32),
+    ]
+    operands = (hid, cot, qkv, up, down, out, small, cosine, sine, key_pos)
     anywhere = pl.BlockSpec(memory_space=pl.ANY)
     return pl.pallas_call(
         lambda *refs: gather_kernel(ctx_count, *refs),
-        out_shape=[jax.ShapeDtypeStruct(*shape) for shape in shapes],
+        out_shape=[jax.ShapeDtypeStruct(*shape) for shape in results],
         in_specs=[anywhere] * len(operands),
-        out_specs=[anywhere] * len(shapes),
-        scratch_shapes=[
+        out_specs=[anywhere] * len(results),
+        scratch_shapes=[pltpu.VMEM(*shape) for shape in scratch]
+        + [
             pltpu.SemaphoreType.DMA((88,)),
             pltpu.SemaphoreType.DMA((88,)),
-            pltpu.SemaphoreType.DMA((16,)),
+            pltpu.SemaphoreType.DMA((40,)),
         ],
         compiler_params=pltpu.CompilerParams(
             collective_id=0, has_side_effects=True, vmem_limit_bytes=VMEM_BYTES
@@ -690,8 +1071,21 @@
     )(*operands)
 
 
-def add_into(total, other, steps):
-    @pl.loop(0, steps)
+def add_rows(total, other, count):
+    step = 16
+    per = total.shape[-2] // step
+
+    @pl.loop(0, count * per)
+    def _(i):
+        k, at = i // per, tile(i % per, step)
+        both = total[k, at, :].astype(jnp.float32) + other[k, at, :].astype(jnp.float32)
+        total[k, at, :] = both.astype(total.dtype)
+
+
+def add_tiles(total, other, pieces):
+    rows = total.shape[-2]
+
+    @pl.loop(0, pieces)
     def _(k):
         both = total[k].astype(jnp.float32) + other[k].astype(jnp.float32)
         total[k] = both.astype(total.dtype)
@@ -702,8 +1096,11 @@
         self.place = place
         c, x, chip = place.c, place.x, place.chip
         self.kept, self.from_core, self.from_plane = kept, from_core, from_plane
-        self.load = copies.inside(partial.at[:, pl.ds(2 * c, 2)], kept)
-        self.swap = copies.remote(partial.at[:, pl.ds(2 * (1 - c), 2)], from_core, place.other_core())
+        given = partial
+        if partial.shape != kept.shape:
+            self.load = copies.inside(partial.at[:, pl.ds(2 * c, 2)], kept)
+            given = partial.at[:, pl.ds(2 * (1 - c), 2)]
+        self.swap = copies.remote(given, from_core, place.other_core())
         self.across = copies.remote(kept.at[:, 1 - x], from_plane, place.other_plane())
         self.scattered = []
         for dz, dy in place.plane_offsets():
@@ -717,21 +1114,28 @@
         self.load.start()
         self.swap.start()
 
-    def cross(self):
-        self.load.wait()
+    def cross(self, loaded=True):
+        if loaded:
+            self.load.wait()
         self.swap.wait_recv()
-        add_into(self.kept, self.from_core, self.kept.shape[0])
+        x = self.place.x
+        self.add(1 - x, self.from_core.at[:, 1 - x])
         self.across.start()
+        self.add(x, self.from_core.at[:, x])
+
+    def add(self, x, other):
+        step = 16
+        per = self.kept.shape[2] // step
+
+        @pl.loop(0, self.kept.shape[0] * per)
+        def _(i):
+            k, at = i // per, tile(i % per, step)
+            both = self.kept[k, x, at, :].astype(jnp.float32) + other[k, at, :].astype(jnp.float32)
+            self.kept[k, x, at, :] = both.astype(self.kept.dtype)
 
     def scatter(self):
         self.across.wait_recv()
-        x = self.place.x
-
-        @pl.loop(0, self.kept.shape[0])
-        def _(k):
-            both = self.kept[k, x].astype(jnp.float32) + self.from_plane[k].astype(jnp.float32)
-            self.kept[k, x] = both.astype(self.kept.dtype)
-
+        self.add(self.place.x, self.from_plane)
         for copy in self.scattered + [self.own]:
             copy.start()
 
@@ -745,152 +1149,489 @@
             copy.wait_send()
 
 
+def weight_grads_by_core(place, tokens, grads, kept, given):
+    chips, half, rows = kept.shape[:3]
+    step = 2 * half * rows
+
+    @pl.loop(0, chips)
+    def _(k):
+        grad = contract_rows(tokens[:, tile(k, step)], grads[...]).astype(jnp.bfloat16)
+        grad = grad.reshape((2,) + kept.shape[1:])
+        kept[k] = jnp.where(place.c == 0, grad[0], grad[1])
+        given[k] = jnp.where(place.c == 0, grad[1], grad[0])
+
+
 class TokenScatter:
-    def __init__(self, place, copies, partial, kept, from_y, from_z, total, result):
+    def __init__(self, place, copies, part, from_y, slots, total, result):
         self.place = place
         z, y, c, x = place.z, place.y, place.c, place.x
-        self.kept, self.from_y, self.from_z, self.total = kept, from_y, from_z, total
-        self.load = copies.inside(partial.at[:, y], kept)
-        self.over = copies.remote(partial.at[:, 1 - y], from_y, place.other_y())
-        self.along = []
-        for dz in range(1, place.line):
-            to = (z + dz) % place.line
-            self.along.append(copies.remote(kept.at[to], from_z.at[dz - 1], place.at(to, y, c, x)))
+        self.part, self.from_y, self.slots, self.total = part, from_y, slots, total
+        self.line = place.line
+        last = self.line - 1
+        self.last = last
+        self.copies = copies
+        self.over_base = copies.reserve(self.line)
+        up = place.at(jnp.minimum(z + 1, last), y, c, x)
+        down = place.at(jnp.maximum(z - 1, 0), y, c, x)
+        self.ups = {d: copies.remote(part.at[d, y], slots.at[d], up) for d in range(1, self.line)}
+        self.downs = {}
+        for d in range(last):
+            slot = jnp.where(z - 1 == d, last + 1, d)
+            self.downs[d] = copies.remote(part.at[d, y], slots.at[slot], down)
         self.swap = copies.remote(total.at[1 - c], result.at[c], place.other_core())
         self.own = copies.inside(total.at[c], result.at[c])
 
-    def start(self):
-        self.load.start()
-        self.over.start()
-
-    def along_z(self):
-        self.load.wait()
-        self.over.wait_recv()
-        add_into(self.kept, self.from_y, self.kept.shape[0])
-        for copy in self.along:
-            copy.start()
+    def over(self, k):
+        y = self.place.y
+        return self.copies.remote_at(
+            self.over_base + k, self.part.at[k, 1 - y], self.from_y.at[k], self.place.other_y()
+        )
+
+    def combine(self, k):
+        self.over(k).wait_recv()
+        add_rows(self.part.at[k, self.place.y], self.from_y.at[k], CORES)
+
+    def step(self, j):
+        z, y, last = self.place.z, self.place.y, self.last
+        above, below = last - j, j
+
+        @pl.when(z < above)
+        def _():
+            self.combine(above)
+
+            @pl.when(z > 0)
+            def _():
+                self.ups[above].wait_recv()
+                add_rows(self.part.at[above, y], self.slots.at[above], CORES)
+
+            self.ups[above].start()
+
+        @pl.when(z > below)
+        def _():
+            self.combine(below)
+
+            @pl.when(z < last)
+            def _():
+                self.downs[below].wait_recv()
+                add_rows(self.part.at[below, y], self.slots.at[below], CORES)
+
+            self.downs[below].start()
 
     def reduce(self):
-        for copy in self.along:
-            copy.wait_recv()
-        z = self.place.z
-
-        @pl.loop(0, CORES)
-        def _(k):
-            total = self.kept[z, k].astype(jnp.float32)
-            for dz in range(self.place.line - 1):
-                total = total + self.from_z[dz, k].astype(jnp.float32)
-            self.total[k] = total
-
+        z, y, last = self.place.z, self.place.y, self.last
+        self.combine(z)
+        for d in range(1, self.line):
+            pl.when(z == d)(lambda: self.ups[d].wait_recv())
+        for d in range(last):
+            pl.when(z == d)(lambda: self.downs[d].wait_recv())
+        step = 16
+        per = self.total.shape[1] // step
+
+        @pl.loop(0, CORES * per)
+        def _(i):
+            k, at = i // per, tile(i % per, step)
+            self.total[k, at, :] = self.part[z, y, k, at, :].astype(jnp.float32)
+
+        def add(slot):
+            @pl.loop(0, CORES * per)
+            def _(i):
+                k, at = i // per, tile(i % per, step)
+                self.total[k, at, :] += self.slots[slot, k, at, :].astype(jnp.float32)
+
+        pl.when(z > 0)(lambda: add(z))
+        pl.when(z < last)(lambda: add(last + 1))
         self.swap.start()
         self.own.start()
 
     def finish(self):
-        self.own.wait()
         self.swap.wait_recv()
 
     def drain(self):
-        self.over.wait_send()
-        for copy in self.along:
-            copy.wait_send()
-        self.swap.wait_send()
-
-
-def scatter_kernel(ctx_count, count_grads, *refs):
+        z, last = self.place.z, self.last
+        for k in range(self.line):
+            self.over(k).wait_send()
+        for d, copy in self.ups.items():
+            pl.when(z < d)(lambda: copy.wait_send())
+        for d, copy in self.downs.items():
+            pl.when(z > d)(lambda: copy.wait_send())
+
+
+def scatter_order(i, last):
+    odd = i % 2
+    return (1 - odd) * (last - i // 2) + odd * (i // 2)
+
+
+def output_parts(scatter, attended_low, activated, out_weight, down_weight):
+    @pl.loop(0, scatter.line)
+    def _(i):
+        k = scatter_order(i, scatter.last)
+        part = scatter.part
+        at = tile(k, part.shape[1] * part.shape[2] * part.shape[3])
+        rows = nn(attended_low[at, :], flat_rows(out_weight[...]))
+        rows = rows + contract_cols(activated[at, :], flat_rows(down_weight[...]))
+        part[k] = rows.astype(part.dtype).reshape(part.shape[1:])
+        scatter.over(k).start()
+
+
+def inner_grads(cot, down_weight, slope, slope_loads, inner_grad):
+    step = slope.shape[1]
+    for i, load in enumerate(slope_loads):
+        load.wait()
+        at = slice(i * step, (i + 1) * step)
+        grad = nn(cot[at, :], flat_rows(down_weight[...])) * slope[i % 2]
+        inner_grad[at, :] = grad.astype(jnp.bfloat16)
+        if i + 2 < len(slope_loads):
+            slope_loads[i + 2].start()
+
+
+def hidden_parts(scatter, inner_grad, up_weight, projected_grad, qkv_weight, hid, stats, vec, sums):
+    sums[...] = jnp.zeros_like(sums)
+
+    def by_eight(values):
+        return jnp.sum(values.reshape(-1, 8, values.shape[1]), axis=0)
+
+    @pl.loop(0, scatter.line)
+    def _(i):
+        k = scatter_order(i, scatter.last)
+        part = scatter.part
+        size = part.shape[2] * part.shape[3]
+
+        @pl.loop(0, LINE_Y)
+        def _(y):
+            at = tile(k * LINE_Y + y, size)
+            one = contract_cols(projected_grad[at, :], flat_rows(qkv_weight[...]))
+            two = contract_cols(inner_grad[at, :], flat_rows(up_weight[...]))
+            xhat = (hid[at, :].astype(jnp.float32) - stats[at, 0:1]) * stats[at, 1:2]
+            sums[0] += by_eight(one * xhat)
+            sums[1] += by_eight(one)
+            sums[2] += by_eight(two * xhat)
+            sums[3] += by_eight(two)
+            rows = one * vec[0:1, :] + two * vec[2:3, :]
+            part[k, y] = rows.astype(part.dtype).reshape(part.shape[2:])
+
+        scatter.over(k).start()
+
+
+COT_SUM, UP_SUM, QKV_SUM = 4, 5, 7
+
+
+def pack_small(place, sums, cot_sum, up_sum, qkv_sum, qkv_rows, tiles):
+    chips, groups = tiles.shape[:2]
+    tiles[...] = jnp.zeros_like(tiles)
+    qkv_rows[...] = jnp.zeros_like(qkv_rows)
+    third = qkv_rows.shape[0] // 3
+    per_head = HEAD // LANES
+    for k in range(3):
+        for u in range(per_head):
+            at = (k * per_head + u) * LANES
+            qkv_rows[pl.ds(k * third + place.chip * per_head + u, 1), :] = qkv_sum[0:1, at : at + LANES]
+    first = jnp.where(place.chip == 0, 1.0, 0.0)
+    norm_sums = [jnp.sum(sums[row], axis=0, keepdims=True) for row in range(4)]
+    norm_sums.append(cot_sum[0:1, :] * first)
+    for pair in range(chips * groups // 2):
+        chip, group = pair // (groups // 2), pair % (groups // 2) * 2
+        at = slice(pair * LANES, (pair + 1) * LANES)
+        for g in (group, group + 1):
+            for row in range(5):
+                tiles[chip, g, row : row + 1, :] = norm_sums[row][:, at]
+            tiles[chip, g, QKV_SUM : QKV_SUM + 3, :] = qkv_rows[3 * pair : 3 * pair + 3, :]
+    for group in range(groups):
+        for u in range(2):
+            at = (group * 2 + u) * LANES
+            row = UP_SUM + u
+            values = up_sum[0:1, at : at + LANES].reshape(1, 1, LANES)
+            tiles[pl.ds(place.chip, 1), group, row : row + 1, :] = values
+
+
+def scatter_kernel(
+    ctx_count,
+    hid_in,
+    cot_in,
+    qkv_in,
+    up_in,
+    down_in,
+    out_in,
+    attended_low_in,
+    projected_grad_in,
+    norm_two_in,
+    activated_in,
+    slope_in,
+    stats_in,
+    vec_in,
+    qkv_sum_in,
+    cot_sum_in,
+    qkv_grad,
+    down_grad,
+    out_grad,
+    small_result,
+    qkv_result,
+    up_result,
+    down_result,
+    out_grad_result,
+    out_result,
+    hid_result,
+    wide,
+    weight,
+    slope,
+    act,
+    attended_low,
+    out_weight,
+    qkv_weight,
+    projected_grad,
+    stats,
+    vec,
+    qkv_sum,
+    cot_sum,
+    up_sum,
+    sums,
+    qkv_rows,
+    tiles,
+    small_kept,
+    small_core,
+    small_plane,
+    qkv_kept,
+    qkv_core,
+    qkv_plane,
+    up_kept,
+    up_core,
+    up_plane,
+    down_kept,
+    down_core,
+    down_plane,
+    out_kept,
+    out_core,
+    out_plane,
+    out_part,
+    out_from_y,
+    out_slots,
+    hid_part,
+    hid_from_y,
+    hid_slots,
+    total,
+    send,
+    recv,
+    local,
+):
     place = Place(ctx_count)
-    take = iter(refs)
-    grads = [next(take) for _ in range(count_grads)]
-    grad_out, out_part, hid_part = next(take), next(take), next(take)
-    grad_results = [next(take) for _ in range(count_grads)]
-    grad_out_result, out_result, hid_result = next(take), next(take), next(take)
-    grad_scratch = [[next(take) for _ in range(3)] for _ in range(count_grads)]
-    grad_out_scratch = [next(take) for _ in range(3)]
-    token_scratch = [[next(take) for _ in range(4)] for _ in range(2)]
-    copies = Copies(next(take), next(take), next(take))
-    scatters = [
-        GradScatter(place, copies, grads[i], *grad_scratch[i], grad_results[i]) for i in range(count_grads)
+    copies = Copies(send, recv, local)
+    c, x = place.c, place.x
+    qkv_s = GradScatter(place, copies, qkv_grad, qkv_kept, qkv_core, qkv_plane, qkv_result)
+    down_s = GradScatter(place, copies, down_grad, down_kept, down_core, down_plane, down_result)
+    up_s = GradScatter(place, copies, down_core, up_kept, up_core, up_plane, up_result)
+    small_s = GradScatter(place, copies, tiles, small_kept, small_core, small_plane, small_result)
+    outs_s = TokenScatter(place, copies, out_part, out_from_y, out_slots, total, out_result)
+    hid_s = TokenScatter(place, copies, hid_part, hid_from_y, hid_slots, total, hid_result)
+    out_load = copies.inside(out_grad.at[pl.ds(2 * c, 2)], out_kept)
+    out_swap = copies.remote(out_grad.at[pl.ds(2 * (1 - c), 2)], out_core, place.other_core())
+    out_across = copies.remote(out_kept.at[1 - x], out_plane, place.other_plane())
+    out_own = copies.inside(out_kept.at[x], out_grad_result)
+    loads = {
+        name: copies.inside(src, dst)
+        for name, src, dst in (
+            ("activated", activated_in, act),
+            ("attended_low", attended_low_in, attended_low),
+            ("out", out_in, out_weight),
+            ("down", down_in, weight),
+            ("cot", cot_in, wide),
+            ("norm_two", norm_two_in, wide),
+            ("qkv", qkv_in, qkv_weight),
+            ("projected_grad", projected_grad_in, projected_grad),
+            ("stats", stats_in, stats),
+            ("vec", vec_in, vec),
+            ("qkv_sum", qkv_sum_in, qkv_sum),
+            ("cot_sum", cot_sum_in, cot_sum),
+            ("up", up_in, weight),
+            ("hid", hid_in, wide),
+        )
+    }
+    early = ("activated", "attended_low", "out", "down", "cot", "qkv", "projected_grad")
+    early += ("stats", "vec", "qkv_sum", "cot_sum")
+
+    def out_cross():
+        out_load.wait()
+        out_swap.wait_recv()
+        add_rows(out_kept, out_core, 2)
+        out_across.start()
+
+    def out_finish():
+        out_across.wait_recv()
+        step = 16
+
+        @pl.loop(0, out_plane.shape[0] // step)
+        def _(i):
+            at = tile(i, step)
+            both = out_kept[x, at, :].astype(jnp.float32) + out_plane[at, :].astype(jnp.float32)
+            out_kept[x, at, :] = both.astype(out_kept.dtype)
+
+        out_own.start()
+
+    step = slope.shape[1]
+    slope_loads = [
+        copies.inside(slope_in.at[pl.ds(i * step, step)], slope.at[i % 2]) for i in range(slope_in.shape[0] // step)
     ]
-    outs_s = TokenScatter(place, copies, out_part, *token_scratch[0], out_result)
-    hid_s = TokenScatter(place, copies, hid_part, *token_scratch[1], hid_result)
-    c, x = place.c, place.x
-    kept, from_core, from_plane = grad_out_scratch
-    load = copies.inside(grad_out.at[pl.ds(2 * c, 2)], kept)
-    swap = copies.remote(grad_out.at[pl.ds(2 * (1 - c), 2)], from_core, place.other_core())
-    across = copies.remote(kept.at[1 - x], from_plane, place.other_plane())
-    own = copies.inside(kept.at[x], grad_out_result)
-
+    for name in early:
+        loads[name].start()
+    slope_loads[0].start()
+    slope_loads[1].start()
     greet(place)
-    for scatter in scatters:
-        scatter.start()
-    load.start()
-    swap.start()
-    outs_s.start()
-    for scatter in scatters:
-        scatter.cross()
-    load.wait()
-    swap.wait_recv()
-    add_into(kept, from_core, 2)
-    across.start()
-    hid_s.start()
-    scatters[0].scatter()
-    outs_s.along_z()
-    for scatter in scatters[1:]:
-        scatter.scatter()
-    across.wait_recv()
-    kept[x] = (kept[x].astype(jnp.float32) + from_plane[...].astype(jnp.float32)).astype(kept.dtype)
-    own.start()
-    hid_s.along_z()
+    down_s.start()
+    qkv_s.start()
+    out_load.start()
+    out_swap.start()
+    for name in ("activated", "attended_low", "out", "down"):
+        loads[name].wait()
+    output_parts(outs_s, attended_low, act, out_weight, weight)
+    down_s.cross()
+    qkv_s.cross()
+    out_cross()
+    loads["cot"].wait()
+    inner_grads(wide, weight, slope, slope_loads, act)
+    loads["up"].start()
+    loads["norm_two"].start()
+    outs_s.step(0)
+    loads["norm_two"].wait()
+    weight_grads_by_core(place, wide, act, up_kept, down_core)
+    up_s.swap.start()
+    loads["hid"].start()
+    outs_s.step(1)
+    column_sums(act, up_sum)
+    down_s.scatter()
+    for name in ("qkv", "projected_grad", "stats", "vec", "up", "hid"):
+        loads[name].wait()
+    hidden_parts(hid_s, act, weight, projected_grad, qkv_weight, wide, stats, vec, sums)
+    up_s.cross(loaded=False)
+    outs_s.step(2)
+    qkv_s.scatter()
+    for name in ("qkv_sum", "cot_sum"):
+        loads[name].wait()
+    pack_small(place, sums, cot_sum, up_sum, qkv_sum, qkv_rows, tiles)
+    small_s.start()
     outs_s.reduce()
+    small_s.cross()
+    out_finish()
+    up_s.scatter()
+    small_s.scatter()
+    hid_s.step(0)
+    hid_s.step(1)
+    hid_s.step(2)
+    outs_s.own.wait()
+    outs_s.swap.wait_send()
     hid_s.reduce()
-    for scatter in scatters + [outs_s, hid_s]:
+    grads = (qkv_s, down_s, up_s, small_s)
+    for scatter in grads + (outs_s, hid_s):
         scatter.finish()
-    own.wait()
-    for scatter in scatters + [outs_s, hid_s]:
+    out_own.wait()
+    hid_s.own.wait()
+    hid_s.swap.wait_send()
+    for scatter in grads + (outs_s, hid_s):
         scatter.drain()
-    swap.wait_send()
-    across.wait_send()
-
-
-def scatter_all(ctx_count, grads, grad_out, out_part, hid_part):
-    chips = ctx_count // CORES
+    out_swap.wait_send()
+    out_across.wait_send()
+
+
+def scatter_all(ctx_count, local_rows, operands):
+    f32, b16 = jnp.float32, jnp.bfloat16
+    hid, _, w_qkv, w_up, _, w_out = operands[:6]
+    chips, groups, rows, head3 = w_qkv.shape
+    part = w_up.shape[3]
+    tokens, width = hid.shape
     line = chips // LINE_Y
-    count = len(grads)
-    grad_out_shape = grad_out.shape[1:]
-    token = (CORES,) + out_part.shape[3:]
-    out_shape = [jax.ShapeDtypeStruct((chips,) + g.shape[2:], g.dtype) for g in grads]
-    out_shape += [jax.ShapeDtypeStruct(grad_out_shape, grad_out.dtype)]
-    out_shape += [jax.ShapeDtypeStruct(token, jnp.float32)] * 2
-    scratch = []
-    for g in grads:
-        scratch.append(pltpu.VMEM((chips, 2) + g.shape[2:], g.dtype))
-        scratch.append(pltpu.VMEM((chips, 2) + g.shape[2:], g.dtype))
-        scratch.append(pltpu.VMEM((chips,) + g.shape[2:], g.dtype))
-    scratch.append(pltpu.VMEM((2,) + grad_out_shape, grad_out.dtype))
-    scratch.append(pltpu.VMEM((2,) + grad_out_shape, grad_out.dtype))
-    scratch.append(pltpu.VMEM(grad_out_shape, grad_out.dtype))
-    for part in (out_part, hid_part):
-        scratch.append(pltpu.VMEM((line,) + token, part.dtype))
-        scratch.append(pltpu.VMEM((line,) + token, part.dtype))
-        scratch.append(pltpu.VMEM((line - 1,) + token, part.dtype))
-        scratch.append(pltpu.VMEM(token, jnp.float32))
-    operands = list(grads) + [grad_out, out_part, hid_part]
+    small = (SMALL_ROWS, LANES)
+    token = (CORES, local_rows, width)
+    results = [
+        ((chips,) + small, f32),
+        ((chips, rows, head3), b16),
+        ((chips, rows, part), b16),
+        ((chips, rows, part), b16),
+        ((rows, width), b16),
+        (token, f32),
+        (token, f32),
+    ]
+    scratch = [
+        ((tokens, width), b16),
+        (w_up.shape, b16),
+        ((2, 256, part), f32),
+        ((tokens, part), b16),
+        ((tokens, head3 // 3), b16),
+        (w_out.shape, b16),
+        (w_qkv.shape, b16),
+        ((tokens, head3), b16),
+        ((tokens, LANES), f32),
+        ((8, width), f32),
+        ((8, head3), f32),
+        ((8, width), f32),
+        ((8, part), f32),
+        ((4, 8, width), f32),
+        ((3 * width // LANES, LANES), f32),
+        ((chips, groups) + small, f32),
+    ]
+    for shape, dtype in ((small, f32), ((rows, head3), b16), ((rows, part), b16), ((rows, part), b16)):
+        scratch += [((chips, 2) + shape, dtype)] * 2 + [((chips,) + shape, dtype)]
+    scratch += [((2, rows, width), b16)] * 2 + [((rows, width), b16)]
+    for _ in range(2):
+        scratch += [
+            ((line, LINE_Y) + token, b16),
+            ((line,) + token, b16),
+            ((line + 1,) + token, b16),
+        ]
+    scratch += [(token, f32)]
     anywhere = pl.BlockSpec(memory_space=pl.ANY)
     return pl.pallas_call(
-        lambda *refs: scatter_kernel(ctx_count, count, *refs),
-        out_shape=out_shape,
+        lambda *refs: scatter_kernel(ctx_count, *refs),
+        out_shape=[jax.ShapeDtypeStruct(*shape) for shape in results],
         in_specs=[anywhere] * len(operands),
-        out_specs=[anywhere] * len(out_shape),
-        scratch_shapes=scratch
+        out_specs=[anywhere] * len(results),
+        scratch_shapes=[pltpu.VMEM(*shape) for shape in scratch]
         + [
-            pltpu.SemaphoreType.DMA((64,)),
-            pltpu.SemaphoreType.DMA((64,)),
-            pltpu.SemaphoreType.DMA((16,)),
+            pltpu.SemaphoreType.DMA((80,)),
+            pltpu.SemaphoreType.DMA((80,)),
+            pltpu.SemaphoreType.DMA((40,)),
         ],
         compiler_params=pltpu.CompilerParams(
             collective_id=1, has_side_effects=True, vmem_limit_bytes=VMEM_BYTES
         ),
         name="scatter_all",
     )(*operands)
+
+
+def small_tile(ln1_gain, ln1_bias, ln2_gain, ln2_bias, out_bias, down_bias, qkv_bias, up_bias):
+    half = LANES // 2
+
+    def put(values, row, lane):
+        values = values.astype(jnp.float32).reshape(1, -1)
+        return lax.pad(
+            values,
+            jnp.float32(0),
+            ((row, SMALL_ROWS - 1 - row, 0), (lane, LANES - lane - values.shape[1], 0)),
+        )
+
+    total = jnp.zeros((SMALL_ROWS, LANES), jnp.float32)
+    for row, values in (
+        (GAIN_ONE, ln1_gain),
+        (SHIFT_ONE, ln1_bias),
+        (GAIN_TWO, ln2_gain),
+        (SHIFT_TWO, ln2_bias),
+        (OUT_BIAS, out_bias),
+        (DOWN_BIAS, down_bias),
+    ):
+        total = total + put(values, row, 0) + put(values, row, half)
+    total = total + put(qkv_bias[:LANES], QKV_BIAS, 0)
+    total = total + put(qkv_bias[LANES:], QKV_BIAS + 1, 0) + put(qkv_bias[:half], QKV_BIAS + 1, half)
+    total = total + put(qkv_bias[half:], QKV_BIAS + 2, 0)
+    return total + put(up_bias[:LANES], UP_BIAS, 0) + put(up_bias[LANES:], UP_BIAS + 1, 0)
+
+
+def rotation_tables(positions):
+    half_rot = ROT // 2
+    where = positions.astype(jnp.float32)[:, None]
+    frequency = 1.0 / 10000.0 ** (jnp.arange(half_rot).astype(jnp.float32) * 2.0 / ROT)
+    angles = where * frequency[None, :]
+    cos, sin = jnp.cos(angles), jnp.sin(angles)
+    rest = jnp.ones((positions.shape[0], LANES - ROT), jnp.float32)
+    return (
+        jnp.concatenate([cos, cos, rest], axis=1),
+        jnp.concatenate([-sin, sin, rest * where], axis=1),
+    )
 
 
 def split_body(
@@ -914,18 +1655,34 @@
     ctx_count = lax.axis_size("ctx")
     chips = ctx_count // CORES
     total_rows = local_rows * ctx_count
-    scaling = HEAD ** (-0.5)
     f32, b16 = jnp.float32, jnp.bfloat16
     head_id = lax.axis_index("ctx") // CORES
-
     owned = width // (ctx_count * 2)
-    vectors = (ln1_gain, ln1_bias, ln2_gain, ln2_bias, out_bias, down_bias, qkv_bias, up_bias)
-    flat = jnp.concatenate([v.astype(f32) for v in vectors])
-    used = flat.shape[0]
-    small_rows = 8 * (-(-used // 1024))
-    small = jnp.pad(flat, (0, small_rows * 128 - used)).reshape(small_rows, 128)
-
-    hid_all, cot_all, w_qkv, w_up, w_down, w_out, small_all = gather_all(
+    positions = row_positions(pairing, jnp.int32(0), total_rows, local_rows // 2, ctx_count)
+    cosine, sine = rotation_tables(positions)
+    key_pos = jnp.broadcast_to(positions.astype(f32)[None, :], (8, total_rows))
+
+    (
+        hid_all,
+        cot_all,
+        w_qkv,
+        w_up,
+        w_down,
+        w_out,
+        small_all,
+        attended_low,
+        projected_grad,
+        norm_two,
+        activated,
+        slope,
+        grad_qkv,
+        grad_down,
+        grad_out,
+        vec,
+        stats,
+        qkv_sum,
+        cot_sum,
+    ) = gather_all(
         ctx_count,
         jnp.swapaxes(hidden, 0, 1),
         jnp.swapaxes(cotangent, 0, 1),
@@ -933,118 +1690,40 @@
         up_weight,
         down_weight,
         out_weight,
-        small,
-    )
-    w_qkv = w_qkv.reshape(width, -1)
-    w_up = w_up.reshape(width, -1)
-    w_down = w_down.reshape(width, -1)
-    w_out = w_out.reshape(-1, width)
-    part = w_up.shape[1]
-    smalls = small_all.reshape(ctx_count * 2, -1)
-    full = []
-    at = 0
-    for v in vectors:
-        full.append(smalls[:, at : at + v.shape[0]].reshape(-1))
-        at += v.shape[0]
-    gain_one, shift_one, gain_two, shift_two, b_out, b_down, b_qkv, b_up = full
-    b_qkv = lax.dynamic_slice_in_dim(b_qkv.reshape(3, -1), head_id * HEAD, HEAD, axis=1).reshape(-1)
-    b_up = lax.dynamic_slice_in_dim(b_up, head_id * part, part)
-
-    x = hid_all.reshape(total_rows, width).astype(f32)
-    cot = cot_all.reshape(total_rows, width)
-    average = jnp.mean(x, axis=-1, keepdims=True)
-    spread = jnp.mean((x - average) ** 2, axis=-1, keepdims=True)
-    xhat = (x - average) * lax.rsqrt(spread + LN_EPSILON)
-    norm_one = (xhat * gain_one + shift_one).astype(b16)
-    norm_two = (xhat * gain_two + shift_two).astype(b16)
-    positions = row_positions(pairing, jnp.int32(0), total_rows, local_rows // 2, ctx_count)
-
-    projected = jnp.dot(norm_one, w_qkv, preferred_element_type=f32) + b_qkv
-    (query_f, key_f), rotation_pull = jax.vjp(
-        lambda q, k: (rotate(q, positions), rotate(k, positions)),
-        projected[:, :HEAD],
-        projected[:, HEAD : 2 * HEAD],
-    )
-    query, key = query_f.astype(b16), key_f.astype(b16)
-    value = projected[:, 2 * HEAD :].astype(b16)
-    scores = contract_cols(query, key) * scaling
-    allowed = positions[None, :] <= positions[:, None]
-    highest = jnp.max(jnp.where(allowed, scores, VERY_LOW), axis=-1, keepdims=True)
-    weights = jnp.where(allowed, jnp.exp(scores - highest), 0.0)
-    probs = weights / jnp.sum(weights, axis=-1, keepdims=True)
-    probs_low = probs.astype(b16)
-    attended = jnp.dot(probs_low, value, preferred_element_type=f32)
-    attended_low = attended.astype(b16)
-
-    inner = jnp.dot(norm_two, w_up, preferred_element_type=f32) + b_up
-    activated_f, gelu_pull = jax.vjp(gelu_exact, inner)
-    activated = activated_f.astype(b16)
-    out_part = jnp.dot(attended_low, w_out, preferred_element_type=f32) + contract_cols(activated, w_down)
-
-    up_grad = jnp.dot(cot, w_down, preferred_element_type=f32)
-    inner_grad = gelu_pull(up_grad)[0].astype(b16)
-    norm_two_grad = contract_cols(inner_grad, w_up)
-    grad_up = contract_rows(norm_two, inner_grad)
-    grad_down = contract_rows(cot, activated)
-
-    attended_grad = contract_cols(cot, w_out).astype(b16)
-    grad_out = contract_rows(attended_low, cot)
-    row_delta = jnp.sum(attended_grad.astype(f32) * attended, axis=-1, keepdims=True)
-    prob_grad = contract_cols(attended_grad, value)
-    score_grad = (probs * (prob_grad - row_delta)).astype(b16)
-    query_grad = jnp.dot(score_grad, key, preferred_element_type=f32) * scaling
-    key_grad = contract_rows(score_grad, query) * scaling
-    value_grad = contract_rows(probs_low, attended_grad)
-    query_pre, key_pre = rotation_pull((query_grad, key_grad))
-    projected_grad = jnp.concatenate([query_pre, key_pre, value_grad], axis=1).astype(b16)
-    norm_one_grad = contract_cols(projected_grad, w_qkv)
-    grad_qkv = contract_rows(norm_one, projected_grad)
-    hid_part = norm_one_grad * gain_one + norm_two_grad * gain_two
-
-    cot_sum = jnp.where(head_id == 0, jnp.sum(cot.astype(f32), axis=0), 0.0)
-    qkv_sum = jnp.sum(projected_grad.astype(f32), axis=0).reshape(3, HEAD)
-    qkv_sum = lax.dynamic_update_slice_in_dim(
-        jnp.zeros((3, width), f32), qkv_sum, head_id * HEAD, axis=1
-    )
-    up_sum = lax.dynamic_update_slice_in_dim(
-        jnp.zeros((part * chips,), f32),
-        jnp.sum(inner_grad.astype(f32), axis=0),
-        head_id * part,
-        axis=0,
-    )
-    sums = (
-        jnp.sum(norm_one_grad * xhat, axis=0),
-        jnp.sum(norm_one_grad, axis=0),
-        jnp.sum(norm_two_grad * xhat, axis=0),
-        jnp.sum(norm_two_grad, axis=0),
-        cot_sum,
-        qkv_sum,
-        up_sum,
-    )
-    tiles = jnp.concatenate([v.reshape(ctx_count * 2, -1) for v in sums], axis=1)
-    tile_used = tiles.shape[1]
-    tile_rows = 8 * (-(-tile_used // 1024))
-    tiles = jnp.pad(tiles, ((0, 0), (0, tile_rows * 128 - tile_used)))
-
-    groups = 2 * CORES
-    line = chips // LINE_Y
-    by_owner = (chips, groups, owned, -1)
-    by_rows = (line, LINE_Y, CORES, local_rows, width)
-    small_sum, qkv_sum, up_sum, down_sum, out_sum, out_rows, hid_rows = scatter_all(
+        small_tile(ln1_gain, ln1_bias, ln2_gain, ln2_bias, out_bias, down_bias, qkv_bias, up_bias),
+        cosine,
+        sine,
+        key_pos,
+    )
+    smalls = small_all.reshape(ctx_count * 2, SMALL_ROWS, LANES)
+    b_both = (smalls[:, OUT_BIAS, :owned] + smalls[:, DOWN_BIAS, :owned]).reshape(-1)
+    small_sum, qkv_rows, up_rows, down_rows, out_sum, out_rows, hid_rows = scatter_all(
         ctx_count,
-        [
-            tiles.reshape(chips, groups, tile_rows, 128),
-            grad_qkv.astype(b16).reshape(by_owner),
-            grad_up.astype(b16).reshape(by_owner),
-            grad_down.astype(b16).reshape(by_owner),
-        ],
-        grad_out.astype(b16).reshape(groups, owned, width),
-        out_part.astype(b16).reshape(by_rows),
-        hid_part.astype(b16).reshape(by_rows),
+        local_rows,
+        (
+            hid_all,
+            cot_all,
+            w_qkv,
+            w_up,
+            w_down,
+            w_out,
+            attended_low,
+            projected_grad,
+            norm_two,
+            activated,
+            slope,
+            stats,
+            vec,
+            qkv_sum,
+            cot_sum,
+            grad_qkv,
+            grad_down,
+            grad_out,
+        ),
     )
 
     own = hidden.astype(f32)
-    output = (own + jnp.swapaxes(out_rows, 0, 1) + (b_out + b_down)).astype(b16)
+    output = (own + jnp.swapaxes(out_rows, 0, 1) + b_both).astype(b16)
     average = jnp.mean(own, axis=-1, keepdims=True)
     spread = jnp.mean((own - average) ** 2, axis=-1, keepdims=True)
     scale = lax.rsqrt(spread + LN_EPSILON)
@@ -1053,13 +1732,12 @@
     grad_hidden = cotangent.astype(f32) + scale * (
         e - jnp.mean(e, axis=-1, keepdims=True) - xhat * jnp.mean(e * xhat, axis=-1, keepdims=True)
     )
-    mine = jnp.sum(small_sum, axis=0).reshape(-1)
-    cuts = []
-    at = 0
-    for v in sums:
-        step = v.size // (ctx_count * 2)
-        cuts.append(mine[at : at + step])
-        at += step
+    small = jnp.sum(small_sum, axis=0)
+    odd = lax.axis_index("fsdp") == 1
+    halves = jnp.where(odd, small[: COT_SUM + 1, owned:], small[: COT_SUM + 1, :owned])
+    three = small[QKV_SUM : QKV_SUM + 3].reshape(-1)
+    qkv_bias_sum = jnp.where(odd, three[3 * owned :], three[: 3 * owned])
+    up_bias_sum = small[UP_SUM : UP_SUM + 2].reshape(-1)
 
     def columns(pieces, thirds):
         rows = pieces.shape[1]
@@ -1069,18 +1747,18 @@
     return (
         output,
         grad_hidden,
-        cuts[0],
-        cuts[1],
-        columns(qkv_sum, 3),
-        cuts[5],
+        halves[0],
+        halves[1],
+        columns(qkv_rows, 3),
+        qkv_bias_sum,
         out_sum.astype(f32),
-        cuts[4],
-        cuts[2],
-        cuts[3],
-        columns(up_sum, 1),
-        cuts[6],
-        columns(down_sum, 1),
-        cuts[4],
+        halves[COT_SUM],
+        halves[2],
+        halves[3],
+        columns(up_rows, 1),
+        up_bias_sum,
+        columns(down_rows, 1),
+        halves[COT_SUM],
     )
 
 

time: 522 us -> 398 us (0.76)
  matrix products: 95.3 us -> 0 us
  other arithmetic: 25.4 us -> 11.7 us
  local copies, waits for them, and re-layouts: 27.1 us -> 16.7 us
    dot_general x18 -> x0, matrix products: 95.3 us -> none  [the longest x6 29.8 us: contract_cols(): lax.dot_general(left, right, (((1,), (1,)), ((), ())), preferred_element_...]
    pallas_call x1, Pallas kernels: 225 us -> 170 us  [scatter_all(): pl.pallas_call(lambda *refs: scatter_kernel(ctx_count, *refs), out_shape=...]
    pallas_call x1, Pallas kernels: 144 us -> 196 us  [gather_all(): pl.pallas_call(lambda *refs: gather_kernel(ctx_count, *refs), out_shape=[...]
    reduce_sum x5 -> x1, other arithmetic: 9.04 us -> 0.01 us  [split_body(): small = jnp.sum(small_sum, axis=0)]
    unnamed x55 -> x24, local copies, waits for them, and re-layouts: 14.7 us -> 8.36 us
    concatenate x2 -> x1, local copies, waits for them, and re-layouts: 5.52 us -> 0.07 us  [rotation_tables(): jnp.concatenate([cos, cos, rest], axis=1)]
where the time goes in v2:
time: 398 us; the launch traced here: 395 us
  Pallas kernels  366 us (92%)
  local copies, waits for them, and re-layouts  16.7 us (4%)
  other arithmetic  11.7 us (3%)
    pallas_call x1, Pallas kernels, gather_all(): pl.pallas_call(lambda *refs: gather_kernel(ctx_count, *refs), out_shape=[...  196 us
    pallas_call x1, Pallas kernels, scatter_all(): pl.pallas_call(lambda *refs: scatter_kernel(ctx_count, *refs), out_shape=...  170 us
    unnamed x24, local copies, waits for them, and re-layouts  8.36 us

profile of v2, /device:TPU:9, one launch (start us, length us, event | category | flops | bytes accessed | tf_op | source)
XLA Modules:
  0.0 395.1 jit_solution(6167679324088270600)
XLA Ops:
  0.6 0.8 slice_bitcast_fusion.8
  1.5 0.7 slice_bitcast_fusion.11
  2.2 0.7 bitcast_convert_fusion
  2.9 0.7 bitcast_convert_fusion.2
  3.5 0.7 bitcast_convert_fusion.4
  4.2 0.7 convert_add_fusion.1.refs_6_
  4.9 0.7 select_reduce_fusion
  5.7 1.9 fusion.11
  7.9 1.4 maximum_maximum_fusion
  9.3 0.6 broadcast_in_dim.19.refs_9_
  9.9 1.3 copy_bitcast_fusion
  11.3 195.7 %gather_all.1 = (bf16[1024,2048]{1,0:T(8,128)(2,1)}, bf16[1024,2048]{1,0:T(8,128)(2,1)}, bf16[8,4,64,768]{3,2,1,0:T(8,128)(2,1)}, bf16[8,4,64,1024]{3,2,1,0:T(8,...) custom-call(bf16[2,64,2048]{2,1,0:T(8,128)(2,1)} %get-tuple-element., ...), custom_call_target="tpu_custom_call" | custom-call | tf_op jit(solution)/shard_map/gather_all/pallas_call | solution.py:1056
  207.0 170.2 %scatter_all.1 = (f32[8,16,128]{2,1,0:T(8,128)}, bf16[8,64,768]{2,1,0:T(8,128)(2,1)}, bf16[8,64,1024]{2,1,0:T(8,128)(2,1)}, bf16[8,64,1024]{2,1,0:T(8,128)(2,1)}...) custom-call(bf16[1024,2048]{1,0:T(8,128)(2,1)} %get-tuple-element.40.refs_0_, ...), custom_call_target="tpu_custom_call" | custom-call | tf_op jit(solution)/shard_map/scatter_all/pallas_call | solution.py:1579
  377.2 2.5 reshape.292
  379.7 0.9 copy.67
  380.7 1.6 copy.72
  382.5 1.5 copy.73
  384.4 1.5 copy.74
  386.8 1.0 fusion.12
  388.0 0.8 fusion.7
  388.8 1.8 copy.71
  390.6 1.3 copy.70
  392.0 0.8 convert_element_type.57
  393.4 0.6 slice_select_fusion.1
  (40 shorter events, 3.7 us)
Async XLA Ops:
  7.6 2.4 copy-start
  7.6 2.3 copy-start.2
  380.6 1.6 copy-start.4
  382.5 1.6 copy-start.3
  384.4 2.0 copy-start.1
  385.9 2.1 copy-start.5
  388.8 3.1 copy-start.6
  388.8 4.0 %copy-start.7 = (f32[8,16,128]{2,1,0:T(8,128)S(1)}, f32[8,16,128]{2,1,0:T(8,128)}, u32[]{:S(2)}) copy-start(f32[8,16,128]{2,1,0:T(8,128)} %get-tuple-element.61) | copy-start | bytes 196612
  393.4 1.7 copy-start.8

commit v3 on v2

--- a/solution.py
+++ b/solution.py
@@ -1,3 +1,5 @@
+import functools
+
 import jax
 import jax.numpy as jnp
 from jax import lax
@@ -537,30 +539,36 @@
 
 
 class WeightGather:
-    def __init__(self, place, copies, pieces, whole):
+    def __init__(self, place, copies, pieces, whole, columns=slice(None)):
         self.place = place
         group = 2 * place.c + place.x
-        self.scattered = []
+        self.by_chip = []
         for dz, dy in place.plane_offsets():
             z, y = place.shifted(dz, dy)
             device = place.at(z, y, place.c, place.x)
-            for src, dst in pieces(z * LINE_Y + y, place.chip, group):
-                self.scattered.append(copies.remote(src, dst, device))
+            self.by_chip.append(
+                [copies.remote(src, dst, device) for src, dst in pieces(z * LINE_Y + y, place.chip, group)]
+            )
         self.kept = [copies.inside(src, dst) for src, dst in pieces(place.chip, place.chip, group)]
-        mine = whole.at[:, group]
+        mine = whole.at[:, group, :, columns]
         self.across = copies.remote(mine, mine, place.other_plane())
-        pair = whole.at[:, pl.ds(2 * place.c, 2)]
+        pair = whole.at[:, pl.ds(2 * place.c, 2), :, columns]
         self.swap = copies.remote(pair, pair, place.other_core())
 
+    def send(self, i):
+        for copy in self.by_chip[i] + (self.kept if i == 0 else []):
+            copy.start()
+
     def scatter(self):
-        for copy in self.scattered + self.kept:
-            copy.start()
+        for i in range(len(self.by_chip)):
+            self.send(i)
 
     def cross(self):
         for copy in self.kept:
             copy.wait()
-        for copy in self.scattered:
-            copy.wait_recv()
+        for copies in self.by_chip:
+            for copy in copies:
+                copy.wait_recv()
         self.across.start()
 
     def share(self):
@@ -571,8 +579,85 @@
         self.swap.wait_recv()
 
     def drain(self):
-        for copy in self.scattered + [self.across, self.swap]:
+        for copy in sum(self.by_chip, []) + [self.across, self.swap]:
             copy.wait_send()
+
+
+NORM_PARTS = 4
+GATHER_ORDER = (
+    "qkv 6",
+    "hid spread",
+    "up b 0",
+    "up a 0",
+    "out start",
+    "qkv 1",
+    "qkv 0",
+    "hid 0",
+    "small cross",
+    "up a 1",
+    "qkv 2",
+    "small share",
+    "down b 0",
+    "up b 5",
+    "up b 2",
+    "hid 1",
+    "up a 3",
+    "small done",
+    "up a 5",
+    "out share",
+    "qkv 5",
+    "cot spread",
+    "qkv 3",
+    "qkv 4",
+    "up a 4",
+    "qkv cross",
+    "hid 2",
+    "down a 0",
+    "up a 6",
+    "up a 2",
+    "up b 1",
+    "up b 3",
+    "cot 0",
+    "up a cross",
+    "hid done",
+    "norm",
+    "up b 4",
+    "up b 6",
+    "qkv share",
+    "norm",
+    "down a 2",
+    "cot 1",
+    "down a 1",
+    "down a 4",
+    "up b cross",
+    "down a 5",
+    "norm",
+    "norm",
+    "norm done",
+    "up a share",
+    "project",
+    "down a 6",
+    "down a 3",
+    "cot 2",
+    "up b share",
+    "attend",
+    "down a cross",
+    "down b 3",
+    "down b 2",
+    "down b 5",
+    "inner",
+    "down b 4",
+    "down b 6",
+    "down b 1",
+    "cot done",
+    "out grads",
+    "down b cross",
+    "down grads",
+    "attention back",
+    "down a share",
+    "down b share",
+    "qkv grads",
+)
 
 
 def nn(left, right):
@@ -850,17 +935,25 @@
             for k in range(3)
         ]
 
-    def slice_pieces(source, whole):
-        return lambda to, row, group: [
-            (source.at[:, pl.ds(pl.multiple_of(to * part, part), part)], whole.at[row, group])
-        ]
+    half = part // 2
+
+    def half_gather(source, whole, first):
+        columns = pl.ds(first, half)
+
+        def pieces(to, row, group):
+            given = pl.ds(pl.multiple_of(to * part + first, half), half)
+            return [(source.at[:, given], whole.at[row, group, :, columns])]
+
+        return WeightGather(place, copies, pieces, whole, columns)
 
     hid_g = TokenGather(place, copies, hid, hid_all)
     cot_g = TokenGather(place, copies, cot, cot_all)
     small_g = WeightGather(place, copies, lambda to, row, group: [(small, small_all.at[row, group])], small_all)
     qkv_g = WeightGather(place, copies, qkv_pieces, qkv_all)
-    up_g = WeightGather(place, copies, slice_pieces(up, up_all), up_all)
-    down_g = WeightGather(place, copies, slice_pieces(down, down_all), down_all)
+    weights = {"qkv": qkv_g}
+    for name, source, whole in (("up", up, up_all), ("down", down, down_all)):
+        weights[name + " a"] = half_gather(source, whole, 0)
+        weights[name + " b"] = half_gather(source, whole, half)
     group = 2 * place.c + place.x
     out_mine = copies.inside(out, out_all.at[group])
     out_across = copies.remote(out, out_all.at[group], place.other_plane())
@@ -902,82 +995,126 @@
         loads[name].start()
         loads[name].wait()
 
+    rows = hid_v.shape[0]
+    normed = iter(range(NORM_PARTS))
+
+    def norm_next():
+        part_rows = rows // NORM_PARTS
+        norm_rows(next(normed) * part_rows, part_rows, hid_v, vec, norm_one, norm_two, stats)
+
+    def norm_done():
+        stores["norm_two"].start()
+        stores["stats"].start()
+
+    def small_done():
+        small_g.finish()
+        fetch("small")
+        assemble_small(place, small_v, vec, qkv_rows, qkv_bias, up_bias)
+        stores["vec"].start()
+
+    def hid_done():
+        hid_g.finish()
+        fetch("hid")
+
+    def project_all():
+        qkv_g.finish()
+        fetch("qkv")
+        for name in ("cosine", "sine", "key_pos"):
+            loads[name].wait()
+        project(norm_one, qkv_v, qkv_bias, cosine, sine, query, key, value)
+
+    def attend_all():
+        attend(query, key, value, sine, key_pos, attended, attended_low, probs, probs_low)
+        stores["attended_low"].start()
+
+    def inner_all():
+        weights["up a"].finish()
+        weights["up b"].finish()
+        fetch("up")
+        feed_inner(norm_two, up_v, up_bias, activated, slope)
+        stores["activated"].start()
+        stores["slope"].start()
+
+    def out_start():
+        out_mine.start()
+        out_across.start()
+
+    def out_share():
+        out_mine.wait()
+        out_across.wait_recv()
+        out_swap.start()
+
+    def cot_done():
+        cot_g.finish()
+        loads["cot"].start()
+        out_swap.wait_recv()
+        fetch("out")
+        loads["cot"].wait()
+
+    def out_grads():
+        attended_grads(cot_v, out_v, attended_low, attended_grad, out_grad)
+        stores["out_grad"].start()
+
+    def down_grads():
+        weight_grads(cot_v, activated, up_v)
+        stores["down_grad"].start()
+        column_sums(cot_v, cot_sum)
+        stores["cot_sum"].start()
+
+    def attention_back():
+        attention_grads(
+            query, key, value, cosine, sine, attended, attended_grad, probs, probs_low, score_grad, projected_grad
+        )
+        stores["projected_grad"].start()
+
+    def qkv_grads():
+        weight_grads(norm_one, projected_grad, qkv_v)
+        stores["qkv_grad"].start()
+        column_sums(projected_grad, qkv_sum)
+        stores["qkv_sum"].start()
+
+    steps = {
+        "hid spread": hid_g.spread,
+        "cot spread": cot_g.spread,
+        "small cross": small_g.cross,
+        "small share": small_g.share,
+        "small done": small_done,
+        "out start": out_start,
+        "out share": out_share,
+        "hid done": hid_done,
+        "norm": norm_next,
+        "norm done": norm_done,
+        "project": project_all,
+        "attend": attend_all,
+        "inner": inner_all,
+        "cot done": cot_done,
+        "out grads": out_grads,
+        "down grads": down_grads,
+        "attention back": attention_back,
+        "qkv grads": qkv_grads,
+    }
+    for j in range(place.line - 1):
+        steps["hid %d" % j] = functools.partial(hid_g.step, j)
+        steps["cot %d" % j] = functools.partial(cot_g.step, j)
+    for name, gather in weights.items():
+        for i in range(len(gather.by_chip)):
+            steps["%s %d" % (name, i)] = functools.partial(gather.send, i)
+        steps[name + " cross"] = gather.cross
+        steps[name + " share"] = gather.share
+
     for name in ("cosine", "sine", "key_pos"):
         loads[name].start()
     greet(place)
     hid_g.start()
     cot_g.start()
     small_g.scatter()
-    qkv_g.scatter()
-    hid_g.spread()
-    out_mine.start()
-    out_across.start()
-    up_g.scatter()
-    small_g.cross()
-    hid_g.step(0)
-    qkv_g.cross()
-    small_g.share()
-    hid_g.step(1)
-    cot_g.spread()
-    hid_g.step(2)
-    down_g.scatter()
-    small_g.finish()
-    fetch("small")
-    assemble_small(place, small_v, vec, qkv_rows, qkv_bias, up_bias)
-    stores["vec"].start()
-    qkv_g.share()
-    cot_g.step(0)
-    hid_g.finish()
-    fetch("hid")
-    rows = hid_v.shape[0]
-    norm_rows(0, rows // 2, hid_v, vec, norm_one, norm_two, stats)
-    cot_g.step(1)
-    up_g.cross()
-    norm_rows(rows // 2, rows // 2, hid_v, vec, norm_one, norm_two, stats)
-    stores["norm_two"].start()
-    stores["stats"].start()
-    cot_g.step(2)
-    qkv_g.finish()
-    fetch("qkv")
-    for name in ("cosine", "sine", "key_pos"):
-        loads[name].wait()
-    project(norm_one, qkv_v, qkv_bias, cosine, sine, query, key, value)
-    out_mine.wait()
-    out_across.wait_recv()
-    out_swap.start()
-    down_g.cross()
-    up_g.share()
-    attend(query, key, value, sine, key_pos, attended, attended_low, probs, probs_low)
-    stores["attended_low"].start()
-    up_g.finish()
-    fetch("up")
-    down_g.share()
-    feed_inner(norm_two, up_v, up_bias, activated, slope)
-    stores["activated"].start()
-    stores["slope"].start()
-    cot_g.finish()
-    loads["cot"].start()
-    out_swap.wait_recv()
-    fetch("out")
-    loads["cot"].wait()
-    attended_grads(cot_v, out_v, attended_low, attended_grad, out_grad)
-    stores["out_grad"].start()
-    weight_grads(cot_v, activated, up_v)
-    stores["down_grad"].start()
-    column_sums(cot_v, cot_sum)
-    stores["cot_sum"].start()
-    attention_grads(
-        query, key, value, cosine, sine, attended, attended_grad, probs, probs_low, score_grad, projected_grad
-    )
-    stores["projected_grad"].start()
-    weight_grads(norm_one, projected_grad, qkv_v)
-    stores["qkv_grad"].start()
-    column_sums(projected_grad, qkv_sum)
-    stores["qkv_sum"].start()
-    down_g.finish()
+    for name in GATHER_ORDER:
+        steps[name]()
+    weights["down a"].finish()
+    weights["down b"].finish()
     for store in stores.values():
         store.wait()
-    for gather in (hid_g, cot_g, small_g, qkv_g, up_g, down_g):
+    for gather in [hid_g, cot_g, small_g] + list(weights.values()):
         gather.drain()
     out_across.wait_send()
     out_swap.wait_send()
@@ -1060,9 +1197,9 @@
         out_specs=[anywhere] * len(results),
         scratch_shapes=[pltpu.VMEM(*shape) for shape in scratch]
         + [
-            pltpu.SemaphoreType.DMA((88,)),
-            pltpu.SemaphoreType.DMA((88,)),
-            pltpu.SemaphoreType.DMA((40,)),
+            pltpu.SemaphoreType.DMA((112,)),
+            pltpu.SemaphoreType.DMA((112,)),
+            pltpu.SemaphoreType.DMA((48,)),
         ],
         compiler_params=pltpu.CompilerParams(
             collective_id=0, has_side_effects=True, vmem_limit_bytes=VMEM_BYTES
@@ -1092,30 +1229,37 @@
 
 
 class GradScatter:
-    def __init__(self, place, copies, partial, kept, from_core, from_plane, result):
+    def __init__(self, place, copies, partial, kept, from_core, from_plane, result, columns=None):
         self.place = place
         c, x, chip = place.c, place.x, place.chip
         self.kept, self.from_core, self.from_plane = kept, from_core, from_plane
-        given = partial
+        self.columns = cols = slice(0, kept.shape[3]) if columns is None else columns
+        self.load = None
+        given = partial.at[:, :, :, cols]
         if partial.shape != kept.shape:
-            self.load = copies.inside(partial.at[:, pl.ds(2 * c, 2)], kept)
-            given = partial.at[:, pl.ds(2 * (1 - c), 2)]
-        self.swap = copies.remote(given, from_core, place.other_core())
-        self.across = copies.remote(kept.at[:, 1 - x], from_plane, place.other_plane())
+            self.load = copies.inside(partial.at[:, pl.ds(2 * c, 2), :, cols], kept.at[:, :, :, cols])
+            given = partial.at[:, pl.ds(2 * (1 - c), 2), :, cols]
+        self.swap = copies.remote(given, from_core.at[:, :, :, cols], place.other_core())
+        self.across = copies.remote(
+            kept.at[:, 1 - x, :, cols], from_plane.at[:, :, cols], place.other_plane()
+        )
         self.scattered = []
         for dz, dy in place.plane_offsets():
             z, y = place.shifted(dz, dy)
             self.scattered.append(
-                copies.remote(kept.at[z * LINE_Y + y, x], result.at[chip], place.at(z, y, c, x))
+                copies.remote(
+                    kept.at[z * LINE_Y + y, x, :, cols], result.at[chip, :, cols], place.at(z, y, c, x)
+                )
             )
-        self.own = copies.inside(kept.at[chip, x], result.at[chip])
+        self.own = copies.inside(kept.at[chip, x, :, cols], result.at[chip, :, cols])
 
     def start(self):
-        self.load.start()
+        if self.load is not None:
+            self.load.start()
         self.swap.start()
 
-    def cross(self, loaded=True):
-        if loaded:
+    def cross(self):
+        if self.load is not None:
             self.load.wait()
         self.swap.wait_recv()
         x = self.place.x
@@ -1126,12 +1270,13 @@
     def add(self, x, other):
         step = 16
         per = self.kept.shape[2] // step
+        cols = self.columns
 
         @pl.loop(0, self.kept.shape[0] * per)
         def _(i):
             k, at = i // per, tile(i % per, step)
-            both = self.kept[k, x, at, :].astype(jnp.float32) + other[k, at, :].astype(jnp.float32)
-            self.kept[k, x, at, :] = both.astype(self.kept.dtype)
+            both = self.kept[k, x, at, cols].astype(jnp.float32) + other[k, at, cols].astype(jnp.float32)
+            self.kept[k, x, at, cols] = both.astype(self.kept.dtype)
 
     def scatter(self):
         self.across.wait_recv()
@@ -1149,16 +1294,16 @@
             copy.wait_send()
 
 
-def weight_grads_by_core(place, tokens, grads, kept, given):
+def weight_grads_by_core(place, tokens, grads, kept, given, columns):
     chips, half, rows = kept.shape[:3]
     step = 2 * half * rows
 
     @pl.loop(0, chips)
     def _(k):
-        grad = contract_rows(tokens[:, tile(k, step)], grads[...]).astype(jnp.bfloat16)
-        grad = grad.reshape((2,) + kept.shape[1:])
-        kept[k] = jnp.where(place.c == 0, grad[0], grad[1])
-        given[k] = jnp.where(place.c == 0, grad[1], grad[0])
+        grad = contract_rows(tokens[:, tile(k, step)], grads[:, columns]).astype(jnp.bfloat16)
+        grad = grad.reshape(2, half, rows, grad.shape[1])
+        kept[k, :, :, columns] = jnp.where(place.c == 0, grad[0], grad[1])
+        given[k, :, :, columns] = jnp.where(place.c == 0, grad[1], grad[0])
 
 
 class TokenScatter:
@@ -1171,15 +1316,20 @@
         self.last = last
         self.copies = copies
         self.over_base = copies.reserve(self.line)
-        up = place.at(jnp.minimum(z + 1, last), y, c, x)
-        down = place.at(jnp.maximum(z - 1, 0), y, c, x)
-        self.ups = {d: copies.remote(part.at[d, y], slots.at[d], up) for d in range(1, self.line)}
-        self.downs = {}
-        for d in range(last):
-            slot = jnp.where(z - 1 == d, last + 1, d)
-            self.downs[d] = copies.remote(part.at[d, y], slots.at[slot], down)
+        self.up_base = copies.reserve(self.line)
+        self.down_base = copies.reserve(self.line)
+        self.above = place.at(jnp.minimum(z + 1, last), y, c, x)
+        self.below = place.at(jnp.maximum(z - 1, 0), y, c, x)
         self.swap = copies.remote(total.at[1 - c], result.at[c], place.other_core())
         self.own = copies.inside(total.at[c], result.at[c])
+
+    def order(self, i):
+        last = self.last
+        chunk = 0
+        for z in range(self.line):
+            far = sorted(range(self.line), key=lambda k: (-abs(k - z), min(k, last - k)))
+            chunk = jnp.where(self.place.z == z, far[i], chunk)
+        return chunk
 
     def over(self, k):
         y = self.place.y
@@ -1187,43 +1337,49 @@
             self.over_base + k, self.part.at[k, 1 - y], self.from_y.at[k], self.place.other_y()
         )
 
+    def up(self, k):
+        return self.copies.remote_at(
+            self.up_base + k, self.part.at[k, self.place.y], self.slots.at[k], self.above
+        )
+
+    def down(self, k):
+        slot = jnp.where(self.place.z - 1 == k, self.line, k)
+        return self.copies.remote_at(
+            self.down_base + k, self.part.at[k, self.place.y], self.slots.at[slot], self.below
+        )
+
     def combine(self, k):
         self.over(k).wait_recv()
         add_rows(self.part.at[k, self.place.y], self.from_y.at[k], CORES)
 
-    def step(self, j):
-        z, y, last = self.place.z, self.place.y, self.last
-        above, below = last - j, j
-
-        @pl.when(z < above)
+    def step(self, i):
+        z, y = self.place.z, self.place.y
+        k = self.order(i)
+        self.combine(k)
+
+        @pl.when(k > z)
         def _():
-            self.combine(above)
-
             @pl.when(z > 0)
             def _():
-                self.ups[above].wait_recv()
-                add_rows(self.part.at[above, y], self.slots.at[above], CORES)
-
-            self.ups[above].start()
-
-        @pl.when(z > below)
+                self.up(k).wait_recv()
+                add_rows(self.part.at[k, y], self.slots.at[k], CORES)
+
+            self.up(k).start()
+
+        @pl.when(k < z)
         def _():
-            self.combine(below)
-
-            @pl.when(z < last)
+            @pl.when(z < self.last)
             def _():
-                self.downs[below].wait_recv()
-                add_rows(self.part.at[below, y], self.slots.at[below], CORES)
-
-            self.downs[below].start()
+                self.down(k).wait_recv()
+                add_rows(self.part.at[k, y], self.slots.at[k], CORES)
+
+            self.down(k).start()
 
     def reduce(self):
         z, y, last = self.place.z, self.place.y, self.last
         self.combine(z)
-        for d in range(1, self.line):
-            pl.when(z == d)(lambda: self.ups[d].wait_recv())
-        for d in range(last):
-            pl.when(z == d)(lambda: self.downs[d].wait_recv())
+        pl.when(z > 0)(lambda: self.up(z).wait_recv())
+        pl.when(z < last)(lambda: self.down(z).wait_recv())
         step = 16
         per = self.total.shape[1] // step
 
@@ -1250,27 +1406,19 @@
         z, last = self.place.z, self.last
         for k in range(self.line):
             self.over(k).wait_send()
-        for d, copy in self.ups.items():
-            pl.when(z < d)(lambda: copy.wait_send())
-        for d, copy in self.downs.items():
-            pl.when(z > d)(lambda: copy.wait_send())
-
-
-def scatter_order(i, last):
-    odd = i % 2
-    return (1 - odd) * (last - i // 2) + odd * (i // 2)
-
-
-def output_parts(scatter, attended_low, activated, out_weight, down_weight):
-    @pl.loop(0, scatter.line)
-    def _(i):
-        k = scatter_order(i, scatter.last)
-        part = scatter.part
-        at = tile(k, part.shape[1] * part.shape[2] * part.shape[3])
-        rows = nn(attended_low[at, :], flat_rows(out_weight[...]))
-        rows = rows + contract_cols(activated[at, :], flat_rows(down_weight[...]))
-        part[k] = rows.astype(part.dtype).reshape(part.shape[1:])
-        scatter.over(k).start()
+            pl.when(z < k)(lambda: self.up(k).wait_send())
+            pl.when(z > k)(lambda: self.down(k).wait_send())
+
+
+def output_part(scatter, i, attended_low, activated, out_weight, down_weight):
+    k = scatter.order(i)
+    part = scatter.part
+    size = part.shape[1] * part.shape[2] * part.shape[3]
+    at = tile(k, size)
+    rows = nn(attended_low[at, :], flat_rows(out_weight[...]))
+    rows = rows + contract_cols(activated[at, :], flat_rows(down_weight[...]))
+    part[k] = rows.astype(part.dtype).reshape(part.shape[1:])
+    scatter.over(k).start()
 
 
 def inner_grads(cot, down_weight, slope, slope_loads, inner_grad):
@@ -1284,32 +1432,28 @@
             slope_loads[i + 2].start()
 
 
-def hidden_parts(scatter, inner_grad, up_weight, projected_grad, qkv_weight, hid, stats, vec, sums):
-    sums[...] = jnp.zeros_like(sums)
-
+def hidden_part(scatter, i, inner_grad, up_weight, projected_grad, qkv_weight, hid, stats, vec, sums):
     def by_eight(values):
         return jnp.sum(values.reshape(-1, 8, values.shape[1]), axis=0)
 
-    @pl.loop(0, scatter.line)
-    def _(i):
-        k = scatter_order(i, scatter.last)
-        part = scatter.part
-        size = part.shape[2] * part.shape[3]
-
-        @pl.loop(0, LINE_Y)
-        def _(y):
-            at = tile(k * LINE_Y + y, size)
-            one = contract_cols(projected_grad[at, :], flat_rows(qkv_weight[...]))
-            two = contract_cols(inner_grad[at, :], flat_rows(up_weight[...]))
-            xhat = (hid[at, :].astype(jnp.float32) - stats[at, 0:1]) * stats[at, 1:2]
-            sums[0] += by_eight(one * xhat)
-            sums[1] += by_eight(one)
-            sums[2] += by_eight(two * xhat)
-            sums[3] += by_eight(two)
-            rows = one * vec[0:1, :] + two * vec[2:3, :]
-            part[k, y] = rows.astype(part.dtype).reshape(part.shape[2:])
-
-        scatter.over(k).start()
+    k = scatter.order(i)
+    part = scatter.part
+    size = part.shape[2] * part.shape[3]
+
+    @pl.loop(0, LINE_Y)
+    def _(y):
+        at = tile(k * LINE_Y + y, size)
+        one = contract_cols(projected_grad[at, :], flat_rows(qkv_weight[...]))
+        two = contract_cols(inner_grad[at, :], flat_rows(up_weight[...]))
+        xhat = (hid[at, :].astype(jnp.float32) - stats[at, 0:1]) * stats[at, 1:2]
+        sums[0] += by_eight(one * xhat)
+        sums[1] += by_eight(one)
+        sums[2] += by_eight(two * xhat)
+        sums[3] += by_eight(two)
+        rows = one * vec[0:1, :] + two * vec[2:3, :]
+        part[k, y] = rows.astype(part.dtype).reshape(part.shape[2:])
+
+    scatter.over(k).start()
 
 
 COT_SUM, UP_SUM, QKV_SUM = 4, 5, 7
@@ -1341,6 +1485,52 @@
             row = UP_SUM + u
             values = up_sum[0:1, at : at + LANES].reshape(1, 1, LANES)
             tiles[pl.ds(place.chip, 1), group, row : row + 1, :] = values
+
+
+SCATTER_ORDER = (
+    "outs tile 0",
+    "qkv swap",
+    "down a swap",
+    "down b swap",
+    "out swap",
+    "outs tile 1",
+    "qkv cross",
+    "down a cross",
+    "outs tile 2",
+    "outs tile 3",
+    "outs 0",
+    "inner",
+    "down b cross",
+    "up a grad",
+    "qkv scatter",
+    "up sum",
+    "up b grad",
+    "outs 1",
+    "outs 2",
+    "up a swap",
+    "hid tile 0",
+    "hid tile 1",
+    "up b swap",
+    "down b scatter",
+    "hid tile 2",
+    "down a scatter",
+    "hid tile 3",
+    "out cross",
+    "up b cross",
+    "pack",
+    "hid 0",
+    "small swap",
+    "hid 1",
+    "small cross",
+    "up b scatter",
+    "small scatter",
+    "up a cross",
+    "out finish",
+    "hid 2",
+    "up a scatter",
+    "outs reduce",
+    "hid reduce",
+)
 
 
 def scatter_kernel(
@@ -1415,10 +1605,17 @@
     place = Place(ctx_count)
     copies = Copies(send, recv, local)
     c, x = place.c, place.x
-    qkv_s = GradScatter(place, copies, qkv_grad, qkv_kept, qkv_core, qkv_plane, qkv_result)
-    down_s = GradScatter(place, copies, down_grad, down_kept, down_core, down_plane, down_result)
-    up_s = GradScatter(place, copies, down_core, up_kept, up_core, up_plane, up_result)
-    small_s = GradScatter(place, copies, tiles, small_kept, small_core, small_plane, small_result)
+    half = up_kept.shape[3] // 2
+    halves = {" a": slice(0, half), " b": slice(half, 2 * half)}
+    grads = {
+        "qkv": GradScatter(place, copies, qkv_grad, qkv_kept, qkv_core, qkv_plane, qkv_result),
+        "small": GradScatter(place, copies, tiles, small_kept, small_core, small_plane, small_result),
+    }
+    for name, cols in halves.items():
+        grads["down" + name] = GradScatter(
+            place, copies, down_grad, down_kept, down_core, down_plane, down_result, cols
+        )
+        grads["up" + name] = GradScatter(place, copies, down_core, up_kept, up_core, up_plane, up_result, cols)
     outs_s = TokenScatter(place, copies, out_part, out_from_y, out_slots, total, out_result)
     hid_s = TokenScatter(place, copies, hid_part, hid_from_y, hid_slots, total, hid_result)
     out_load = copies.inside(out_grad.at[pl.ds(2 * c, 2)], out_kept)
@@ -1469,61 +1666,86 @@
     slope_loads = [
         copies.inside(slope_in.at[pl.ds(i * step, step)], slope.at[i % 2]) for i in range(slope_in.shape[0] // step)
     ]
+    waited = set()
+
+    def need(*names):
+        for name in names:
+            if name not in waited:
+                waited.add(name)
+                loads[name].wait()
+
+    def output_tile(i):
+        need("activated", "attended_low", "out", "down")
+        output_part(outs_s, i, attended_low, act, out_weight, weight)
+
+    def inner_all():
+        need("cot")
+        inner_grads(wide, weight, slope, slope_loads, act)
+        loads["up"].start()
+        loads["norm_two"].start()
+
+    def up_half(name, last):
+        need("norm_two")
+        weight_grads_by_core(place, wide, act, up_kept, down_core, halves[name])
+        if last:
+            loads["hid"].start()
+
+    def hidden_tile(i):
+        if i == 0:
+            need("qkv", "projected_grad", "stats", "vec", "up", "hid")
+            sums[...] = jnp.zeros_like(sums)
+        hidden_part(hid_s, i, act, weight, projected_grad, qkv_weight, wide, stats, vec, sums)
+
+    def pack():
+        need("qkv_sum", "cot_sum")
+        pack_small(place, sums, cot_sum, up_sum, qkv_sum, qkv_rows, tiles)
+
+    def out_start():
+        out_load.start()
+        out_swap.start()
+
+    def hidden_reduce():
+        outs_s.own.wait()
+        outs_s.swap.wait_send()
+        hid_s.reduce()
+
+    steps = {
+        "out swap": out_start,
+        "out cross": out_cross,
+        "out finish": out_finish,
+        "inner": inner_all,
+        "up a grad": functools.partial(up_half, " a", False),
+        "up b grad": functools.partial(up_half, " b", True),
+        "up sum": lambda: column_sums(act, up_sum),
+        "pack": pack,
+        "outs reduce": outs_s.reduce,
+        "hid reduce": hidden_reduce,
+    }
+    for name, scatter in grads.items():
+        steps[name + " swap"] = scatter.start
+        steps[name + " cross"] = scatter.cross
+        steps[name + " scatter"] = scatter.scatter
+    for i in range(outs_s.line):
+        steps["outs tile %d" % i] = functools.partial(output_tile, i)
+        steps["hid tile %d" % i] = functools.partial(hidden_tile, i)
+    for j in range(outs_s.last):
+        steps["outs %d" % j] = functools.partial(outs_s.step, j)
+        steps["hid %d" % j] = functools.partial(hid_s.step, j)
+
     for name in early:
         loads[name].start()
     slope_loads[0].start()
     slope_loads[1].start()
     greet(place)
-    down_s.start()
-    qkv_s.start()
-    out_load.start()
-    out_swap.start()
-    for name in ("activated", "attended_low", "out", "down"):
-        loads[name].wait()
-    output_parts(outs_s, attended_low, act, out_weight, weight)
-    down_s.cross()
-    qkv_s.cross()
-    out_cross()
-    loads["cot"].wait()
-    inner_grads(wide, weight, slope, slope_loads, act)
-    loads["up"].start()
-    loads["norm_two"].start()
-    outs_s.step(0)
-    loads["norm_two"].wait()
-    weight_grads_by_core(place, wide, act, up_kept, down_core)
-    up_s.swap.start()
-    loads["hid"].start()
-    outs_s.step(1)
-    column_sums(act, up_sum)
-    down_s.scatter()
-    for name in ("qkv", "projected_grad", "stats", "vec", "up", "hid"):
-        loads[name].wait()
-    hidden_parts(hid_s, act, weight, projected_grad, qkv_weight, wide, stats, vec, sums)
-    up_s.cross(loaded=False)
-    outs_s.step(2)
-    qkv_s.scatter()
-    for name in ("qkv_sum", "cot_sum"):
-        loads[name].wait()
-    pack_small(place, sums, cot_sum, up_sum, qkv_sum, qkv_rows, tiles)
-    small_s.start()
-    outs_s.reduce()
-    small_s.cross()
-    out_finish()
-    up_s.scatter()
-    small_s.scatter()
-    hid_s.step(0)
-    hid_s.step(1)
-    hid_s.step(2)
-    outs_s.own.wait()
-    outs_s.swap.wait_send()
-    hid_s.reduce()
-    grads = (qkv_s, down_s, up_s, small_s)
-    for scatter in grads + (outs_s, hid_s):
+    for name in SCATTER_ORDER:
+        steps[name]()
+    scatters = list(grads.values()) + [outs_s, hid_s]
+    for scatter in scatters:
         scatter.finish()
     out_own.wait()
     hid_s.own.wait()
     hid_s.swap.wait_send()
-    for scatter in grads + (outs_s, hid_s):
+    for scatter in scatters:
         scatter.drain()
     out_swap.wait_send()
     out_across.wait_send()
@@ -1583,9 +1805,9 @@
         out_specs=[anywhere] * len(results),
         scratch_shapes=[pltpu.VMEM(*shape) for shape in scratch]
         + [
-            pltpu.SemaphoreType.DMA((80,)),
-            pltpu.SemaphoreType.DMA((80,)),
-            pltpu.SemaphoreType.DMA((40,)),
+            pltpu.SemaphoreType.DMA((96,)),
+            pltpu.SemaphoreType.DMA((96,)),
+            pltpu.SemaphoreType.DMA((48,)),
         ],
         compiler_params=pltpu.CompilerParams(
             collective_id=1, has_side_effects=True, vmem_limit_bytes=VMEM_BYTES

time: 398 us -> 339 us (0.85)
  Pallas kernels: 366 us -> 307 us
    pallas_call x1, Pallas kernels: 196 us -> 162 us  [gather_all(): pl.pallas_call(lambda *refs: gather_kernel(ctx_count, *refs), out_shape=[...]
    pallas_call x1, Pallas kernels: 170 us -> 146 us  [scatter_all(): pl.pallas_call(lambda *refs: scatter_kernel(ctx_count, *refs), out_shape=...]
where the time goes in v3:
time: 339 us; the launch traced here: 337 us
  Pallas kernels  307 us (91%)
  local copies, waits for them, and re-layouts  17 us (5%)
  other arithmetic  11.7 us (3%)
    pallas_call x1, Pallas kernels, gather_all(): pl.pallas_call(lambda *refs: gather_kernel(ctx_count, *refs), out_shape=[...  162 us
    pallas_call x1, Pallas kernels, scatter_all(): pl.pallas_call(lambda *refs: scatter_kernel(ctx_count, *refs), out_shape=...  146 us
    unnamed x24, local copies, waits for them, and re-layouts  8.36 us

profile of v3, /device:TPU:9, one launch (start us, length us, event | category | flops | bytes accessed | tf_op | source)
XLA Modules:
  0.0 337.0 jit_solution(9022596243509331189)
XLA Ops:
  0.6 0.8 slice_bitcast_fusion.8
  1.5 0.7 slice_bitcast_fusion.11
  2.2 0.7 bitcast_convert_fusion
  2.9 0.7 bitcast_convert_fusion.2
  3.5 0.7 bitcast_convert_fusion.4
  4.2 0.7 convert_add_fusion.1.refs_6_
  4.9 0.7 select_reduce_fusion
  5.7 1.9 fusion.11
  7.9 1.4 maximum_maximum_fusion
  9.3 0.6 broadcast_in_dim.19.refs_9_
  9.9 1.3 copy_bitcast_fusion
  11.3 161.7 %gather_all.1 = (bf16[1024,2048]{1,0:T(8,128)(2,1)}, bf16[1024,2048]{1,0:T(8,128)(2,1)}, bf16[8,4,64,768]{3,2,1,0:T(8,128)(2,1)}, bf16[8,4,64,1024]{3,2,1,0:T(8,...) custom-call(bf16[2,64,2048]{2,1,0:T(8,128)(2,1)} %get-tuple-element., ...), custom_call_target="tpu_custom_call" | custom-call | tf_op jit(solution)/shard_map/gather_all/pallas_call | solution.py:1193
  173.0 145.7 %scatter_all.1 = (f32[8,16,128]{2,1,0:T(8,128)}, bf16[8,64,768]{2,1,0:T(8,128)(2,1)}, bf16[8,64,1024]{2,1,0:T(8,128)(2,1)}, bf16[8,64,1024]{2,1,0:T(8,128)(2,1)}...) custom-call(bf16[1024,2048]{1,0:T(8,128)(2,1)} %get-tuple-element.40.refs_0_, ...), custom_call_target="tpu_custom_call" | custom-call | tf_op jit(solution)/shard_map/scatter_all/pallas_call | solution.py:1801
  318.7 2.8 reshape.292
  321.5 0.9 copy.67
  322.5 1.6 copy.72
  324.3 1.5 copy.73
  326.2 1.5 copy.74
  328.7 1.0 fusion.12
  329.8 0.8 fusion.7
  330.7 1.8 copy.71
  332.4 1.3 copy.70
  333.8 0.8 convert_element_type.57
  335.2 0.6 slice_select_fusion.1
  (40 shorter events, 3.7 us)
Async XLA Ops:
  7.6 2.4 copy-start
  7.6 2.3 copy-start.2
  322.5 1.6 copy-start.4
  324.3 1.6 copy-start.3
  326.2 2.0 copy-start.1
  327.7 2.1 copy-start.5
  330.6 3.1 copy-start.6
  330.6 4.0 %copy-start.7 = (f32[8,16,128]{2,1,0:T(8,128)S(1)}, f32[8,16,128]{2,1,0:T(8,128)}, u32[]{:S(2)}) copy-start(f32[8,16,128]{2,1,0:T(8,128)} %get-tuple-element.61) | copy-start | bytes 196612
  335.2 1.7 copy-start.8

commit v4 on v3

--- a/solution.py
+++ b/solution.py
@@ -464,7 +464,7 @@
         partners.append(place.at(z, y, place.c, place.x))
     for partner in partners:
         pl.semaphore_signal(barrier, inc=1, device_id=partner, device_id_type=MESH)
-    pl.semaphore_wait(barrier, len(partners))
+    return lambda: pl.semaphore_wait(barrier, len(partners))
 
 
 class TokenGather:
@@ -592,6 +592,7 @@
     "out start",
     "qkv 1",
     "qkv 0",
+    "tables",
     "hid 0",
     "small cross",
     "up a 1",
@@ -690,12 +691,74 @@
     return lax.broadcasted_iota(jnp.int32, shape, len(shape) - 1)
 
 
+def pack_parameters(vectors, tile_ref):
+    half = LANES // 2
+    ln1_gain, ln1_bias, ln2_gain, ln2_bias, out_bias, down_bias, qkv_bias, up_bias = [
+        ref[...].astype(jnp.float32).reshape(1, -1) for ref in vectors
+    ]
+    tile_ref[...] = jnp.zeros_like(tile_ref)
+    for row, values in (
+        (GAIN_ONE, ln1_gain),
+        (SHIFT_ONE, ln1_bias),
+        (GAIN_TWO, ln2_gain),
+        (SHIFT_TWO, ln2_bias),
+        (OUT_BIAS, out_bias),
+        (DOWN_BIAS, down_bias),
+    ):
+        tile_ref[row : row + 1, :half] = values
+        tile_ref[row : row + 1, half:] = values
+    tile_ref[QKV_BIAS : QKV_BIAS + 1, :] = qkv_bias[:, :LANES]
+    tile_ref[QKV_BIAS + 1 : QKV_BIAS + 2, :half] = qkv_bias[:, LANES:]
+    tile_ref[QKV_BIAS + 1 : QKV_BIAS + 2, half:] = qkv_bias[:, :half]
+    tile_ref[QKV_BIAS + 2 : QKV_BIAS + 3, :] = qkv_bias[:, half:]
+    tile_ref[UP_BIAS : UP_BIAS + 1, :] = up_bias[:, :LANES]
+    tile_ref[UP_BIAS + 1 : UP_BIAS + 2, :] = up_bias[:, LANES:]
+
+
+def position_tables(ctx_count, pairing, cosine, sine, key_pos):
+    block_rows = cosine.shape[0] // (2 * ctx_count)
+    half_rot = ROT // 2
+    lane = lanes_of((block_rows, LANES))
+    power = (lane % half_rot).astype(jnp.float32) * (2.0 / ROT)
+    frequency = jnp.exp(power * -9.210340371976184)
+    row = lax.broadcasted_iota(jnp.int32, (block_rows, LANES), 0)
+
+    @pl.loop(0, ctx_count)
+    def _(device):
+        owned = pairing[device]
+        for late in range(2):
+            block = 2 * ctx_count - 1 - owned if late else owned
+            where = (block * block_rows + row).astype(jnp.float32)
+            angles = where * frequency
+            at = tile(2 * device + late, block_rows)
+            cosine[at, :] = jnp.where(lane < ROT, jnp.cos(angles), 1.0)
+            sin = jnp.sin(angles)
+            sine[at, :] = jnp.where(lane < half_rot, -sin, jnp.where(lane < ROT, sin, where))
+
+    lane = lanes_of((8, LANES))
+    per = LANES // (2 * block_rows)
+    for first in range(0, ctx_count, per):
+        block = jnp.zeros((8, LANES), jnp.int32)
+        for device in range(per):
+            owned = pairing[first + device]
+            for late in range(2):
+                value = 2 * ctx_count - 1 - owned if late else owned
+                block = jnp.where(lane // block_rows == 2 * device + late, value, block)
+        at = first * 2 * block_rows
+        key_pos[:, at : at + LANES] = (block * block_rows + lane % block_rows).astype(jnp.float32)
+
+
+def split_sequences(rows, own):
+    for i in range(rows.shape[1]):
+        own[i] = rows[:, i, :]
+
+
 def assemble_small(place, small, vec, qkv_rows, qkv_bias, up_bias):
     chips, groups = small.shape[:2]
     low = lanes_of((1, LANES)) < LANES // 2
     for pair in range(chips * groups // 2):
         chip, group = pair // (groups // 2), pair % (groups // 2) * 2
-        for row in range(4):
+        for row in range(6):
             a = small[chip, group, row : row + 1, :]
             b = small[chip, group + 1, row : row + 1, :]
             vec[row : row + 1, pair * LANES : (pair + 1) * LANES] = jnp.where(low, a, b)
@@ -856,16 +919,21 @@
 
 def gather_kernel(
     ctx_count,
-    hid,
-    cot,
+    hid_in,
+    cot_in,
+    ln1_gain_in,
+    ln1_bias_in,
+    ln2_gain_in,
+    ln2_bias_in,
+    out_bias_in,
+    down_bias_in,
+    qkv_bias_in,
+    up_bias_in,
     qkv,
     up,
     down,
     out,
-    small,
-    cosine_in,
-    sine_in,
-    key_pos_in,
+    pairing,
     hid_all,
     cot_all,
     qkv_all,
@@ -885,6 +953,19 @@
     stats_out,
     qkv_sum_out,
     cot_sum_out,
+    hid_rows,
+    cot_rows,
+    hid,
+    cot,
+    ln1_gain,
+    ln1_bias,
+    ln2_gain,
+    ln2_bias,
+    out_bias,
+    down_bias,
+    qkv_bias_own,
+    up_bias_own,
+    small,
     hid_v,
     cot_v,
     qkv_v,
@@ -962,9 +1043,8 @@
     loads = {
         name: copies.inside(src, dst)
         for name, src, dst in (
-            ("cosine", cosine_in, cosine),
-            ("sine", sine_in, sine),
-            ("key_pos", key_pos_in, key_pos),
+            ("hid rows", hid_in, hid_rows),
+            ("cot rows", cot_in, cot_rows),
             ("small", small_all, small_v),
             ("hid", hid_all, hid_v),
             ("cot", cot_all, cot_v),
@@ -1019,8 +1099,6 @@
     def project_all():
         qkv_g.finish()
         fetch("qkv")
-        for name in ("cosine", "sine", "key_pos"):
-            loads[name].wait()
         project(norm_one, qkv_v, qkv_bias, cosine, sine, query, key, value)
 
     def attend_all():
@@ -1074,6 +1152,7 @@
         stores["qkv_sum"].start()
 
     steps = {
+        "tables": lambda: position_tables(ctx_count, pairing, cosine, sine, key_pos),
         "hid spread": hid_g.spread,
         "cot spread": cot_g.spread,
         "small cross": small_g.cross,
@@ -1102,12 +1181,34 @@
         steps[name + " cross"] = gather.cross
         steps[name + " share"] = gather.share
 
-    for name in ("cosine", "sine", "key_pos"):
-        loads[name].start()
-    greet(place)
+    vectors = (ln1_gain, ln1_bias, ln2_gain, ln2_bias, out_bias, down_bias, qkv_bias_own, up_bias_own)
+    vectors_in = (
+        ln1_gain_in,
+        ln1_bias_in,
+        ln2_gain_in,
+        ln2_bias_in,
+        out_bias_in,
+        down_bias_in,
+        qkv_bias_in,
+        up_bias_in,
+    )
+    vector_loads = [copies.inside(src, dst) for src, dst in zip(vectors_in, vectors)]
+    loads["hid rows"].start()
+    for load in vector_loads:
+        load.start()
+    loads["cot rows"].start()
+    answered = greet(place)
+    loads["hid rows"].wait()
+    split_sequences(hid_rows, hid)
+    for load in vector_loads:
+        load.wait()
+    pack_parameters(vectors, small)
+    answered()
     hid_g.start()
+    small_g.scatter()
+    loads["cot rows"].wait()
+    split_sequences(cot_rows, cot)
     cot_g.start()
-    small_g.scatter()
     for name in GATHER_ORDER:
         steps[name]()
     weights["down a"].finish()
@@ -1120,20 +1221,22 @@
     out_swap.wait_send()
 
 
-def gather_all(ctx_count, hid, cot, qkv, up, down, out, small, cosine, sine, key_pos):
+def gather_all(ctx_count, hid, cot, vectors, qkv, up, down, out, pairing):
     f32, b16 = jnp.float32, jnp.bfloat16
     chips = ctx_count // CORES
     rows = qkv.shape[0]
     groups = CORES * 2
-    tokens = ctx_count * hid.shape[1]
+    tokens = ctx_count * hid.shape[0]
     width = out.shape[1]
     head3, part = qkv.shape[1] // chips, up.shape[1] // chips
     head = head3 // 3
     qkv_s = ((chips, groups, rows, head3), b16)
     part_s = ((chips, groups, rows, part), b16)
     out_s = ((groups, rows, width), b16)
-    small_s = ((chips, groups) + small.shape, f32)
+    small = (SMALL_ROWS, LANES)
+    small_s = ((chips, groups) + small, f32)
     wide_s, narrow_s = ((tokens, width), b16), ((tokens, head), b16)
+    own_s = ((hid.shape[1], hid.shape[0], width), b16)
     results = [
         wide_s,
         wide_s,
@@ -1156,6 +1259,14 @@
         ((8, width), f32),
     ]
     scratch = [
+        (hid.shape, b16),
+        (cot.shape, b16),
+        own_s,
+        own_s,
+    ]
+    scratch += [(vector.shape, b16) for vector in vectors]
+    scratch += [
+        (small, f32),
         wide_s,
         wide_s,
         qkv_s,
@@ -1188,12 +1299,12 @@
         ((8, head3), f32),
         ((8, width), f32),
     ]
-    operands = (hid, cot, qkv, up, down, out, small, cosine, sine, key_pos)
+    operands = (hid, cot, *vectors, qkv, up, down, out, pairing)
     anywhere = pl.BlockSpec(memory_space=pl.ANY)
     return pl.pallas_call(
         lambda *refs: gather_kernel(ctx_count, *refs),
         out_shape=[jax.ShapeDtypeStruct(*shape) for shape in results],
-        in_specs=[anywhere] * len(operands),
+        in_specs=[anywhere] * (len(operands) - 1) + [pl.BlockSpec(memory_space=pltpu.SMEM)],
         out_specs=[anywhere] * len(results),
         scratch_shapes=[pltpu.VMEM(*shape) for shape in scratch]
         + [
@@ -1736,7 +1847,7 @@
         loads[name].start()
     slope_loads[0].start()
     slope_loads[1].start()
-    greet(place)
+    greet(place)()
     for name in SCATTER_ORDER:
         steps[name]()
     scatters = list(grads.values()) + [outs_s, hid_s]
@@ -1816,44 +1927,146 @@
     )(*operands)
 
 
-def small_tile(ln1_gain, ln1_bias, ln2_gain, ln2_bias, out_bias, down_bias, qkv_bias, up_bias):
+def finish_kernel(
+    qkv_in,
+    up_in,
+    down_in,
+    out_in,
+    out_rows_in,
+    hid_rows_in,
+    hidden_in,
+    cotangent_in,
+    small,
+    vec,
+    ln1_gain,
+    ln1_bias,
+    qkv_bias,
+    out_bias,
+    ln2_gain,
+    ln2_bias,
+    up_bias,
+    down_bias,
+    output_out,
+    grad_hidden_out,
+    qkv_out,
+    out_out,
+    up_out,
+    down_out,
+    qkv_rows,
+    up_rows,
+    down_rows,
+    out_piece,
+    out_rows,
+    hid_rows,
+    hidden,
+    cotangent,
+    output,
+    grad_hidden,
+    qkv,
+    out,
+    up,
+    down,
+    load_sems,
+    store_sems,
+):
+    f32 = jnp.float32
+    given = (up_in, down_in, qkv_in, out_in, out_rows_in, hid_rows_in, hidden_in, cotangent_in)
+    held = (up_rows, down_rows, qkv_rows, out_piece, out_rows, hid_rows, hidden, cotangent)
+    loads = [pltpu.make_async_copy(src, dst, load_sems.at[i]) for i, (src, dst) in enumerate(zip(given, held))]
+    made = (up, down, qkv, out, output, grad_hidden)
+    asked = (up_out, down_out, qkv_out, out_out, output_out, grad_hidden_out)
+    stores = [pltpu.make_async_copy(src, dst, store_sems.at[i]) for i, (src, dst) in enumerate(zip(made, asked))]
+    for load in loads:
+        load.start()
+
+    total = jnp.sum(small[...], axis=0)
     half = LANES // 2
-
-    def put(values, row, lane):
-        values = values.astype(jnp.float32).reshape(1, -1)
-        return lax.pad(
-            values,
-            jnp.float32(0),
-            ((row, SMALL_ROWS - 1 - row, 0), (lane, LANES - lane - values.shape[1], 0)),
-        )
-
-    total = jnp.zeros((SMALL_ROWS, LANES), jnp.float32)
-    for row, values in (
-        (GAIN_ONE, ln1_gain),
-        (SHIFT_ONE, ln1_bias),
-        (GAIN_TWO, ln2_gain),
-        (SHIFT_TWO, ln2_bias),
-        (OUT_BIAS, out_bias),
-        (DOWN_BIAS, down_bias),
-    ):
-        total = total + put(values, row, 0) + put(values, row, half)
-    total = total + put(qkv_bias[:LANES], QKV_BIAS, 0)
-    total = total + put(qkv_bias[LANES:], QKV_BIAS + 1, 0) + put(qkv_bias[:half], QKV_BIAS + 1, half)
-    total = total + put(qkv_bias[half:], QKV_BIAS + 2, 0)
-    return total + put(up_bias[:LANES], UP_BIAS, 0) + put(up_bias[LANES:], UP_BIAS + 1, 0)
-
-
-def rotation_tables(positions):
-    half_rot = ROT // 2
-    where = positions.astype(jnp.float32)[:, None]
-    frequency = 1.0 / 10000.0 ** (jnp.arange(half_rot).astype(jnp.float32) * 2.0 / ROT)
-    angles = where * frequency[None, :]
-    cos, sin = jnp.cos(angles), jnp.sin(angles)
-    rest = jnp.ones((positions.shape[0], LANES - ROT), jnp.float32)
-    return (
-        jnp.concatenate([cos, cos, rest], axis=1),
-        jnp.concatenate([-sin, sin, rest * where], axis=1),
-    )
+    odd = lax.axis_index("fsdp") == 1
+    halves = jnp.where(odd, total[: COT_SUM + 1, half:], total[: COT_SUM + 1, :half])
+    for row, ref in enumerate((ln1_gain, ln1_bias, ln2_gain, ln2_bias, out_bias)):
+        ref[...] = halves[row]
+    down_bias[...] = halves[COT_SUM]
+    for u in range(2):
+        up_bias[u * LANES : (u + 1) * LANES] = total[UP_SUM + u]
+    first, middle, last = [total[QKV_SUM + u : QKV_SUM + u + 1] for u in range(3)]
+    even_row = jnp.concatenate([first, middle[:, :half]], axis=1)
+    odd_row = jnp.concatenate([middle[:, half:], last], axis=1)
+    qkv_bias[...] = jnp.where(odd, odd_row, even_row)[0]
+
+    chips = up_rows.shape[0]
+    for i, rows, made_ref in ((0, up_rows, up), (1, down_rows, down)):
+        loads[i].wait()
+        size = rows.shape[2]
+        for k in range(chips):
+            made_ref[:, k * size : (k + 1) * size] = rows[k].astype(f32)
+        stores[i].start()
+    loads[2].wait()
+    third = qkv.shape[1] // 3
+    for k in range(chips):
+        for t in range(3):
+            at = t * third + k * HEAD
+            qkv[:, at : at + HEAD] = qkv_rows[k, :, t * HEAD : (t + 1) * HEAD].astype(f32)
+    stores[2].start()
+    loads[3].wait()
+    out[...] = out_piece[...].astype(f32)
+    stores[3].start()
+
+    for load in loads[4:]:
+        load.wait()
+    bias = vec[OUT_BIAS : OUT_BIAS + 1, :] + vec[DOWN_BIAS : DOWN_BIAS + 1, :]
+    step = 16
+
+    @pl.loop(0, hidden.shape[0] // step)
+    def _(i):
+        at = tile(i, step)
+        both, grads = [], []
+        for s in range(hidden.shape[1]):
+            x = hidden[at, s, :].astype(f32)
+            both.append(x + out_rows[s, at, :] + bias)
+            average = jnp.mean(x, axis=1, keepdims=True)
+            centered = x - average
+            scale = lax.rsqrt(jnp.mean(centered * centered, axis=1, keepdims=True) + LN_EPSILON)
+            xhat = centered * scale
+            e = hid_rows[s, at, :]
+            slope = jnp.mean(e * xhat, axis=1, keepdims=True)
+            back = scale * (e - jnp.mean(e, axis=1, keepdims=True) - xhat * slope)
+            grads.append(cotangent[at, s, :].astype(f32) + back)
+        output[at] = jnp.stack(both, axis=1).astype(output.dtype)
+        grad_hidden[at] = jnp.stack(grads, axis=1)
+
+    stores[4].start()
+    stores[5].start()
+    for store in stores:
+        store.wait()
+
+
+def finish_all(qkv_rows, up_rows, down_rows, out_sum, out_rows, hid_rows, hidden, cotangent, small, vec):
+    f32 = jnp.float32
+    rows, width = out_sum.shape
+    part, head3 = up_rows.shape[0] * up_rows.shape[2], qkv_rows.shape[0] * qkv_rows.shape[2]
+    vectors = [rows, rows, 3 * rows, rows, rows, rows, part // width * rows, rows]
+    big = [
+        (hidden.shape, hidden.dtype),
+        (hidden.shape, f32),
+        ((rows, head3), f32),
+        ((rows, width), f32),
+        ((rows, part), f32),
+        ((rows, part), f32),
+    ]
+    operands = (qkv_rows, up_rows, down_rows, out_sum, out_rows, hid_rows, hidden, cotangent)
+    anywhere, held = pl.BlockSpec(memory_space=pl.ANY), pl.BlockSpec(memory_space=pltpu.VMEM)
+    return pl.pallas_call(
+        finish_kernel,
+        out_shape=[jax.ShapeDtypeStruct((n,), f32) for n in vectors]
+        + [jax.ShapeDtypeStruct(*shape) for shape in big],
+        in_specs=[anywhere] * len(operands) + [held, held],
+        out_specs=[held] * len(vectors) + [anywhere] * len(big),
+        scratch_shapes=[pltpu.VMEM(o.shape, o.dtype) for o in operands]
+        + [pltpu.VMEM(*shape) for shape in big]
+        + [pltpu.SemaphoreType.DMA((8,)), pltpu.SemaphoreType.DMA((8,))],
+        compiler_params=pltpu.CompilerParams(vmem_limit_bytes=VMEM_BYTES),
+        name="finish_all",
+    )(*operands, small, vec)
 
 
 def split_body(
@@ -1873,17 +2086,7 @@
     down_weight,
     down_bias,
 ):
-    local_rows, seq_count, width = hidden.shape
     ctx_count = lax.axis_size("ctx")
-    chips = ctx_count // CORES
-    total_rows = local_rows * ctx_count
-    f32, b16 = jnp.float32, jnp.bfloat16
-    head_id = lax.axis_index("ctx") // CORES
-    owned = width // (ctx_count * 2)
-    positions = row_positions(pairing, jnp.int32(0), total_rows, local_rows // 2, ctx_count)
-    cosine, sine = rotation_tables(positions)
-    key_pos = jnp.broadcast_to(positions.astype(f32)[None, :], (8, total_rows))
-
     (
         hid_all,
         cot_all,
@@ -1891,7 +2094,7 @@
         w_up,
         w_down,
         w_out,
-        small_all,
+        _,
         attended_low,
         projected_grad,
         norm_two,
@@ -1906,22 +2109,18 @@
         cot_sum,
     ) = gather_all(
         ctx_count,
-        jnp.swapaxes(hidden, 0, 1),
-        jnp.swapaxes(cotangent, 0, 1),
+        hidden,
+        cotangent,
+        (ln1_gain, ln1_bias, ln2_gain, ln2_bias, out_bias, down_bias, qkv_bias, up_bias),
         qkv_weight,
         up_weight,
         down_weight,
         out_weight,
-        small_tile(ln1_gain, ln1_bias, ln2_gain, ln2_bias, out_bias, down_bias, qkv_bias, up_bias),
-        cosine,
-        sine,
-        key_pos,
-    )
-    smalls = small_all.reshape(ctx_count * 2, SMALL_ROWS, LANES)
-    b_both = (smalls[:, OUT_BIAS, :owned] + smalls[:, DOWN_BIAS, :owned]).reshape(-1)
+        pairing,
+    )
     small_sum, qkv_rows, up_rows, down_rows, out_sum, out_rows, hid_rows = scatter_all(
         ctx_count,
-        local_rows,
+        hidden.shape[0],
         (
             hid_all,
             cot_all,
@@ -1943,44 +2142,39 @@
             grad_out,
         ),
     )
-
-    own = hidden.astype(f32)
-    output = (own + jnp.swapaxes(out_rows, 0, 1) + b_both).astype(b16)
-    average = jnp.mean(own, axis=-1, keepdims=True)
-    spread = jnp.mean((own - average) ** 2, axis=-1, keepdims=True)
-    scale = lax.rsqrt(spread + LN_EPSILON)
-    xhat = (own - average) * scale
-    e = jnp.swapaxes(hid_rows, 0, 1)
-    grad_hidden = cotangent.astype(f32) + scale * (
-        e - jnp.mean(e, axis=-1, keepdims=True) - xhat * jnp.mean(e * xhat, axis=-1, keepdims=True)
-    )
-    small = jnp.sum(small_sum, axis=0)
-    odd = lax.axis_index("fsdp") == 1
-    halves = jnp.where(odd, small[: COT_SUM + 1, owned:], small[: COT_SUM + 1, :owned])
-    three = small[QKV_SUM : QKV_SUM + 3].reshape(-1)
-    qkv_bias_sum = jnp.where(odd, three[3 * owned :], three[: 3 * owned])
-    up_bias_sum = small[UP_SUM : UP_SUM + 2].reshape(-1)
-
-    def columns(pieces, thirds):
-        rows = pieces.shape[1]
-        split = pieces.astype(f32).reshape(chips, rows, thirds, -1)
-        return jnp.transpose(split, (1, 2, 0, 3)).reshape(rows, -1)
-
+    (
+        grad_ln1_gain,
+        grad_ln1_bias,
+        grad_qkv_bias,
+        grad_out_bias,
+        grad_ln2_gain,
+        grad_ln2_bias,
+        grad_up_bias,
+        grad_down_bias,
+        output,
+        grad_hidden,
+        grad_qkv_weight,
+        grad_out_weight,
+        grad_up_weight,
+        grad_down_weight,
+    ) = finish_all(
+        qkv_rows, up_rows, down_rows, out_sum, out_rows, hid_rows, hidden, cotangent, small_sum, vec
+    )
     return (
         output,
         grad_hidden,
-        halves[0],
-        halves[1],
-        columns(qkv_rows, 3),
-        qkv_bias_sum,
-        out_sum.astype(f32),
-        halves[COT_SUM],
-        halves[2],
-        halves[3],
-        columns(up_rows, 1),
-        up_bias_sum,
-        columns(down_rows, 1),
-        halves[COT_SUM],
+        grad_ln1_gain,
+        grad_ln1_bias,
+        grad_qkv_weight,
+        grad_qkv_bias,
+        grad_out_weight,
+        grad_out_bias,
+        grad_ln2_gain,
+        grad_ln2_bias,
+        grad_up_weight,
+        grad_up_bias,
+        grad_down_weight,
+        grad_down_bias,
     )
 
 

time: 339 us -> 316 us (0.932)
  local copies, waits for them, and re-layouts: 17 us -> 0 us
  other arithmetic: 11.7 us -> 0 us
  Pallas kernels: 307 us -> 314 us
    pallas_call x0 -> x1, Pallas kernels: none -> 10.2 us  [finish_all(): pl.pallas_call(finish_kernel, out_shape=[jax.ShapeDtypeStruct((n,), f32)...]
    unnamed x24 -> x0, local copies, waits for them, and re-layouts: 8.36 us -> none
    reshape x6 -> x0, local copies, waits for them, and re-layouts: 5.86 us -> none  [the longest x2 3.74 us: columns(): return jnp.transpose(split, (1, 2, 0, 3)).reshape(rows, -1)]
    pallas_call x1, Pallas kernels: 162 us -> 158 us  [gather_all(): pl.pallas_call(lambda *refs: gather_kernel(ctx_count, *refs), out_shape=[...]
where the time goes in v4:
time: 316 us; the launch traced here: 315 us
  Pallas kernels  314 us (99%)
    pallas_call x1, Pallas kernels, gather_all(): pl.pallas_call(lambda *refs: gather_kernel(ctx_count, *refs), out_shape=[...  158 us
    pallas_call x1, Pallas kernels, scatter_all(): pl.pallas_call(lambda *refs: scatter_kernel(ctx_count, *refs), out_shape=...  146 us
    pallas_call x1, Pallas kernels, finish_all(): pl.pallas_call(finish_kernel, out_shape=[jax.ShapeDtypeStruct((n,), f32)...  10.2 us

profile of v4, /device:TPU:9, one launch (start us, length us, event | category | flops | bytes accessed | tf_op | source)
XLA Modules:
  0.0 315.0 jit_solution(16236515248379353874)
XLA Ops:
  0.7 157.8 %gather_all.1 = (bf16[1024,2048]{1,0:T(8,128)(2,1)}, bf16[1024,2048]{1,0:T(8,128)(2,1)}, bf16[8,4,64,768]{3,2,1,0:T(8,128)(2,1)}, bf16[8,4,64,1024]{3,2,1,0:T(8,...) custom-call(bf16[64,2,2048]{2,1,0:T(2,128)(2,1)} %hidden_in.1, ...), custom_call_target="tpu_custom_call" | custom-call | tf_op jit(solution)/shard_map/gather_all/pallas_call | solution.py:1304
  158.5 146.0 %scatter_all.1 = (f32[8,16,128]{2,1,0:T(8,128)}, bf16[8,64,768]{2,1,0:T(8,128)(2,1)}, bf16[8,64,1024]{2,1,0:T(8,128)(2,1)}, bf16[8,64,1024]{2,1,0:T(8,128)(2,1)}...) custom-call(bf16[1024,2048]{1,0:T(8,128)(2,1)} %get-tuple-element.53.refs_0_, ...), custom_call_target="tpu_custom_call" | custom-call | tf_op jit(solution)/shard_map/scatter_all/pallas_call | solution.py:1912
  304.5 10.2 %finish_all.1 = (f32[64]{0:T(128)}, f32[64]{0:T(128)}, f32[192]{0:T(256)}, f32[64]{0:T(128)}, f32[64]{0:T(128)}, /*index=5*/f32[64]{0:T(128)}, f32[256]{0:T(256)...) custom-call(bf16[8,64,768]{2,1,0:T(8,128)(2,1)} %get-tuple-element.7, ...), custom_call_target="tpu_custom_call" | custom-call | tf_op jit(solution)/shard_map/finish_all/pallas_call | solution.py:2058

commit v5 on v4

--- a/solution.py
+++ b/solution.py
@@ -467,75 +467,82 @@
     return lambda: pl.semaphore_wait(barrier, len(partners))
 
 
+TOKEN_CHUNKS = 2
+
+
 class TokenGather:
     def __init__(self, place, copies, own, whole):
-        self.place = place
-        self.whole = whole
+        self.place, self.copies, self.whole = place, copies, whole
         c, chip, z, y = place.c, place.chip, place.z, place.y
         rows = own.shape[1]
-        block = whole.at[pl.ds(pl.multiple_of((chip * CORES + c) * rows, rows), rows)]
+        block = whole.at[tile(chip * CORES + c, rows)]
         self.first = copies.remote(own.at[1 - c], block, place.other_core())
         self.mine = copies.inside(own.at[c], block)
-        last = place.line - 1
+        self.size = CORES * rows // TOKEN_CHUNKS
+        self.last = last = place.line - 1
         up = place.at(jnp.minimum(z + 1, last), y, c, place.x)
         down = place.at(jnp.maximum(z - 1, 0), y, c, place.x)
-
-        def pair(zz):
-            first = (jnp.clip(zz, 0, last) * LINE_Y + y) * CORES * rows
-            return whole.at[pl.ds(pl.multiple_of(first, CORES * rows), CORES * rows)]
-
-        self.ups = [copies.remote(pair(z - j), pair(z - j), up) for j in range(last)]
-        self.downs = [copies.remote(pair(z + j), pair(z + j), down) for j in range(last)]
-        self.over_own = copies.remote(pair(z), pair(z), place.other_y())
-        self.over_ups = [copies.remote(pair(z - 1 - j), pair(z - 1 - j), place.other_y()) for j in range(last)]
-        self.over_downs = [copies.remote(pair(z + 1 + j), pair(z + 1 + j), place.other_y()) for j in range(last)]
-        self.last = last
+        over = place.other_y()
+        chunks = range(TOKEN_CHUNKS)
+        self.ups = [[self.copy(z - j, ch, up) for ch in chunks] for j in range(last)]
+        self.downs = [[self.copy(z + j, ch, down) for ch in chunks] for j in range(last)]
+        self.over_own = [self.copy(z, ch, over) for ch in chunks]
+        self.over_ups = [[self.copy(z - 1 - j, ch, over) for ch in chunks] for j in range(last)]
+        self.over_downs = [[self.copy(z + 1 + j, ch, over) for ch in chunks] for j in range(last)]
+
+    def copy(self, z, ch, device):
+        chip = jnp.clip(z, 0, self.last) * LINE_Y + self.place.y
+        chunk = self.whole.at[tile(chip * TOKEN_CHUNKS + ch, self.size)]
+        return self.copies.remote(chunk, chunk, device)
 
     def start(self):
         self.mine.start()
         self.first.start()
 
-    def spread(self):
-        self.mine.wait()
-        self.first.wait_recv()
+    def spread(self, ch):
+        if ch == 0:
+            self.mine.wait()
+            self.first.wait_recv()
         z = self.place.z
-        pl.when(z < self.last)(lambda: self.ups[0].start())
-        pl.when(z > 0)(lambda: self.downs[0].start())
-        self.over_own.start()
-
-    def step(self, j):
+        pl.when(z < self.last)(lambda: self.ups[0][ch].start())
+        pl.when(z > 0)(lambda: self.downs[0][ch].start())
+        self.over_own[ch].start()
+
+    def step(self, j, ch):
         z, last = self.place.z, self.last
 
         @pl.when(z - 1 - j >= 0)
         def _():
-            self.ups[j].wait_recv()
+            self.ups[j][ch].wait_recv()
             if j + 1 < last:
-                pl.when(z < last)(lambda: self.ups[j + 1].start())
-            self.over_ups[j].start()
+                pl.when(z < last)(lambda: self.ups[j + 1][ch].start())
+            self.over_ups[j][ch].start()
 
         @pl.when(z + 1 + j <= last)
         def _():
-            self.downs[j].wait_recv()
+            self.downs[j][ch].wait_recv()
             if j + 1 < last:
-                pl.when(z > 0)(lambda: self.downs[j + 1].start())
-            self.over_downs[j].start()
+                pl.when(z > 0)(lambda: self.downs[j + 1][ch].start())
+            self.over_downs[j][ch].start()
 
     def finish(self):
         z, last = self.place.z, self.last
-        self.over_own.wait_recv()
-        for j in range(last):
-            pl.when(z - 1 - j >= 0)(lambda: self.over_ups[j].wait_recv())
-            pl.when(z + 1 + j <= last)(lambda: self.over_downs[j].wait_recv())
+        for ch in range(TOKEN_CHUNKS):
+            self.over_own[ch].wait_recv()
+            for j in range(last):
+                pl.when(z - 1 - j >= 0)(lambda: self.over_ups[j][ch].wait_recv())
+                pl.when(z + 1 + j <= last)(lambda: self.over_downs[j][ch].wait_recv())
 
     def drain(self):
         z, last = self.place.z, self.last
         self.first.wait_send()
-        self.over_own.wait_send()
-        for j in range(last):
-            pl.when((z - j >= 0) & (z < last))(lambda: self.ups[j].wait_send())
-            pl.when((z + j <= last) & (z > 0))(lambda: self.downs[j].wait_send())
-            pl.when(z - 1 - j >= 0)(lambda: self.over_ups[j].wait_send())
-            pl.when(z + 1 + j <= last)(lambda: self.over_downs[j].wait_send())
+        for ch in range(TOKEN_CHUNKS):
+            self.over_own[ch].wait_send()
+            for j in range(last):
+                pl.when((z - j >= 0) & (z < last))(lambda: self.ups[j][ch].wait_send())
+                pl.when((z + j <= last) & (z > 0))(lambda: self.downs[j][ch].wait_send())
+                pl.when(z - 1 - j >= 0)(lambda: self.over_ups[j][ch].wait_send())
+                pl.when(z + 1 + j <= last)(lambda: self.over_downs[j][ch].wait_send())
 
 
 class WeightGather:
@@ -585,79 +592,86 @@
 
 NORM_PARTS = 4
 GATHER_ORDER = (
+    "qkv 2",
+    "hid spread 0",
+    "qkv 4",
+    "up b 6",
+    "down a 0",
+    "qkv 0",
+    "cot spread 0",
+    "down b 0",
+    "hid 0 0",
+    "hid spread 1",
+    "hid 1 0",
+    "up a 0",
+    "hid 0 1",
+    "qkv 1",
+    "qkv 3",
+    "tables",
+    "small cross",
+    "qkv 5",
+    "up a 6",
+    "up b 2",
     "qkv 6",
-    "hid spread",
+    "hid 1 1",
+    "up a 2",
+    "up a 4",
+    "up b 5",
+    "small share",
+    "up b 4",
+    "up a 5",
+    "up b 3",
+    "down b 6",
+    "down a 5",
+    "out start",
+    "down b 1",
+    "up a 1",
+    "down b 5",
+    "qkv cross",
+    "hid 2 0",
+    "small done",
     "up b 0",
-    "up a 0",
-    "out start",
-    "qkv 1",
-    "qkv 0",
-    "tables",
-    "hid 0",
-    "small cross",
-    "up a 1",
-    "qkv 2",
-    "small share",
-    "down b 0",
-    "up b 5",
-    "up b 2",
-    "hid 1",
+    "hid 2 1",
+    "up b 1",
+    "cot spread 1",
+    "hid done",
+    "cot 0 0",
+    "cot 0 1",
+    "up b cross",
+    "norm",
+    "qkv share",
+    "down b 4",
     "up a 3",
-    "small done",
-    "up a 5",
-    "out share",
-    "qkv 5",
-    "cot spread",
-    "qkv 3",
-    "qkv 4",
-    "up a 4",
-    "qkv cross",
-    "hid 2",
-    "down a 0",
-    "up a 6",
-    "up a 2",
-    "up b 1",
-    "up b 3",
-    "cot 0",
+    "norm",
+    "cot 1 0",
+    "norm",
     "up a cross",
-    "hid done",
-    "norm",
-    "up b 4",
-    "up b 6",
-    "qkv share",
-    "norm",
-    "down a 2",
-    "cot 1",
-    "down a 1",
-    "down a 4",
-    "up b cross",
-    "down a 5",
-    "norm",
+    "down b 2",
     "norm",
     "norm done",
+    "cot 1 1",
+    "up b share",
+    "project",
+    "down b 3",
+    "cot 2 0",
+    "down a 1",
+    "attend",
+    "down a 2",
     "up a share",
-    "project",
+    "down b cross",
+    "out share",
     "down a 6",
     "down a 3",
-    "cot 2",
-    "up b share",
-    "attend",
+    "cot 2 1",
+    "down a 4",
+    "inner",
     "down a cross",
-    "down b 3",
-    "down b 2",
-    "down b 5",
-    "inner",
-    "down b 4",
-    "down b 6",
-    "down b 1",
     "cot done",
-    "out grads",
-    "down b cross",
     "down grads",
+    "attended grads",
+    "down b share",
+    "down a share",
     "attention back",
-    "down a share",
-    "down b share",
-    "qkv grads",
 )
 
 
@@ -856,17 +870,13 @@
         slope[at, :] = normal + inner * density
 
 
-def attended_grads(cot, weight, attended_low, attended_grad, weight_grad):
-    @pl.loop(0, cot.shape[0] // 256)
+def attended_grads(cot, weight, attended_grad):
+    step = 256
+
+    @pl.loop(0, cot.shape[0] // step)
     def _(i):
-        at = tile(i, 256)
+        at = tile(i, step)
         attended_grad[at, :] = contract_cols(cot[at, :], flat_rows(weight[...])).astype(jnp.bfloat16)
-
-    @pl.loop(0, cot.shape[1] // 512)
-    def _(i):
-        at = tile(i, 512)
-        grad = contract_rows(attended_low[...], cot[:, at]).astype(jnp.bfloat16)
-        weight_grad[:, :, at] = grad.reshape(weight_grad.shape[0], weight_grad.shape[1], 512)
 
 
 def attention_grads(
@@ -946,13 +956,10 @@
     norm_two_out,
     activated_out,
     slope_out,
-    qkv_grad_out,
+    norm_one_out,
     down_grad_out,
-    out_grad_out,
     vec_out,
     stats_out,
-    qkv_sum_out,
-    cot_sum_out,
     hid_rows,
     cot_rows,
     hid,
@@ -994,9 +1001,6 @@
     attended_grad,
     score_grad,
     projected_grad,
-    out_grad,
-    qkv_sum,
-    cot_sum,
     send,
     recv,
     local,
@@ -1062,12 +1066,9 @@
             ("norm_two", norm_two, norm_two_out),
             ("activated", activated, activated_out),
             ("slope", slope, slope_out),
-            ("out_grad", out_grad, out_grad_out),
             ("projected_grad", projected_grad, projected_grad_out),
-            ("qkv_grad", qkv_v, qkv_grad_out),
+            ("norm_one", norm_one, norm_one_out),
             ("down_grad", up_v, down_grad_out),
-            ("qkv_sum", qkv_sum, qkv_sum_out),
-            ("cot_sum", cot_sum, cot_sum_out),
         )
     }
 
@@ -1083,6 +1084,7 @@
         norm_rows(next(normed) * part_rows, part_rows, hid_v, vec, norm_one, norm_two, stats)
 
     def norm_done():
+        stores["norm_one"].start()
         stores["norm_two"].start()
         stores["stats"].start()
 
@@ -1130,14 +1132,11 @@
         loads["cot"].wait()
 
     def out_grads():
-        attended_grads(cot_v, out_v, attended_low, attended_grad, out_grad)
-        stores["out_grad"].start()
+        attended_grads(cot_v, out_v, attended_grad)
 
     def down_grads():
         weight_grads(cot_v, activated, up_v)
         stores["down_grad"].start()
-        column_sums(cot_v, cot_sum)
-        stores["cot_sum"].start()
 
     def attention_back():
         attention_grads(
@@ -1145,16 +1144,8 @@
         )
         stores["projected_grad"].start()
 
-    def qkv_grads():
-        weight_grads(norm_one, projected_grad, qkv_v)
-        stores["qkv_grad"].start()
-        column_sums(projected_grad, qkv_sum)
-        stores["qkv_sum"].start()
-
     steps = {
         "tables": lambda: position_tables(ctx_count, pairing, cosine, sine, key_pos),
-        "hid spread": hid_g.spread,
-        "cot spread": cot_g.spread,
         "small cross": small_g.cross,
         "small share": small_g.share,
         "small done": small_done,
@@ -1167,14 +1158,15 @@
         "attend": attend_all,
         "inner": inner_all,
         "cot done": cot_done,
-        "out grads": out_grads,
+        "attended grads": out_grads,
         "down grads": down_grads,
         "attention back": attention_back,
-        "qkv grads": qkv_grads,
     }
-    for j in range(place.line - 1):
-        steps["hid %d" % j] = functools.partial(hid_g.step, j)
-        steps["cot %d" % j] = functools.partial(cot_g.step, j)
+    for ch in range(TOKEN_CHUNKS):
+        for name, gather in (("hid", hid_g), ("cot", cot_g)):
+            steps["%s spread %d" % (name, ch)] = functools.partial(gather.spread, ch)
+            for j in range(place.line - 1):
+                steps["%s %d %d" % (name, j, ch)] = functools.partial(gather.step, j, ch)
     for name, gather in weights.items():
         for i in range(len(gather.by_chip)):
             steps["%s %d" % (name, i)] = functools.partial(gather.send, i)
@@ -1250,13 +1242,10 @@
         wide_s,
         ((tokens, part), b16),
         ((tokens, part), f32),
-        qkv_s,
+        wide_s,
         part_s,
-        out_s,
         ((8, width), f32),
         ((tokens, LANES), f32),
-        ((8, head3), f32),
-        ((8, width), f32),
     ]
     scratch = [
         (hid.shape, b16),
@@ -1295,9 +1284,6 @@
         narrow_s,
         ((tokens, tokens), b16),
         ((tokens, head3), b16),
-        out_s,
-        ((8, head3), f32),
-        ((8, width), f32),
     ]
     operands = (hid, cot, *vectors, qkv, up, down, out, pairing)
     anywhere = pl.BlockSpec(memory_space=pl.ANY)
@@ -1308,8 +1294,8 @@
         out_specs=[anywhere] * len(results),
         scratch_shapes=[pltpu.VMEM(*shape) for shape in scratch]
         + [
-            pltpu.SemaphoreType.DMA((112,)),
-            pltpu.SemaphoreType.DMA((112,)),
+            pltpu.SemaphoreType.DMA((160,)),
+            pltpu.SemaphoreType.DMA((160,)),
             pltpu.SemaphoreType.DMA((48,)),
         ],
         compiler_params=pltpu.CompilerParams(
@@ -1319,24 +1305,14 @@
     )(*operands)
 
 
-def add_rows(total, other, count):
+def add_rows(total, other):
     step = 16
-    per = total.shape[-2] // step
-
-    @pl.loop(0, count * per)
+
+    @pl.loop(0, total.shape[0] // step)
     def _(i):
-        k, at = i // per, tile(i % per, step)
-        both = total[k, at, :].astype(jnp.float32) + other[k, at, :].astype(jnp.float32)
-        total[k, at, :] = both.astype(total.dtype)
-
-
-def add_tiles(total, other, pieces):
-    rows = total.shape[-2]
-
-    @pl.loop(0, pieces)
-    def _(k):
-        both = total[k].astype(jnp.float32) + other[k].astype(jnp.float32)
-        total[k] = both.astype(total.dtype)
+        at = tile(i, step)
+        both = total[at, :].astype(jnp.float32) + other[at, :].astype(jnp.float32)
+        total[at, :] = both.astype(total.dtype)
 
 
 class GradScatter:
@@ -1400,9 +1376,21 @@
         for copy in self.scattered:
             copy.wait_recv()
 
-    def drain(self):
-        for copy in self.scattered + [self.swap, self.across]:
+    def drain(self, swapped=False):
+        for copy in self.scattered + [self.across] + ([] if swapped else [self.swap]):
             copy.wait_send()
+
+
+def out_weight_grads(place, attended_low, cot, kept, given):
+    step = 512
+
+    @pl.loop(0, cot.shape[1] // step)
+    def _(i):
+        at = tile(i, step)
+        grad = contract_rows(attended_low[...], cot[:, at]).astype(jnp.bfloat16)
+        grad = grad.reshape((2,) + kept.shape[:2] + (step,))
+        kept[:, :, at] = jnp.where(place.c == 0, grad[0], grad[1])
+        given[:, :, at] = jnp.where(place.c == 0, grad[1], grad[0])
 
 
 def weight_grads_by_core(place, tokens, grads, kept, given, columns):
@@ -1419,91 +1407,100 @@
 
 class TokenScatter:
     def __init__(self, place, copies, part, from_y, slots, total, result):
-        self.place = place
+        self.place, self.copies = place, copies
         z, y, c, x = place.z, place.y, place.c, place.x
         self.part, self.from_y, self.slots, self.total = part, from_y, slots, total
         self.line = place.line
-        last = self.line - 1
-        self.last = last
-        self.copies = copies
-        self.over_base = copies.reserve(self.line)
-        self.up_base = copies.reserve(self.line)
-        self.down_base = copies.reserve(self.line)
+        self.last = last = self.line - 1
+        self.rows = total.shape[0]
+        self.size = self.rows // TOKEN_CHUNKS
+        count = self.line * TOKEN_CHUNKS
+        self.over_base = copies.reserve(count)
+        self.up_base = copies.reserve(count)
+        self.down_base = copies.reserve(count)
         self.above = place.at(jnp.minimum(z + 1, last), y, c, x)
         self.below = place.at(jnp.maximum(z - 1, 0), y, c, x)
-        self.swap = copies.remote(total.at[1 - c], result.at[c], place.other_core())
-        self.own = copies.inside(total.at[c], result.at[c])
+        half = self.rows // CORES
+        self.swap = copies.remote(total.at[tile(1 - c, half)], result.at[c], place.other_core())
+        self.own = copies.inside(total.at[tile(c, half)], result.at[c])
 
     def order(self, i):
         last = self.last
-        chunk = 0
+        chosen = 0
         for z in range(self.line):
             far = sorted(range(self.line), key=lambda k: (-abs(k - z), min(k, last - k)))
-            chunk = jnp.where(self.place.z == z, far[i], chunk)
-        return chunk
-
-    def over(self, k):
-        y = self.place.y
-        return self.copies.remote_at(
-            self.over_base + k, self.part.at[k, 1 - y], self.from_y.at[k], self.place.other_y()
-        )
-
-    def up(self, k):
-        return self.copies.remote_at(
-            self.up_base + k, self.part.at[k, self.place.y], self.slots.at[k], self.above
-        )
-
-    def down(self, k):
+            chosen = jnp.where(self.place.z == z, far[i], chosen)
+        return chosen
+
+    def chunk(self, ref, k, ch):
+        return ref.at[tile(k * TOKEN_CHUNKS + ch, self.size)]
+
+    def held(self, k, ch):
+        return self.chunk(self.part, k * LINE_Y + self.place.y, ch)
+
+    def copy(self, base, k, ch, src, dst, device):
+        return self.copies.remote_at(base + k * TOKEN_CHUNKS + ch, src, dst, device)
+
+    def over(self, k, ch):
+        src = self.chunk(self.part, k * LINE_Y + 1 - self.place.y, ch)
+        return self.copy(self.over_base, k, ch, src, self.chunk(self.from_y, k, ch), self.place.other_y())
+
+    def up(self, k, ch):
+        return self.copy(self.up_base, k, ch, self.held(k, ch), self.chunk(self.slots, k, ch), self.above)
+
+    def down(self, k, ch):
         slot = jnp.where(self.place.z - 1 == k, self.line, k)
-        return self.copies.remote_at(
-            self.down_base + k, self.part.at[k, self.place.y], self.slots.at[slot], self.below
-        )
-
-    def combine(self, k):
-        self.over(k).wait_recv()
-        add_rows(self.part.at[k, self.place.y], self.from_y.at[k], CORES)
-
-    def step(self, i):
-        z, y = self.place.z, self.place.y
+        return self.copy(self.down_base, k, ch, self.held(k, ch), self.chunk(self.slots, slot, ch), self.below)
+
+    def send_over(self, k):
+        for ch in range(TOKEN_CHUNKS):
+            self.over(k, ch).start()
+
+    def combine(self, k, ch):
+        self.over(k, ch).wait_recv()
+        add_rows(self.held(k, ch), self.chunk(self.from_y, k, ch))
+
+    def step(self, i, ch):
+        z = self.place.z
         k = self.order(i)
-        self.combine(k)
+        self.combine(k, ch)
 
         @pl.when(k > z)
         def _():
             @pl.when(z > 0)
             def _():
-                self.up(k).wait_recv()
-                add_rows(self.part.at[k, y], self.slots.at[k], CORES)
-
-            self.up(k).start()
+                self.up(k, ch).wait_recv()
+                add_rows(self.held(k, ch), self.chunk(self.slots, k, ch))
+
+            self.up(k, ch).start()
 
         @pl.when(k < z)
         def _():
             @pl.when(z < self.last)
             def _():
-                self.down(k).wait_recv()
-                add_rows(self.part.at[k, y], self.slots.at[k], CORES)
-
-            self.down(k).start()
+                self.down(k, ch).wait_recv()
+                add_rows(self.held(k, ch), self.chunk(self.slots, k, ch))
+
+            self.down(k, ch).start()
 
     def reduce(self):
         z, y, last = self.place.z, self.place.y, self.last
-        self.combine(z)
-        pl.when(z > 0)(lambda: self.up(z).wait_recv())
-        pl.when(z < last)(lambda: self.down(z).wait_recv())
         step = 16
-        per = self.total.shape[1] // step
-
-        @pl.loop(0, CORES * per)
+        for ch in range(TOKEN_CHUNKS):
+            self.combine(z, ch)
+            pl.when(z > 0)(lambda: self.up(z, ch).wait_recv())
+            pl.when(z < last)(lambda: self.down(z, ch).wait_recv())
+
+        @pl.loop(0, self.rows // step)
         def _(i):
-            k, at = i // per, tile(i % per, step)
-            self.total[k, at, :] = self.part[z, y, k, at, :].astype(jnp.float32)
+            at = tile((z * LINE_Y + y) * (self.rows // step) + i, step)
+            self.total[tile(i, step), :] = self.part[at, :].astype(jnp.float32)
 
         def add(slot):
-            @pl.loop(0, CORES * per)
+            @pl.loop(0, self.rows // step)
             def _(i):
-                k, at = i // per, tile(i % per, step)
-                self.total[k, at, :] += self.slots[slot, k, at, :].astype(jnp.float32)
+                at = tile(slot * (self.rows // step) + i, step)
+                self.total[tile(i, step), :] += self.slots[at, :].astype(jnp.float32)
 
         pl.when(z > 0)(lambda: add(z))
         pl.when(z < last)(lambda: add(last + 1))
@@ -1514,22 +1511,21 @@
         self.swap.wait_recv()
 
     def drain(self):
-        z, last = self.place.z, self.last
+        z = self.place.z
         for k in range(self.line):
-            self.over(k).wait_send()
-            pl.when(z < k)(lambda: self.up(k).wait_send())
-            pl.when(z > k)(lambda: self.down(k).wait_send())
+            for ch in range(TOKEN_CHUNKS):
+                self.over(k, ch).wait_send()
+                pl.when(z < k)(lambda: self.up(k, ch).wait_send())
+                pl.when(z > k)(lambda: self.down(k, ch).wait_send())
 
 
 def output_part(scatter, i, attended_low, activated, out_weight, down_weight):
     k = scatter.order(i)
-    part = scatter.part
-    size = part.shape[1] * part.shape[2] * part.shape[3]
-    at = tile(k, size)
+    at = tile(k, LINE_Y * scatter.rows)
     rows = nn(attended_low[at, :], flat_rows(out_weight[...]))
     rows = rows + contract_cols(activated[at, :], flat_rows(down_weight[...]))
-    part[k] = rows.astype(part.dtype).reshape(part.shape[1:])
-    scatter.over(k).start()
+    scatter.part[at, :] = rows.astype(scatter.part.dtype)
+    scatter.send_over(k)
 
 
 def inner_grads(cot, down_weight, slope, slope_loads, inner_grad):
@@ -1548,12 +1544,10 @@
         return jnp.sum(values.reshape(-1, 8, values.shape[1]), axis=0)
 
     k = scatter.order(i)
-    part = scatter.part
-    size = part.shape[2] * part.shape[3]
 
     @pl.loop(0, LINE_Y)
     def _(y):
-        at = tile(k * LINE_Y + y, size)
+        at = tile(k * LINE_Y + y, scatter.rows)
         one = contract_cols(projected_grad[at, :], flat_rows(qkv_weight[...]))
         two = contract_cols(inner_grad[at, :], flat_rows(up_weight[...]))
         xhat = (hid[at, :].astype(jnp.float32) - stats[at, 0:1]) * stats[at, 1:2]
@@ -1562,9 +1556,9 @@
         sums[2] += by_eight(two * xhat)
         sums[3] += by_eight(two)
         rows = one * vec[0:1, :] + two * vec[2:3, :]
-        part[k, y] = rows.astype(part.dtype).reshape(part.shape[2:])
-
-    scatter.over(k).start()
+        scatter.part[at, :] = rows.astype(scatter.part.dtype)
+
+    scatter.send_over(k)
 
 
 COT_SUM, UP_SUM, QKV_SUM = 4, 5, 7
@@ -1599,47 +1593,55 @@
 
 
 SCATTER_ORDER = (
+    "down a swap",
     "outs tile 0",
-    "qkv swap",
-    "down a swap",
-    "down b swap",
-    "out swap",
     "outs tile 1",
-    "qkv cross",
+    "qkv grads",
+    "outs 0 0",
     "down a cross",
     "outs tile 2",
+    "down b swap",
+    "outs 0 1",
+    "out grads",
+    "outs 1 0",
+    "down b cross",
+    "qkv swap",
+    "down a scatter",
     "outs tile 3",
-    "outs 0",
+    "out swap",
     "inner",
-    "down b cross",
+    "outs 1 1",
+    "outs 2 0",
+    "qkv cross",
     "up a grad",
+    "down b scatter",
+    "up b grad",
+    "hid tile 0",
+    "up b swap",
+    "outs 2 1",
+    "out cross",
+    "hid tile 1",
+    "hid tile 2",
     "qkv scatter",
+    "hid 0 0",
+    "up a swap",
+    "up b cross",
     "up sum",
-    "up b grad",
-    "outs 1",
-    "outs 2",
-    "up a swap",
-    "hid tile 0",
-    "hid tile 1",
-    "up b swap",
-    "down b scatter",
-    "hid tile 2",
-    "down a scatter",
+    "hid 0 1",
     "hid tile 3",
-    "out cross",
-    "up b cross",
     "pack",
-    "hid 0",
+    "hid 1 0",
     "small swap",
-    "hid 1",
+    "out finish",
     "small cross",
     "up b scatter",
+    "hid 1 1",
+    "hid 2 0",
+    "outs reduce",
+    "up a cross",
+    "hid 2 1",
     "small scatter",
-    "up a cross",
-    "out finish",
-    "hid 2",
     "up a scatter",
-    "outs reduce",
     "hid reduce",
 )
 
@@ -1659,11 +1661,8 @@
     slope_in,
     stats_in,
     vec_in,
-    qkv_sum_in,
-    cot_sum_in,
-    qkv_grad,
+    norm_one_in,
     down_grad,
-    out_grad,
     small_result,
     qkv_result,
     up_result,
@@ -1709,6 +1708,7 @@
     hid_from_y,
     hid_slots,
     total,
+    out_given,
     send,
     recv,
     local,
@@ -1716,10 +1716,11 @@
     place = Place(ctx_count)
     copies = Copies(send, recv, local)
     c, x = place.c, place.x
+    qkv_given = up_kept.at[:, :, :, : qkv_kept.shape[3]]
     half = up_kept.shape[3] // 2
     halves = {" a": slice(0, half), " b": slice(half, 2 * half)}
     grads = {
-        "qkv": GradScatter(place, copies, qkv_grad, qkv_kept, qkv_core, qkv_plane, qkv_result),
+        "qkv": GradScatter(place, copies, qkv_given, qkv_kept, qkv_core, qkv_plane, qkv_result),
         "small": GradScatter(place, copies, tiles, small_kept, small_core, small_plane, small_result),
     }
     for name, cols in halves.items():
@@ -1729,8 +1730,7 @@
         grads["up" + name] = GradScatter(place, copies, down_core, up_kept, up_core, up_plane, up_result, cols)
     outs_s = TokenScatter(place, copies, out_part, out_from_y, out_slots, total, out_result)
     hid_s = TokenScatter(place, copies, hid_part, hid_from_y, hid_slots, total, hid_result)
-    out_load = copies.inside(out_grad.at[pl.ds(2 * c, 2)], out_kept)
-    out_swap = copies.remote(out_grad.at[pl.ds(2 * (1 - c), 2)], out_core, place.other_core())
+    out_swap = copies.remote(out_given, out_core, place.other_core())
     out_across = copies.remote(out_kept.at[1 - x], out_plane, place.other_plane())
     out_own = copies.inside(out_kept.at[x], out_grad_result)
     loads = {
@@ -1746,19 +1746,17 @@
             ("projected_grad", projected_grad_in, projected_grad),
             ("stats", stats_in, stats),
             ("vec", vec_in, vec),
-            ("qkv_sum", qkv_sum_in, qkv_sum),
-            ("cot_sum", cot_sum_in, cot_sum),
+            ("norm_one", norm_one_in, wide),
             ("up", up_in, weight),
             ("hid", hid_in, wide),
         )
     }
-    early = ("activated", "attended_low", "out", "down", "cot", "qkv", "projected_grad")
-    early += ("stats", "vec", "qkv_sum", "cot_sum")
+    early = ("activated", "attended_low", "out", "down", "projected_grad", "norm_one", "qkv", "stats", "vec")
 
     def out_cross():
-        out_load.wait()
         out_swap.wait_recv()
-        add_rows(out_kept, out_core, 2)
+        for k in range(2):
+            add_rows(out_kept.at[k], out_core.at[k])
         out_across.start()
 
     def out_finish():
@@ -1795,7 +1793,21 @@
         loads["up"].start()
         loads["norm_two"].start()
 
+    def qkv_grads():
+        need("projected_grad", "norm_one")
+        columns = slice(0, qkv_kept.shape[3])
+        weight_grads_by_core(place, wide, projected_grad, qkv_kept, qkv_given, columns)
+        loads["cot"].start()
+        column_sums(projected_grad, qkv_sum)
+
+    def out_grads():
+        need("attended_low", "cot")
+        out_weight_grads(place, attended_low, wide, out_kept, out_given)
+        column_sums(wide, cot_sum)
+
     def up_half(name, last):
+        if not last:
+            grads["qkv"].swap.wait_send()
         need("norm_two")
         weight_grads_by_core(place, wide, act, up_kept, down_core, halves[name])
         if last:
@@ -1808,12 +1820,7 @@
         hidden_part(hid_s, i, act, weight, projected_grad, qkv_weight, wide, stats, vec, sums)
 
     def pack():
-        need("qkv_sum", "cot_sum")
         pack_small(place, sums, cot_sum, up_sum, qkv_sum, qkv_rows, tiles)
-
-    def out_start():
-        out_load.start()
-        out_swap.start()
 
     def hidden_reduce():
         outs_s.own.wait()
@@ -1821,7 +1828,9 @@
         hid_s.reduce()
 
     steps = {
-        "out swap": out_start,
+        "qkv grads": qkv_grads,
+        "out grads": out_grads,
+        "out swap": out_swap.start,
         "out cross": out_cross,
         "out finish": out_finish,
         "inner": inner_all,
@@ -1840,8 +1849,9 @@
         steps["outs tile %d" % i] = functools.partial(output_tile, i)
         steps["hid tile %d" % i] = functools.partial(hidden_tile, i)
     for j in range(outs_s.last):
-        steps["outs %d" % j] = functools.partial(outs_s.step, j)
-        steps["hid %d" % j] = functools.partial(hid_s.step, j)
+        for ch in range(TOKEN_CHUNKS):
+            steps["outs %d %d" % (j, ch)] = functools.partial(outs_s.step, j, ch)
+            steps["hid %d %d" % (j, ch)] = functools.partial(hid_s.step, j, ch)
 
     for name in early:
         loads[name].start()
@@ -1850,14 +1860,15 @@
     greet(place)()
     for name in SCATTER_ORDER:
         steps[name]()
-    scatters = list(grads.values()) + [outs_s, hid_s]
-    for scatter in scatters:
+    for scatter in list(grads.values()) + [outs_s, hid_s]:
         scatter.finish()
     out_own.wait()
     hid_s.own.wait()
     hid_s.swap.wait_send()
-    for scatter in scatters:
-        scatter.drain()
+    for name, scatter in grads.items():
+        scatter.drain(name == "qkv")
+    outs_s.drain()
+    hid_s.drain()
     out_swap.wait_send()
     out_across.wait_send()
 
@@ -1901,13 +1912,14 @@
     for shape, dtype in ((small, f32), ((rows, head3), b16), ((rows, part), b16), ((rows, part), b16)):
         scratch += [((chips, 2) + shape, dtype)] * 2 + [((chips,) + shape, dtype)]
     scratch += [((2, rows, width), b16)] * 2 + [((rows, width), b16)]
+    chip_rows = CORES * local_rows
     for _ in range(2):
         scratch += [
-            ((line, LINE_Y) + token, b16),
-            ((line,) + token, b16),
-            ((line + 1,) + token, b16),
+            ((tokens, width), b16),
+            ((line * chip_rows, width), b16),
+            (((line + 1) * chip_rows, width), b16),
         ]
-    scratch += [(token, f32)]
+    scratch += [((chip_rows, width), f32), ((2, rows, width), b16)]
     anywhere = pl.BlockSpec(memory_space=pl.ANY)
     return pl.pallas_call(
         lambda *refs: scatter_kernel(ctx_count, *refs),
@@ -1916,8 +1928,8 @@
         out_specs=[anywhere] * len(results),
         scratch_shapes=[pltpu.VMEM(*shape) for shape in scratch]
         + [
-            pltpu.SemaphoreType.DMA((96,)),
-            pltpu.SemaphoreType.DMA((96,)),
+            pltpu.SemaphoreType.DMA((128,)),
+            pltpu.SemaphoreType.DMA((128,)),
             pltpu.SemaphoreType.DMA((48,)),
         ],
         compiler_params=pltpu.CompilerParams(
@@ -2100,13 +2112,10 @@
         norm_two,
         activated,
         slope,
-        grad_qkv,
+        norm_one,
         grad_down,
-        grad_out,
         vec,
         stats,
-        qkv_sum,
-        cot_sum,
     ) = gather_all(
         ctx_count,
         hidden,
@@ -2135,11 +2144,8 @@
             slope,
             stats,
             vec,
-            qkv_sum,
-            cot_sum,
-            grad_qkv,
+            norm_one,
             grad_down,
-            grad_out,
         ),
     )
     (

time: 316 us -> 303 us (0.959)
  Pallas kernels: 314 us -> 300 us
    pallas_call x1, Pallas kernels: 146 us -> 138 us  [scatter_all(): pl.pallas_call(lambda *refs: scatter_kernel(ctx_count, *refs), out_shape=...]
    pallas_call x1, Pallas kernels: 158 us -> 152 us  [gather_all(): pl.pallas_call(lambda *refs: gather_kernel(ctx_count, *refs), out_shape=[...]
where the time goes in v5:
time: 303 us; the launch traced here: 301 us
  Pallas kernels  300 us (99%)
    pallas_call x1, Pallas kernels, gather_all(): pl.pallas_call(lambda *refs: gather_kernel(ctx_count, *refs), out_shape=[...  152 us
    pallas_call x1, Pallas kernels, scatter_all(): pl.pallas_call(lambda *refs: scatter_kernel(ctx_count, *refs), out_shape=...  138 us
    pallas_call x1, Pallas kernels, finish_all(): pl.pallas_call(finish_kernel, out_shape=[jax.ShapeDtypeStruct((n,), f32)...  10.2 us

profile of v5, /device:TPU:9, one launch (start us, length us, event | category | flops | bytes accessed | tf_op | source)
XLA Modules:
  0.0 301.1 jit_solution(12313386996985336011)
XLA Ops:
  0.7 151.6 %gather_all.1 = (bf16[1024,2048]{1,0:T(8,128)(2,1)}, bf16[1024,2048]{1,0:T(8,128)(2,1)}, bf16[8,4,64,768]{3,2,1,0:T(8,128)(2,1)}, bf16[8,4,64,1024]{3,2,1,0:T(8,...) custom-call(bf16[64,2,2048]{2,1,0:T(2,128)(2,1)} %hidden_in.1, ...), custom_call_target="tpu_custom_call" | custom-call | tf_op jit(solution)/shard_map/gather_all/pallas_call | solution.py:1290
  152.2 138.4 %scatter_all.1 = (f32[8,16,128]{2,1,0:T(8,128)}, bf16[8,64,768]{2,1,0:T(8,128)(2,1)}, bf16[8,64,1024]{2,1,0:T(8,128)(2,1)}, bf16[8,64,1024]{2,1,0:T(8,128)(2,1)}...) custom-call(bf16[1024,2048]{1,0:T(8,128)(2,1)} %get-tuple-element.50.refs_0_, ...), custom_call_target="tpu_custom_call" | custom-call | tf_op jit(solution)/shard_map/scatter_all/pallas_call | solution.py:1924
  290.6 10.2 %finish_all.1 = (f32[64]{0:T(128)}, f32[64]{0:T(128)}, f32[192]{0:T(256)}, f32[64]{0:T(128)}, f32[64]{0:T(128)}, /*index=5*/f32[64]{0:T(128)}, f32[256]{0:T(256)...) custom-call(bf16[8,64,768]{2,1,0:T(8,128)(2,1)} %get-tuple-element.6, ...), custom_call_target="tpu_custom_call" | custom-call | tf_op jit(solution)/shard_map/finish_all/pallas_call | solution.py:2070

commit v6 on v5

--- a/solution.py
+++ b/solution.py
@@ -464,7 +464,7 @@
         partners.append(place.at(z, y, place.c, place.x))
     for partner in partners:
         pl.semaphore_signal(barrier, inc=1, device_id=partner, device_id_type=MESH)
-    return lambda: pl.semaphore_wait(barrier, len(partners))
+    pl.semaphore_wait(barrier, len(partners))
 
 
 TOKEN_CHUNKS = 2
@@ -590,88 +590,90 @@
             copy.wait_send()
 
 
-NORM_PARTS = 4
+NORM_PARTS = 2
+DOWN_PARTS = "ab"
 GATHER_ORDER = (
+    "qkv 6",
+    "up a 0",
+    "up a 3",
+    "qkv 0",
+    "up b 2",
+    "prepare hid",
+    "up b 0",
+    "small scatter",
+    "hid spread 0",
+    "qkv 5",
+    "tables",
     "qkv 2",
-    "hid spread 0",
+    "small cross",
+    "hid spread 1",
+    "prepare cot",
+    "hid 0 0",
+    "hid 0 1",
+    "small share",
+    "up a 2",
+    "down a 0",
+    "out start",
+    "hid 1 0",
+    "small done",
+    "up b 6",
+    "down b 5",
+    "qkv 1",
+    "down a 3",
+    "qkv 3",
+    "up b 1",
+    "hid 1 1",
+    "hid 2 0",
     "qkv 4",
-    "up b 6",
-    "down a 0",
-    "qkv 0",
+    "up a 4",
+    "up b 3",
     "cot spread 0",
-    "down b 0",
-    "hid 0 0",
-    "hid spread 1",
-    "hid 1 0",
-    "up a 0",
-    "hid 0 1",
-    "qkv 1",
-    "qkv 3",
-    "tables",
-    "small cross",
-    "qkv 5",
+    "qkv cross",
+    "down a 1",
+    "hid 2 1",
+    "down a 6",
+    "up b 4",
+    "up b 5",
+    "down a 5",
+    "down a 4",
+    "cot 0 0",
+    "up b cross",
+    "hid done",
+    "up a 5",
+    "up a 1",
     "up a 6",
-    "up b 2",
-    "qkv 6",
-    "hid 1 1",
-    "up a 2",
-    "up a 4",
-    "up b 5",
-    "small share",
-    "up b 4",
-    "up a 5",
-    "up b 3",
-    "down b 6",
-    "down a 5",
-    "out start",
-    "down b 1",
-    "up a 1",
-    "down b 5",
-    "qkv cross",
-    "hid 2 0",
-    "small done",
-    "up b 0",
-    "hid 2 1",
-    "up b 1",
-    "cot spread 1",
-    "hid done",
-    "cot 0 0",
-    "cot 0 1",
-    "up b cross",
     "norm",
     "qkv share",
-    "down b 4",
-    "up a 3",
-    "norm",
+    "out share",
+    "cot spread 1",
     "cot 1 0",
     "norm",
+    "norm done",
     "up a cross",
+    "cot 0 1",
+    "down a 2",
+    "down b 0",
+    "project",
+    "up a share",
+    "up b share",
+    "down b 4",
+    "down b 6",
+    "down b 1",
+    "cot 2 0",
+    "down a cross",
+    "attend",
+    "cot 1 1",
     "down b 2",
-    "norm",
-    "norm done",
-    "cot 1 1",
-    "up b share",
-    "project",
     "down b 3",
-    "cot 2 0",
-    "down a 1",
-    "attend",
-    "down a 2",
-    "up a share",
+    "inner",
+    "down a share",
+    "cot 2 1",
     "down b cross",
-    "out share",
-    "down a 6",
-    "down a 3",
-    "cot 2 1",
-    "down a 4",
-    "inner",
-    "down a cross",
     "cot done",
+    "attended grads",
+    "attention back",
+    "down b share",
     "down grads",
-    "attended grads",
-    "down b share",
-    "down a share",
-    "attention back",
 )
 
 
@@ -795,7 +797,7 @@
 
 
 def norm_rows(start, count, hid, vec, norm_one, norm_two, stats):
-    step = 16
+    step = 128
 
     @pl.loop(0, count // step)
     def _(i):
@@ -918,13 +920,13 @@
 
 
 def column_sums(values, result):
-    step = 16
-
-    def add(i, total):
-        return total + values[tile(i, step), :].astype(jnp.float32)
-
-    total = lax.fori_loop(0, values.shape[0] // step, add, jnp.zeros((step, values.shape[1]), jnp.float32))
-    result[0:1, :] = jnp.sum(total, axis=0, keepdims=True)
+    step = 128
+    result[...] = jnp.zeros_like(result)
+
+    @pl.loop(0, values.shape[0] // step)
+    def _(i):
+        part = values[tile(i, step), :].astype(jnp.float32)
+        result[...] += jnp.sum(part.reshape(-1, 8, values.shape[1]), axis=0)
 
 
 def gather_kernel(
@@ -1020,13 +1022,11 @@
             for k in range(3)
         ]
 
-    half = part // 2
-
-    def half_gather(source, whole, first):
-        columns = pl.ds(first, half)
+    def part_gather(source, whole, first, size):
+        columns = pl.ds(first, size)
 
         def pieces(to, row, group):
-            given = pl.ds(pl.multiple_of(to * part + first, half), half)
+            given = pl.ds(pl.multiple_of(to * part + first, size), size)
             return [(source.at[:, given], whole.at[row, group, :, columns])]
 
         return WeightGather(place, copies, pieces, whole, columns)
@@ -1036,9 +1036,10 @@
     small_g = WeightGather(place, copies, lambda to, row, group: [(small, small_all.at[row, group])], small_all)
     qkv_g = WeightGather(place, copies, qkv_pieces, qkv_all)
     weights = {"qkv": qkv_g}
-    for name, source, whole in (("up", up, up_all), ("down", down, down_all)):
-        weights[name + " a"] = half_gather(source, whole, 0)
-        weights[name + " b"] = half_gather(source, whole, half)
+    for name, source, whole, letters in (("up", up, up_all, "ab"), ("down", down, down_all, DOWN_PARTS)):
+        size = part // len(letters)
+        for i, letter in enumerate(letters):
+            weights[name + " " + letter] = part_gather(source, whole, i * size, size)
     group = 2 * place.c + place.x
     out_mine = copies.inside(out, out_all.at[group])
     out_across = copies.remote(out, out_all.at[group], place.other_plane())
@@ -1189,22 +1190,31 @@
     for load in vector_loads:
         load.start()
     loads["cot rows"].start()
-    answered = greet(place)
-    loads["hid rows"].wait()
-    split_sequences(hid_rows, hid)
-    for load in vector_loads:
-        load.wait()
-    pack_parameters(vectors, small)
-    answered()
-    hid_g.start()
-    small_g.scatter()
-    loads["cot rows"].wait()
-    split_sequences(cot_rows, cot)
-    cot_g.start()
+    greet(place)
+
+    def prepare_hid():
+        loads["hid rows"].wait()
+        split_sequences(hid_rows, hid)
+        hid_g.start()
+
+    def prepare_cot():
+        loads["cot rows"].wait()
+        split_sequences(cot_rows, cot)
+        cot_g.start()
+
+    def prepare_small():
+        for load in vector_loads:
+            load.wait()
+        pack_parameters(vectors, small)
+        small_g.scatter()
+
+    steps["prepare hid"] = prepare_hid
+    steps["prepare cot"] = prepare_cot
+    steps["small scatter"] = prepare_small
     for name in GATHER_ORDER:
         steps[name]()
-    weights["down a"].finish()
-    weights["down b"].finish()
+    for letter in DOWN_PARTS:
+        weights["down " + letter].finish()
     for store in stores.values():
         store.wait()
     for gather in [hid_g, cot_g, small_g] + list(weights.values()):
@@ -1294,8 +1304,8 @@
         out_specs=[anywhere] * len(results),
         scratch_shapes=[pltpu.VMEM(*shape) for shape in scratch]
         + [
-            pltpu.SemaphoreType.DMA((160,)),
-            pltpu.SemaphoreType.DMA((160,)),
+            pltpu.SemaphoreType.DMA((176,)),
+            pltpu.SemaphoreType.DMA((176,)),
             pltpu.SemaphoreType.DMA((48,)),
         ],
         compiler_params=pltpu.CompilerParams(
@@ -1306,7 +1316,7 @@
 
 
 def add_rows(total, other):
-    step = 16
+    step = 64
 
     @pl.loop(0, total.shape[0] // step)
     def _(i):
@@ -1355,15 +1365,12 @@
         self.add(x, self.from_core.at[:, x])
 
     def add(self, x, other):
-        step = 16
-        per = self.kept.shape[2] // step
         cols = self.columns
 
-        @pl.loop(0, self.kept.shape[0] * per)
-        def _(i):
-            k, at = i // per, tile(i % per, step)
-            both = self.kept[k, x, at, cols].astype(jnp.float32) + other[k, at, cols].astype(jnp.float32)
-            self.kept[k, x, at, cols] = both.astype(self.kept.dtype)
+        @pl.loop(0, self.kept.shape[0])
+        def _(k):
+            both = self.kept[k, x, :, cols].astype(jnp.float32) + other[k, :, cols].astype(jnp.float32)
+            self.kept[k, x, :, cols] = both.astype(self.kept.dtype)
 
     def scatter(self):
         self.across.wait_recv()
@@ -1485,7 +1492,7 @@
 
     def reduce(self):
         z, y, last = self.place.z, self.place.y, self.last
-        step = 16
+        step = 64
         for ch in range(TOKEN_CHUNKS):
             self.combine(z, ch)
             pl.when(z > 0)(lambda: self.up(z, ch).wait_recv())
@@ -1568,15 +1575,17 @@
     chips, groups = tiles.shape[:2]
     tiles[...] = jnp.zeros_like(tiles)
     qkv_rows[...] = jnp.zeros_like(qkv_rows)
+    qkv_total = jnp.sum(qkv_sum[...], axis=0, keepdims=True)
+    up_total = jnp.sum(up_sum[...], axis=0, keepdims=True)
     third = qkv_rows.shape[0] // 3
     per_head = HEAD // LANES
     for k in range(3):
         for u in range(per_head):
             at = (k * per_head + u) * LANES
-            qkv_rows[pl.ds(k * third + place.chip * per_head + u, 1), :] = qkv_sum[0:1, at : at + LANES]
+            qkv_rows[pl.ds(k * third + place.chip * per_head + u, 1), :] = qkv_total[:, at : at + LANES]
     first = jnp.where(place.chip == 0, 1.0, 0.0)
     norm_sums = [jnp.sum(sums[row], axis=0, keepdims=True) for row in range(4)]
-    norm_sums.append(cot_sum[0:1, :] * first)
+    norm_sums.append(jnp.sum(cot_sum[...], axis=0, keepdims=True) * first)
     for pair in range(chips * groups // 2):
         chip, group = pair // (groups // 2), pair % (groups // 2) * 2
         at = slice(pair * LANES, (pair + 1) * LANES)
@@ -1588,7 +1597,7 @@
         for u in range(2):
             at = (group * 2 + u) * LANES
             row = UP_SUM + u
-            values = up_sum[0:1, at : at + LANES].reshape(1, 1, LANES)
+            values = up_total[:, at : at + LANES].reshape(1, 1, LANES)
             tiles[pl.ds(place.chip, 1), group, row : row + 1, :] = values
 
 
@@ -1761,14 +1770,7 @@
 
     def out_finish():
         out_across.wait_recv()
-        step = 16
-
-        @pl.loop(0, out_plane.shape[0] // step)
-        def _(i):
-            at = tile(i, step)
-            both = out_kept[x, at, :].astype(jnp.float32) + out_plane[at, :].astype(jnp.float32)
-            out_kept[x, at, :] = both.astype(out_kept.dtype)
-
+        add_rows(out_kept.at[x], out_plane)
         out_own.start()
 
     step = slope.shape[1]
@@ -1857,7 +1859,7 @@
         loads[name].start()
     slope_loads[0].start()
     slope_loads[1].start()
-    greet(place)()
+    greet(place)
     for name in SCATTER_ORDER:
         steps[name]()
     for scatter in list(grads.values()) + [outs_s, hid_s]:
@@ -2026,7 +2028,7 @@
     for load in loads[4:]:
         load.wait()
     bias = vec[OUT_BIAS : OUT_BIAS + 1, :] + vec[DOWN_BIAS : DOWN_BIAS + 1, :]
-    step = 16
+    step = 32
 
     @pl.loop(0, hidden.shape[0] // step)
     def _(i):

time: 303 us -> 300 us (0.990)
    pallas_call x1, Pallas kernels: 152 us -> 149 us  [gather_all(): pl.pallas_call(lambda *refs: gather_kernel(ctx_count, *refs), out_shape=[...]
where the time goes in v6:
time: 300 us
  Pallas kernels  299 us (100%)
    pallas_call x1, Pallas kernels, gather_all(): pl.pallas_call(lambda *refs: gather_kernel(ctx_count, *refs), out_shape=[...  149 us
    pallas_call x1, Pallas kernels, scatter_all(): pl.pallas_call(lambda *refs: scatter_kernel(ctx_count, *refs), out_shape=...  140 us
    pallas_call x1, Pallas kernels, finish_all(): pl.pallas_call(finish_kernel, out_shape=[jax.ShapeDtypeStruct((n,), f32)...  10 us

profile of v6, /device:TPU:9, one launch (start us, length us, event | category | flops | bytes accessed | tf_op | source)
XLA Modules:
  0.0 299.7 jit_solution(13029433970415000716)
XLA Ops:
  0.7 148.5 %gather_all.1 = (bf16[1024,2048]{1,0:T(8,128)(2,1)}, bf16[1024,2048]{1,0:T(8,128)(2,1)}, bf16[8,4,64,768]{3,2,1,0:T(8,128)(2,1)}, bf16[8,4,64,1024]{3,2,1,0:T(8,...) custom-call(bf16[64,2,2048]{2,1,0:T(2,128)(2,1)} %hidden_in.1, ...), custom_call_target="tpu_custom_call" | custom-call | tf_op jit(solution)/shard_map/gather_all/pallas_call | solution.py:1300
  149.2 140.3 %scatter_all.1 = (f32[8,16,128]{2,1,0:T(8,128)}, bf16[8,64,768]{2,1,0:T(8,128)(2,1)}, bf16[8,64,1024]{2,1,0:T(8,128)(2,1)}, bf16[8,64,1024]{2,1,0:T(8,128)(2,1)}...) custom-call(bf16[1024,2048]{1,0:T(8,128)(2,1)} %get-tuple-element.50.refs_0_, ...), custom_call_target="tpu_custom_call" | custom-call | tf_op jit(solution)/shard_map/scatter_all/pallas_call | solution.py:1926
  289.4 10.0 %finish_all.1 = (f32[64]{0:T(128)}, f32[64]{0:T(128)}, f32[192]{0:T(256)}, f32[64]{0:T(128)}, f32[64]{0:T(128)}, /*index=5*/f32[64]{0:T(128)}, f32[256]{0:T(256)...) custom-call(bf16[8,64,768]{2,1,0:T(8,128)(2,1)} %get-tuple-element.6, ...), custom_call_target="tpu_custom_call" | custom-call | tf_op jit(solution)/shard_map/finish_all/pallas_call | solution.py:2072

commit v7 on v6

--- a/solution.py
+++ b/solution.py
@@ -952,7 +952,6 @@
     up_all,
     down_all,
     out_all,
-    small_all,
     attended_low_out,
     projected_grad_out,
     norm_two_out,
@@ -1017,7 +1016,7 @@
         return [
             (
                 qkv.at[:, pl.ds(pl.multiple_of(k * width + to * head, head), head)],
-                qkv_all.at[row, group, :, pl.ds(k * head, head)],
+                qkv_v.at[row, group, :, pl.ds(k * head, head)],
             )
             for k in range(3)
         ]
@@ -1031,36 +1030,35 @@
 
         return WeightGather(place, copies, pieces, whole, columns)
 
-    hid_g = TokenGather(place, copies, hid, hid_all)
-    cot_g = TokenGather(place, copies, cot, cot_all)
-    small_g = WeightGather(place, copies, lambda to, row, group: [(small, small_all.at[row, group])], small_all)
-    qkv_g = WeightGather(place, copies, qkv_pieces, qkv_all)
+    hid_g = TokenGather(place, copies, hid, hid_v)
+    cot_g = TokenGather(place, copies, cot, cot_v)
+    small_g = WeightGather(place, copies, lambda to, row, group: [(small, small_v.at[row, group])], small_v)
+    qkv_g = WeightGather(place, copies, qkv_pieces, qkv_v)
     weights = {"qkv": qkv_g}
-    for name, source, whole, letters in (("up", up, up_all, "ab"), ("down", down, down_all, DOWN_PARTS)):
+    for name, source, whole, letters in (("up", up, up_v, "ab"), ("down", down, down_all, DOWN_PARTS)):
         size = part // len(letters)
         for i, letter in enumerate(letters):
             weights[name + " " + letter] = part_gather(source, whole, i * size, size)
     group = 2 * place.c + place.x
-    out_mine = copies.inside(out, out_all.at[group])
-    out_across = copies.remote(out, out_all.at[group], place.other_plane())
-    out_pair = out_all.at[pl.ds(2 * place.c, 2)]
+    out_mine = copies.inside(out, out_v.at[group])
+    out_across = copies.remote(out, out_v.at[group], place.other_plane())
+    out_pair = out_v.at[pl.ds(2 * place.c, 2)]
     out_swap = copies.remote(out_pair, out_pair, place.other_core())
     loads = {
         name: copies.inside(src, dst)
         for name, src, dst in (
             ("hid rows", hid_in, hid_rows),
             ("cot rows", cot_in, cot_rows),
-            ("small", small_all, small_v),
-            ("hid", hid_all, hid_v),
-            ("cot", cot_all, cot_v),
-            ("qkv", qkv_all, qkv_v),
-            ("up", up_all, up_v),
-            ("out", out_all, out_v),
         )
     }
     stores = {
         name: copies.inside(src, dst)
         for name, src, dst in (
+            ("hid", hid_v, hid_all),
+            ("cot", cot_v, cot_all),
+            ("qkv", qkv_v, qkv_all),
+            ("up", up_v, up_all),
+            ("out", out_v, out_all),
             ("vec", vec, vec_out),
             ("stats", stats, stats_out),
             ("attended_low", attended_low, attended_low_out),
@@ -1073,10 +1071,6 @@
         )
     }
 
-    def fetch(name):
-        loads[name].start()
-        loads[name].wait()
-
     rows = hid_v.shape[0]
     normed = iter(range(NORM_PARTS))
 
@@ -1091,17 +1085,16 @@
 
     def small_done():
         small_g.finish()
-        fetch("small")
         assemble_small(place, small_v, vec, qkv_rows, qkv_bias, up_bias)
         stores["vec"].start()
 
     def hid_done():
         hid_g.finish()
-        fetch("hid")
+        stores["hid"].start()
 
     def project_all():
         qkv_g.finish()
-        fetch("qkv")
+        stores["qkv"].start()
         project(norm_one, qkv_v, qkv_bias, cosine, sine, query, key, value)
 
     def attend_all():
@@ -1111,7 +1104,7 @@
     def inner_all():
         weights["up a"].finish()
         weights["up b"].finish()
-        fetch("up")
+        stores["up"].start()
         feed_inner(norm_two, up_v, up_bias, activated, slope)
         stores["activated"].start()
         stores["slope"].start()
@@ -1127,15 +1120,17 @@
 
     def cot_done():
         cot_g.finish()
-        loads["cot"].start()
+        stores["cot"].start()
         out_swap.wait_recv()
-        fetch("out")
-        loads["cot"].wait()
+        stores["out"].start()
 
     def out_grads():
         attended_grads(cot_v, out_v, attended_grad)
 
     def down_grads():
+        stores["up"].wait()
+        weights["up a"].drain()
+        weights["up b"].drain()
         weight_grads(cot_v, activated, up_v)
         stores["down_grad"].start()
 
@@ -1215,9 +1210,10 @@
         steps[name]()
     for letter in DOWN_PARTS:
         weights["down " + letter].finish()
-    for store in stores.values():
-        store.wait()
-    for gather in [hid_g, cot_g, small_g] + list(weights.values()):
+    for name, store in stores.items():
+        if name != "up":
+            store.wait()
+    for gather in [hid_g, cot_g, small_g] + [weights[name] for name in weights if name[:2] != "up"]:
         gather.drain()
     out_across.wait_send()
     out_swap.wait_send()
@@ -1246,7 +1242,6 @@
         part_s,
         part_s,
         out_s,
-        small_s,
         narrow_s,
         ((tokens, head3), b16),
         wide_s,
@@ -2108,7 +2103,6 @@
         w_up,
         w_down,
         w_out,
-        _,
         attended_low,
         projected_grad,
         norm_two,

time: 300 us -> 295 us (0.983)
  Pallas kernels: 299 us -> 294 us
where the time goes in v7:
time: 295 us
  Pallas kernels  294 us (100%)
    pallas_call x1, Pallas kernels, gather_all(): pl.pallas_call(lambda *refs: gather_kernel(ctx_count, *refs), out_shape=[...  146 us
    pallas_call x1, Pallas kernels, scatter_all(): pl.pallas_call(lambda *refs: scatter_kernel(ctx_count, *refs), out_shape=...  138 us
    pallas_call x1, Pallas kernels, finish_all(): pl.pallas_call(finish_kernel, out_shape=[jax.ShapeDtypeStruct((n,), f32)...  10 us

profile of v7, /device:TPU:9, one launch (start us, length us, event | category | flops | bytes accessed | tf_op | source)
XLA Modules:
  0.0 294.5 jit_solution(4164802872985358046)
XLA Ops:
  0.7 145.9 %gather_all.1 = (bf16[1024,2048]{1,0:T(8,128)(2,1)}, bf16[1024,2048]{1,0:T(8,128)(2,1)}, bf16[8,4,64,768]{3,2,1,0:T(8,128)(2,1)}, bf16[8,4,64,1024]{3,2,1,0:T(8,...) custom-call(bf16[64,2,2048]{2,1,0:T(2,128)(2,1)} %hidden_in.1, ...), custom_call_target="tpu_custom_call" | custom-call | tf_op jit(solution)/shard_map/gather_all/pallas_call | solution.py:1295
  146.6 137.8 %scatter_all.1 = (f32[8,16,128]{2,1,0:T(8,128)}, bf16[8,64,768]{2,1,0:T(8,128)(2,1)}, bf16[8,64,1024]{2,1,0:T(8,128)(2,1)}, bf16[8,64,1024]{2,1,0:T(8,128)(2,1)}...) custom-call(bf16[1024,2048]{1,0:T(8,128)(2,1)} %get-tuple-element.50.refs_0_, ...), custom_call_target="tpu_custom_call" | custom-call | tf_op jit(solution)/shard_map/scatter_all/pallas_call | solution.py:1921
  284.3 10.0 %finish_all.1 = (f32[64]{0:T(128)}, f32[64]{0:T(128)}, f32[192]{0:T(256)}, f32[64]{0:T(128)}, f32[64]{0:T(128)}, /*index=5*/f32[64]{0:T(128)}, f32[256]{0:T(256)...) custom-call(bf16[8,64,768]{2,1,0:T(8,128)(2,1)} %get-tuple-element.6, ...), custom_call_target="tpu_custom_call" | custom-call | tf_op jit(solution)/shard_map/finish_all/pallas_call | solution.py:2067
